TPU v7x, 32 devices: a whole 2x2x4 slice. The times are simulated.
32 devices in a mesh: dp: 4 (over x, core), expert: 8 (over z, y).
Axes of the slice: x: 2, y: 2, z: 4, core: 2. Of those that a mesh axis runs over, the one named last changes fastest.
Arguments:
- tokens: bfloat16 [1024, 5120], P('expert', 'dp'), may hold values from -6 to 6
- out_grad: bfloat16 [1024, 5120], P('expert', 'dp'), may hold values from -0.59765625 to 0.59765625
- gate_values: float32 [1024, 2], P('expert'), may hold values from 0.05 to 0.5
- route_lists: int32 [1024, 2], P('expert'), may hold values from 0 to 3, all different within a row; in each aligned block of 128 rows (0 to 127, 128 to 255, ...) at most 72 rows name the same one
- expert_pairs: int32 [4], replicated, may hold values from 0 to 3, as said below
- gate_weight: bfloat16 [8, 5120, 1024], P('expert', 'dp'), as said below
- up_weight: bfloat16 [8, 5120, 1024], P('expert', 'dp'), as said below
- down_weight: bfloat16 [8, 1024, 5120], P('expert', None, 'dp'), as said below
Outputs:
- layer_output: bfloat16 [1024, 5120], P('expert', 'dp')
- token_grad: bfloat16 [1024, 5120], P('expert', 'dp')
- gate_value_grad: float32 [1024, 2], P('expert')
- gate_weight_grad: bfloat16 [8, 5120, 1024], P('expert', 'dp')
- up_weight_grad: bfloat16 [8, 5120, 1024], P('expert', 'dp')
- down_weight_grad: bfloat16 [8, 1024, 5120], P('expert', None, 'dp')
Inputs may be any that keep to these rules, and one draw needn't show every extreme that they name: `route_lists`: each token names 2 different experts; within each aligned block of 128 tokens no expert is named by more than 72 tokens. `expert_pairs`: a permutation; pair p is made of slots p and p + 4. `gate_weight`: slots p and p + 4 hold equal matrices, those of expert expert_pairs[p]. `up_weight`: slots p and p + 4 hold equal matrices. `down_weight`: slots p and p + 4 hold equal matrices.
All inputs are finite; a program needn't handle non-finite values.
Results may differ from a plain program's by a relative error of at most 0.023.
Values may be sent and summed in bfloat16 or wider, within the bound.
No kernel may reach another device: no remote copies, remote signals or barrier semaphores. Data moves between devices by JAX's collectives and lax.ppermute only.
A program may use at most 128 MiB of HBM per device.

v0:
```python
import jax
import jax.numpy as jnp
from jax import lax
from jax.sharding import PartitionSpec as P

HALF = 36


def partner(x, axis, distance):
    return lax.ppermute(x, axis, [(i, i ^ 1 << distance) for i in range(lax.axis_size(axis))])


def shards(
    tokens, out_grad, gate_values, route_lists, expert_pairs, gate_weight, up_weight, down_weight
):
    tok_rows, width_dev = tokens.shape
    top_count = route_lists.shape[1]
    slot_count = lax.axis_size("expert")
    pair_count = slot_count // 2
    swap_bit = slot_count.bit_length() - 2
    contract_first = (((0,), (0,)), ((), ()))
    contract_second = (((1,), (1,)), ((), ()))
    catalog = jnp.arange(pair_count, dtype=jnp.int32)
    chosen = (route_lists[:, :, None] == catalog[None, None, :]).astype(jnp.int32)
    present = jnp.sum(chosen, axis=1)
    before = jnp.cumsum(present, axis=0) - present
    position = jnp.sum(chosen * before[:, None, :], axis=2)
    owner_pair = jnp.sum(
        jnp.where(
            route_lists[:, :, None] == expert_pairs[None, None, :], catalog[None, None, :], 0
        ),
        axis=2,
    )
    is_upper = (position >= HALF).astype(jnp.int32)
    target = (owner_pair + pair_count * is_upper) * HALF + position - HALF * is_upper
    capacity = slot_count * HALF
    flat_count = tok_rows * top_count
    slot_table = (
        jnp.full((capacity,), flat_count, jnp.int32)
        .at[target.reshape(-1)]
        .set(jnp.arange(flat_count, dtype=jnp.int32))
    )
    token_of = jnp.where(slot_table < flat_count, slot_table // top_count, tok_rows)
    padded_tokens = jnp.concatenate([tokens, jnp.zeros((1, width_dev), jnp.bfloat16)], axis=0)
    scaled_cot = (
        (gate_values[:, :, None] * out_grad.astype(jnp.float32)[:, None, :])
        .astype(jnp.bfloat16)
        .reshape(flat_count, width_dev)
    )
    padded_cot = jnp.concatenate([scaled_cot, jnp.zeros((1, width_dev), jnp.bfloat16)], axis=0)
    sent_tokens = padded_tokens[token_of].reshape(slot_count, HALF, width_dev)
    sent_cot = padded_cot[slot_table].reshape(slot_count, HALF, width_dev)
    got_tokens, got_cot = (
        lax.all_to_all(sent_tokens, "expert", split_axis=0, concat_axis=0, tiled=True),
        lax.all_to_all(sent_cot, "expert", split_axis=0, concat_axis=0, tiled=True),
    )
    row_total = slot_count * HALF
    rows_in = got_tokens.reshape(row_total, width_dev)
    cot_rows = got_cot.reshape(row_total, width_dev)
    w_gate = gate_weight[0]
    w_up = up_weight[0]
    w_down = down_weight[0]
    part_gate = jnp.dot(rows_in, w_gate, preferred_element_type=jnp.float32)
    part_up = jnp.dot(rows_in, w_up, preferred_element_type=jnp.float32)
    gate_pre, up_pre = (
        lax.psum(part_gate.astype(jnp.bfloat16), "dp").astype(jnp.float32),
        lax.psum(part_up.astype(jnp.bfloat16), "dp").astype(jnp.float32),
    )
    hidden = (jax.nn.silu(gate_pre) * up_pre).astype(jnp.bfloat16)
    expert_out = jnp.dot(hidden, w_down, preferred_element_type=jnp.float32).astype(jnp.bfloat16)
    grad_down = lax.dot_general(
        hidden, cot_rows, contract_first, preferred_element_type=jnp.float32
    ).astype(jnp.bfloat16)
    back_part = lax.dot_general(
        cot_rows, w_down, contract_second, preferred_element_type=jnp.float32
    )
    hidden_grad = lax.psum(back_part.astype(jnp.bfloat16), "dp").astype(jnp.float32)
    sigmoid_gate = jax.nn.sigmoid(gate_pre)
    up_grad = (hidden_grad * gate_pre * sigmoid_gate).astype(jnp.bfloat16)
    pre_grad = (
        hidden_grad * up_pre * sigmoid_gate * (1.0 + gate_pre * (1.0 - sigmoid_gate))
    ).astype(jnp.bfloat16)
    row_input_grad = (
        lax.dot_general(pre_grad, w_gate, contract_second, preferred_element_type=jnp.float32)
        + lax.dot_general(up_grad, w_up, contract_second, preferred_element_type=jnp.float32)
    ).astype(jnp.bfloat16)
    grad_gate = lax.dot_general(
        rows_in, pre_grad, contract_first, preferred_element_type=jnp.float32
    ).astype(jnp.bfloat16)
    grad_up = lax.dot_general(
        rows_in, up_grad, contract_first, preferred_element_type=jnp.float32
    ).astype(jnp.bfloat16)
    partner_gate, partner_up, partner_down = partner(
        (grad_gate, grad_up, grad_down), "expert", swap_bit
    )
    back_out, back_grad = (
        lax.all_to_all(
            expert_out.reshape(slot_count, HALF, width_dev),
            "expert",
            split_axis=0,
            concat_axis=0,
            tiled=True,
        ),
        lax.all_to_all(
            row_input_grad.reshape(slot_count, HALF, width_dev),
            "expert",
            split_axis=0,
            concat_axis=0,
            tiled=True,
        ),
    )
    out_each = back_out.reshape(capacity, width_dev)[target].astype(jnp.float32)
    grad_each = back_grad.reshape(capacity, width_dev)[target].astype(jnp.float32)
    layer_output = jnp.sum(gate_values[:, :, None] * out_each, axis=1).astype(jnp.bfloat16)
    token_grad = jnp.sum(grad_each, axis=1).astype(jnp.bfloat16)
    inner_dots = jnp.sum(out_grad.astype(jnp.float32)[:, None, :] * out_each, axis=2)
    gate_value_grad = lax.psum(inner_dots, "dp")
    gate_weight_grad = (grad_gate.astype(jnp.float32) + partner_gate.astype(jnp.float32)).astype(
        jnp.bfloat16
    )[None]
    up_weight_grad = (grad_up.astype(jnp.float32) + partner_up.astype(jnp.float32)).astype(
        jnp.bfloat16
    )[None]
    down_weight_grad = (grad_down.astype(jnp.float32) + partner_down.astype(jnp.float32)).astype(
        jnp.bfloat16
    )[None]
    return (
        layer_output,
        token_grad,
        gate_value_grad,
        gate_weight_grad,
        up_weight_grad,
        down_weight_grad,
    )


def solution(mesh):
    placed = (
        P("expert", "dp"),
        P("expert", "dp"),
        P("expert", None),
        P("expert", None),
        P(),
        P("expert", "dp", None),
        P("expert", "dp", None),
        P("expert", None, "dp"),
    )
    return jax.shard_map(
        shards,
        mesh=mesh,
        in_specs=placed,
        out_specs=(
            P("expert", "dp"),
            P("expert", "dp"),
            P("expert", None),
            P("expert", "dp", None),
            P("expert", "dp", None),
            P("expert", None, "dp"),
        ),
        check_vma=False,
    )
```

profile of v0, /device:TPU:0, one launch (start us, length us, event | category | flops | bytes accessed | tf_op | source)
XLA Modules:
  0.0 515.3 jit_solution(13119675361986686623)
XLA Ops:
  7.2 0.9 select_reduce_fusion.1
  8.1 0.1 copy.25
  8.2 0.2 reduce_window_sum.11
  8.4 0.1 copy.27
  8.5 0.7 select_reduce_fusion
  9.2 0.1 copy.24
  9.3 0.1 reduce_sum.66
  9.4 0.1 copy.28
  9.5 0.1 reduce_sum.69
  9.7 1.4 scatter_custom_fusion
  11.1 1.0 concatenate.6
  12.1 2.7 gather_fusion
  14.8 2.1 reshape.143
  16.9 7.3 %all-to-all-start = ((bf16[8,36,1280]{2,1,0:T(8,128)(2,1)}), bf16[8,36,1280]{2,1,0:T(8,128)(2,1)}, u32[]{:S(2)}, u32[]{:S(2)}) async-start(bf16[8,36,1280]{2,1,0:T(8,128)(2,1)} %reshape.143), calls=%async_computation | async-start | bytes 1638400 | tf_op jit(solution)/shard_map/all_to_all | solution.py:54
  24.2 0.1 copy.23
  24.3 0.1 mul.114
  24.5 1.4 mul.116
  25.9 3.0 mul.117
  28.9 1.4 multiply_convert_fusion
  30.4 2.7 gather_fusion.2
  33.1 2.0 reshape.147
  35.1 10.1 %all-to-all-done = bf16[8,36,1280]{2,1,0:T(8,128)(2,1)} async-done(((bf16[8,36,1280]{2,1,0:T(8,128)(2,1)}), bf16[8,36,1280]{2,1,0:T(8,128)(2,1)}, u32[]{:S(2)}, u32[]{:S(2)}) %all-to-all-start) | async-done | bytes 737312 | tf_op jit(solution)/shard_map/all_to_all | solution.py:54
  45.2 3.5 all-to-all-start.2
  48.8 0.0 all-reduce.5.cloned.1.call-start
  48.8 2.1 reshape.144
  50.9 3.9 fusion.17
  54.8 1.7 fusion.14
  56.5 13.3 %all-to-all-done.2 = bf16[8,36,1280]{2,1,0:T(8,128)(2,1)S(1)} async-done(((bf16[8,36,1280]{2,1,0:T(8,128)(2,1)}), bf16[8,36,1280]{2,1,0:T(8,128)(2,1)S(1)}, u32[]{:S(2)}, u32[]{:S(2)}) %all-to-all-start.2) | async-done | bytes 737312 | tf_op jit(solution)/shard_map/all_to_all | solution.py:55
  69.8 1.1 reshape.148
  70.9 2.9 fusion.20
  73.8 45.6 %all-reduce.5.cloned.1.call-done = (bf16[288,1024]{1,0:T(8,128)(2,1)}, bf16[288,1024]{1,0:T(8,128)(2,1)}, bf16[288,1024]{1,0:T(8,128)(2,1)}) async-done(((bf16[288,1024]{1,0:T(8,128)(2,1)}, bf16[288,1024]{1,0:T(8,128)(2,1)}, bf16[288,1024]{1,0:T(8,128)(2,1)}), (bf16[288,1024]{1,0:T(8,128)(2,1)}, bf16[288,1024]{1,0:T(8,128)(2,1)}, bf16[288,1024]{1,0:T(8,128)(2,1)})) %all-reduce.5.cloned.1.call-update) | async-done | bytes 1769488 | tf_op jit(solution)/shard_map/psum | solution.py:67
  119.4 2.4 convolution_convert_fusion.3
  121.8 1.0 reshape.145
  122.8 5.5 %all-to-all-start.1 = ((bf16[8,36,1280]{2,1,0:T(8,128)(2,1)}), bf16[8,36,1280]{2,1,0:T(8,128)(2,1)S(1)}, u32[]{:S(2)}, u32[]{:S(2)}) async-start(bf16[8,36,1280]{2,1,0:T(8,128)(2,1)} %reshape.145), calls=%async_computation.1 | async-start | bytes 1638400 | tf_op jit(solution)/shard_map/all_to_all | solution.py:97
  128.3 4.8 convolution_convert_fusion.1
  133.1 2.9 collective-permute-start.1
  136.0 3.2 convolution_convert_fusion.2
  139.3 0.0 collective-permute-start
  139.3 1.4 fusion.10
  140.7 0.3 copy-done.10
  141.0 2.1 fusion
  143.2 2.1 reshape.149
  145.2 117.7 %all-to-all-done.1 = bf16[8,36,1280]{2,1,0:T(8,128)(2,1)S(1)} async-done(((bf16[8,36,1280]{2,1,0:T(8,128)(2,1)}), bf16[8,36,1280]{2,1,0:T(8,128)(2,1)S(1)}, u32[]{:S(2)}, u32[]{:S(2)}) %all-to-all-start.1) | async-done | bytes 737312 | tf_op jit(solution)/shard_map/all_to_all | solution.py:97
  262.9 4.2 all-to-all-start.3
  267.2 4.7 convolution_convert_fusion
  271.9 2.8 collective-permute-start.2
  274.7 0.9 convert_element_type.98
  275.6 0.1 copy.29
  275.7 0.1 reshape.161
  275.8 1.3 reshape.146
  277.1 2.2 gather_fusion.1
  279.3 2.9 reshape.195
  282.1 4.2 multiply_reduce_fusion
  286.3 11.7 %psum.31 = f32[128,2]{1,0:T(8,128)S(1)} all-reduce(f32[128,2]{1,0:T(8,128)S(1)} %get-tuple-element.18), channel_id=1, replica_groups=mesh['dp'=4,'expert'=8] {'dp'}, use_global_device_ids=true, to_apply=%region_11.12 | all-reduce | flops 256 | bytes 2048 | tf_op jit(solution)/shard_map/psum | solution.py:117
  298.0 0.6 copy.31
  298.6 150.5 %all-to-all-done.3 = bf16[8,36,1280]{2,1,0:T(8,128)(2,1)} async-done(((bf16[8,36,1280]{2,1,0:T(8,128)(2,1)}), bf16[8,36,1280]{2,1,0:T(8,128)(2,1)}, u32[]{:S(2)}, u32[]{:S(2)}) %all-to-all-start.3) | async-done | bytes 737312 | tf_op jit(solution)/shard_map/all_to_all | solution.py:104
  449.2 1.3 reshape.150
  450.4 2.1 gather_fusion.3
  452.5 2.0 reshape.180
  454.5 2.5 reduce_sum.73
  457.0 5.3 %fusion.2 = bf16[1,1280,1024]{2,1,0:T(8,128)(2,1)} fusion(bf16[1280,1024]{1,0:T(8,128)(2,1)} %collective-permute-done.1, bf16[1280,1024]{1,0:T(8,128)(2,1)} %convolution_convert_fusion.1), kind=kLoop, calls=%fused_computation.15 | loop fusion | flops 5242880 | bytes 7864320 | tf_op jit(solution)/shard_map/broadcast_in_dim | solution.py:121
  462.3 5.3 %fusion.1 = bf16[1,1280,1024]{2,1,0:T(8,128)(2,1)} fusion(bf16[1280,1024]{1,0:T(8,128)(2,1)} %collective-permute-done, bf16[1280,1024]{1,0:T(8,128)(2,1)} %convolution_convert_fusion.2), kind=kLoop, calls=%fused_computation.14 | loop fusion | flops 5242880 | bytes 7864320 | tf_op jit(solution)/shard_map/broadcast_in_dim | solution.py:118
  467.5 36.2 %collective-permute-done.2 = bf16[1024,1280]{1,0:T(8,128)(2,1)} collective-permute-done((bf16[1024,1280]{1,0:T(8,128)(2,1)}, bf16[1024,1280]{1,0:T(8,128)(2,1)}, u32[]{:S(2)}, u32[]{:S(2)}) %collective-permute-start.2) | collective-permute-done | bytes 2621472 | tf_op jit(solution)/shard_map/ppermute | solution.py:10
  503.8 4.7 fusion.3
  (38 shorter events, 0.2 us)
Async XLA Ops:
  7.2 63.7 %copy-start = (bf16[1,1024,1280]{2,1,0:T(8,128)(2,1)S(1)}, bf16[1,1024,1280]{2,1,0:T(8,128)(2,1)}, u32[]{:S(2)}) copy-start(bf16[1,1024,1280]{2,1,0:T(8,128)(2,1)} %param.15) | copy-start | bytes 7864324
  14.8 9.4 %copy-start.7 = (f32[128,2]{0,1:T(2,128)S(1)}, f32[128,2]{0,1:T(2,128)}, u32[]{:S(2)}) copy-start(f32[128,2]{0,1:T(2,128)} %param.10) | copy-start | bytes 3076
  14.8 9.7 %copy-start.3 = (bf16[128,1280]{1,0:T(8,128)(2,1)S(1)}, bf16[128,1280]{1,0:T(8,128)(2,1)}, u32[]{:S(2)}) copy-start(bf16[128,1280]{1,0:T(8,128)(2,1)} %param.9) | copy-start | bytes 983044
  16.9 28.3 %all-to-all-start = ((bf16[8,36,1280]{2,1,0:T(8,128)(2,1)}), bf16[8,36,1280]{2,1,0:T(8,128)(2,1)}, u32[]{:S(2)}, u32[]{:S(2)}) async-start(bf16[8,36,1280]{2,1,0:T(8,128)(2,1)} %reshape.143), calls=%async_computation | async-start | bytes 1638400 | tf_op jit(solution)/shard_map/all_to_all | solution.py:54
  45.2 24.6 %all-to-all-start.2 = ((bf16[8,36,1280]{2,1,0:T(8,128)(2,1)}), bf16[8,36,1280]{2,1,0:T(8,128)(2,1)S(1)}, u32[]{:S(2)}, u32[]{:S(2)}) async-start(bf16[8,36,1280]{2,1,0:T(8,128)(2,1)} %reshape.147), calls=%async_computation.2 | async-start | bytes 1638400 | tf_op jit(solution)/shard_map/all_to_all | solution.py:55
  48.8 70.6 %all-reduce.5.cloned.1.call-start = ((), (), s32[]{:S(2)}) async-start(), calls=%async_computation.4 | async-start | bytes 3538944 | tf_op jit(solution)/shard_map/psum | solution.py:67
  50.9 3.9 copy-start.5
  50.9 3.9 copy-start.8
  122.8 140.2 %all-to-all-start.1 = ((bf16[8,36,1280]{2,1,0:T(8,128)(2,1)}), bf16[8,36,1280]{2,1,0:T(8,128)(2,1)S(1)}, u32[]{:S(2)}, u32[]{:S(2)}) async-start(bf16[8,36,1280]{2,1,0:T(8,128)(2,1)} %reshape.145), calls=%async_computation.1 | async-start | bytes 1638400 | tf_op jit(solution)/shard_map/all_to_all | solution.py:97
  128.3 7.7 %copy-start.6 = (bf16[288,1280]{1,0:T(8,128)(2,1)S(1)}, bf16[288,1280]{1,0:T(8,128)(2,1)}, u32[]{:S(2)}) copy-start(bf16[288,1280]{1,0:T(8,128)(2,1)} %reshape.144) | copy-start | bytes 2211844
  128.3 7.7 %copy-start.11 = (bf16[288,1024]{1,0:T(8,128)(2,1)S(1)}, bf16[288,1024]{1,0:T(8,128)(2,1)}, u32[]{:S(2)}) copy-start(bf16[288,1024]{1,0:T(8,128)(2,1)} %get-tuple-element.22) | copy-start | bytes 1769476
  128.3 7.7 %copy-start.12 = (bf16[288,1024]{1,0:T(8,128)(2,1)S(1)}, bf16[288,1024]{1,0:T(8,128)(2,1)}, u32[]{:S(2)}) copy-start(bf16[288,1024]{1,0:T(8,128)(2,1)} %get-tuple-element.23) | copy-start | bytes 1769476
  128.3 7.7 %copy-start.13 = (bf16[288,1024]{1,0:T(8,128)(2,1)S(1)}, bf16[288,1024]{1,0:T(8,128)(2,1)}, u32[]{:S(2)}) copy-start(bf16[288,1024]{1,0:T(8,128)(2,1)} %get-tuple-element.24) | copy-start | bytes 1769476
  133.1 6.2 %copy-start.9 = (bf16[1,1280,1024]{2,1,0:T(8,128)(2,1)S(1)}, bf16[1,1280,1024]{2,1,0:T(8,128)(2,1)}, u32[]{:S(2)}) copy-start(bf16[1,1280,1024]{2,1,0:T(8,128)(2,1)} %param.13) | copy-start | bytes 7864324
  133.1 323.9 %collective-permute-start.1 = (bf16[1280,1024]{1,0:T(8,128)(2,1)}, bf16[1280,1024]{1,0:T(8,128)(2,1)}, u32[]{:S(2)}, u32[]{:S(2)}) collective-permute-start(bf16[1280,1024]{1,0:T(8,128)(2,1)} %convolution_convert_fusion.1), channel_id=1, source_target_pairs={{0,4},{1,5},{2,6},{3,7},{4,0},{5,1},{6,2},{7,3},{8,12},{9,13},{10,... | collective-permute-start | bytes 7864328 | tf_op jit(solution)/shard_map/ppermute | solution.py:10
  139.3 1.7 copy-start.10
  139.3 323.0 %collective-permute-start = (bf16[1280,1024]{1,0:T(8,128)(2,1)}, bf16[1280,1024]{1,0:T(8,128)(2,1)}, u32[]{:S(2)}, u32[]{:S(2)}) collective-permute-start(bf16[1280,1024]{1,0:T(8,128)(2,1)} %convolution_convert_fusion.2), channel_id=1, source_target_pairs={{0,4},{1,5},{2,6},{3,7},{4,0},{5,1},{6,2},{7,3},{8,12},{9,13},{10,... | collective-permute-start | bytes 7864328 | tf_op jit(solution)/shard_map/ppermute | solution.py:10
  262.9 8.9 %copy-start.1 = (bf16[8,36,1280]{2,1,0:T(8,128)(2,1)}, bf16[8,36,1280]{2,1,0:T(8,128)(2,1)S(1)}, u32[]{:S(2)}) copy-start(bf16[8,36,1280]{2,1,0:T(8,128)(2,1)S(1)} %all-to-all-done.1) | copy-start | bytes 2211844
  262.9 186.2 %all-to-all-start.3 = ((bf16[8,36,1280]{2,1,0:T(8,128)(2,1)}), bf16[8,36,1280]{2,1,0:T(8,128)(2,1)}, u32[]{:S(2)}, u32[]{:S(2)}) async-start(bf16[8,36,1280]{2,1,0:T(8,128)(2,1)} %reshape.149), calls=%async_computation.3 | async-start | bytes 1638400 | tf_op jit(solution)/shard_map/all_to_all | solution.py:104
  267.2 7.5 %copy-start.4 = (bf16[128,1280]{1,0:T(8,128)(2,1)S(1)}, bf16[128,1280]{1,0:T(8,128)(2,1)}, u32[]{:S(2)}) copy-start(bf16[128,1280]{1,0:T(8,128)(2,1)} %param.9) | copy-start | bytes 983044
  271.9 231.9 %collective-permute-start.2 = (bf16[1024,1280]{1,0:T(8,128)(2,1)}, bf16[1024,1280]{1,0:T(8,128)(2,1)}, u32[]{:S(2)}, u32[]{:S(2)}) collective-permute-start(bf16[1024,1280]{1,0:T(8,128)(2,1)} %convolution_convert_fusion), channel_id=1, source_target_pairs={{0,4},{1,5},{2,6},{3,7},{4,0},{5,1},{6,2},{7,3},{8,12},{9,13},{10,... | collective-permute-start | bytes 7864328 | tf_op jit(solution)/shard_map/ppermute | solution.py:10
  279.3 2.9 copy-start.2
Sparse Core Ops, SparseCore 0:
  73.9 45.3 all-reduce.4
where the time goes:
time: 516 us; the launch traced here: 515 us
  waiting for transfers between devices  374 us (72%)
  local copies, waits for them, and re-layouts  36.4 us (7%)
  matrix products  27 us (5%)
  starting transfers between devices  26.4 us (5%)
  other arithmetic  26 us (5%)
  between operations  14.3 us (3%)
  blocking collectives  11.7 us (2%)
    all_to_all x1, waiting for transfers between devices, shards(): lax.all_to_all(row_input_grad.reshape(slot_count, HALF, width_dev), 'expe...  151 us
    all_to_all x1, waiting for transfers between devices, shards(): lax.all_to_all(expert_out.reshape(slot_count, HALF, width_dev), 'expert',...  118 us
    psum x1, waiting for transfers between devices, shards(): lax.psum(part_up.astype(jnp.bfloat16), 'dp').astype(jnp.float32)  45.6 us
    ppermute x3, waiting for transfers between devices, partner(): lax.ppermute(x, axis, [(i, i ^ 1 << distance) for i in range(lax.axis_siz...  36.2 us
    all_to_all x1, waiting for transfers between devices, shards(): lax.all_to_all(sent_cot, 'expert', split_axis=0, concat_axis=0, tiled=True)  13.3 us
    psum x1, blocking collectives, shards(): gate_value_grad = lax.psum(inner_dots, 'dp')  11.7 us
  transfers between devices with their start and end apart: 8, of which 6 were waited for; matrix products, arithmetic and copies ran while one was open for 13% of the time, Pallas kernels for 0%

commit v1 on v0

v1 whole, which is shorter than its diff:
```python
import jax
import jax.numpy as jnp
from jax import lax
from jax.sharding import PartitionSpec as P

HALF = 36
CAP = 2 * HALF
FIRST = (((0,), (0,)), ((), ()))
SECOND = (((1,), (1,)), ((), ()))


def hop(x, axis, distance):
    return lax.ppermute(x, axis, [(i, i ^ distance) for i in range(lax.axis_size(axis))])


def dot32(a, b, dims=(((1,), (0,)), ((), ()))):
    return lax.dot_general(a, b, dims, preferred_element_type=jnp.float32)


def routing(routes, gates, names):
    tok = routes.shape[1]
    hits = routes[:, None, :] == names[None, :, None]
    named = jnp.any(hits, axis=0)
    earlier = jnp.arange(tok)[:, None] < jnp.arange(tok)[None, :]
    before = dot32(named.astype(jnp.bfloat16), earlier.astype(jnp.bfloat16)).astype(jnp.int32)
    place = jnp.where(named, before, -1)
    pick = place[:, None, :] == jnp.arange(CAP)[None, :, None]
    gate_at = jnp.sum(jnp.where(hits, gates[:, None, :], 0.0), axis=0)
    row_gate = jnp.sum(jnp.where(pick, gate_at[:, None, :], 0.0), axis=2)
    return hits, pick, row_gate.reshape(-1)


def dispatch(pick, block, scale=None):
    rows = dot32(pick.reshape(-1, pick.shape[2]).astype(jnp.bfloat16), block)
    if scale is not None:
        rows = rows * scale[:, None]
    rows = rows.astype(jnp.bfloat16)
    parts = [rows[:CAP]]
    for d in range(1, pick.shape[0]):
        parts.append(hop(rows[d * CAP : (d + 1) * CAP], "expert", d))
    return jnp.concatenate(parts, axis=0)


def forward(rows, cot, w_gate, w_up, w_down, core):
    width = w_gate.shape[1] // 2
    parts = [dot32(rows, w_gate), dot32(rows, w_up), dot32(cot, w_down, SECOND)]
    parts = [p.astype(jnp.bfloat16) for p in parts]

    def side(which):
        return jnp.concatenate(
            [lax.dynamic_slice_in_dim(p, which * width, width, axis=1) for p in parts], axis=1
        )

    total = side(core).astype(jnp.float32) + hop(side(1 - core), "dp", 1).astype(jnp.float32)
    total = total.astype(jnp.bfloat16)
    distance = 2
    while distance < lax.axis_size("dp"):
        total = total.astype(jnp.float32) + hop(total, "dp", distance).astype(jnp.float32)
        total = total.astype(jnp.bfloat16)
        distance *= 2
    other = hop(total, "dp", 1)
    low = jnp.where(core == 0, total, other).astype(jnp.float32)
    high = jnp.where(core == 0, other, total).astype(jnp.float32)
    return [
        jnp.concatenate([low[:, i * width : (i + 1) * width], high[:, i * width : (i + 1) * width]], axis=1)
        for i in range(3)
    ]


def middle(gate_pre, up_pre, hidden_grad):
    sig = jax.nn.sigmoid(gate_pre)
    silu = gate_pre * sig
    hidden = (silu * up_pre).astype(jnp.bfloat16)
    up_grad = (hidden_grad * silu).astype(jnp.bfloat16)
    pre_grad = (hidden_grad * up_pre * sig * (1.0 + gate_pre * (1.0 - sig))).astype(jnp.bfloat16)
    return hidden, up_grad, pre_grad


def shards(
    tokens, out_grad, gate_values, route_lists, expert_pairs, gate_weight, up_weight, down_weight
):
    top = route_lists.shape[1]
    width = tokens.shape[1]
    pairs = lax.axis_size("expert") // 2
    low = lax.axis_index("expert") % pairs
    core = lax.axis_index("dp") % 2
    places = jnp.arange(pairs, dtype=jnp.int32)
    names = jnp.sum(
        jnp.where((low ^ places)[:, None] == places[None, :], expert_pairs[None, :], 0), axis=1
    )
    w_gate, w_up, w_down = gate_weight[0], up_weight[0], down_weight[0]

    routes, gates = route_lists.T, gate_values.T
    info = jnp.concatenate([routes.astype(jnp.float32), gates], axis=0)
    far_info = hop(info, "expert", pairs)
    hits, pick, row_gate = routing(routes, gates, names)
    rows = dispatch(pick, tokens)
    far_tokens = hop(tokens, "expert", pairs)
    cot = dispatch(pick, out_grad, row_gate)
    far_grad = hop(out_grad, "expert", pairs)

    gate_pre, up_pre, hidden_grad = forward(rows, cot, w_gate, w_up, w_down, core)
    hidden, up_grad, pre_grad = middle(gate_pre, up_pre, hidden_grad)
    inner = jnp.sum(hidden.astype(jnp.float32) * hidden_grad, axis=1, keepdims=True)
    inner_high = inner.astype(jnp.bfloat16)
    inner_low = (inner - inner_high.astype(jnp.float32)).astype(jnp.bfloat16)

    expert_out = dot32(hidden, w_down).astype(jnp.bfloat16)
    input_grad = (dot32(pre_grad, w_gate, SECOND) + dot32(up_grad, w_up, SECOND)).astype(
        jnp.bfloat16
    )
    back = jnp.concatenate(
        [expert_out, input_grad, jnp.pad(jnp.concatenate([inner_high, inner_low], axis=1), ((0, 0), (0, 126)))],
        axis=1,
    )
    back = jnp.concatenate(
        [back[:CAP]] + [hop(back[d * CAP : (d + 1) * CAP], "expert", d) for d in range(1, pairs)],
        axis=0,
    )
    all_pick = pick.reshape(pairs * CAP, -1).astype(jnp.bfloat16)
    token_grad = dot32(all_pick, back[:, width : 2 * width], FIRST).astype(jnp.bfloat16)
    layer_output = 0.0
    inners = []
    for k in range(top):
        mine = (pick & hits[k][:, None, :]).reshape(pairs * CAP, -1).astype(jnp.bfloat16)
        layer_output += gate_values[:, k : k + 1] * dot32(mine, back[:, :width], FIRST)
        ends = dot32(mine, back[:, 2 * width :], FIRST)
        inners.append(ends[:, 0:1] + ends[:, 1:2])
    layer_output = layer_output.astype(jnp.bfloat16)
    gate_value_grad = jnp.concatenate(inners, axis=1) / gate_values

    far_routes, far_gates = far_info[:top].astype(jnp.int32), far_info[top:]
    _, far_pick, far_row_gate = routing(far_routes, far_gates, names)
    far_rows = dispatch(far_pick, far_tokens)
    far_cot = dispatch(far_pick, far_grad, far_row_gate)
    far_hidden, far_up, far_pre = middle(*forward(far_rows, far_cot, w_gate, w_up, w_down, core))

    def both(a, b):
        return jnp.concatenate([a, b], axis=0)

    all_rows = both(rows, far_rows)
    grad_gate = dot32(all_rows, both(pre_grad, far_pre), FIRST).astype(jnp.bfloat16)
    grad_up = dot32(all_rows, both(up_grad, far_up), FIRST).astype(jnp.bfloat16)
    grad_down = dot32(both(hidden, far_hidden), both(cot, far_cot), FIRST).astype(jnp.bfloat16)
    return layer_output, token_grad, gate_value_grad, grad_gate[None], grad_up[None], grad_down[None]


def solution(mesh):
    row = P("expert", "dp")
    small = P("expert", None)
    tall = P("expert", "dp", None)
    wide = P("expert", None, "dp")
    return jax.shard_map(
        shards,
        mesh=mesh,
        in_specs=(row, row, small, small, P(), tall, tall, wide),
        out_specs=(row, row, small, tall, tall, wide),
        check_vma=False,
    )
```

time: 516 us -> 153 us (0.30)
  waiting for transfers between devices: 374 us -> 68.7 us
  local copies, waits for them, and re-layouts: 36.4 us -> 11 us
  other arithmetic: 26 us -> 10.9 us
  between operations: 14.3 us -> 1.29 us
  blocking collectives: 11.7 us -> 0 us
    all_to_all x4 -> x0, waiting for transfers between devices: 292 us -> none  [the longest x1 151 us: shards(): lax.all_to_all(row_input_grad.reshape(slot_count, HALF, width_dev), 'expe...]
    psum x1 -> x0, waiting for transfers between devices: 45.6 us -> none  [shards(): lax.psum(part_up.astype(jnp.bfloat16), 'dp').astype(jnp.float32)]
    ppermute x3 -> x24, waiting for transfers between devices: 36.2 us -> 68.7 us  [hop(): lax.ppermute(x, axis, [(i, i ^ distance) for i in range(lax.axis_size(axi...]
    ppermute x3 -> x24, starting transfers between devices: 5.75 us -> 27.9 us  [hop(): lax.ppermute(x, axis, [(i, i ^ distance) for i in range(lax.axis_size(axi...]
    all_to_all x4 -> x0, starting transfers between devices: 20.6 us -> none  [the longest x1 7.28 us: shards(): lax.all_to_all(sent_tokens, 'expert', split_axis=0, concat_axis=0, tiled=...]
    broadcast_in_dim x3 -> x0, other arithmetic: 15.2 us -> none  [the longest x1 5.27 us: shards(): (grad_gate.astype(jnp.float32) + partner_gate.astype(jnp.float32)).astype...]
    reshape x8 -> x0, local copies, waits for them, and re-layouts: 12.9 us -> none  [the longest x1 2.11 us: shards(): sent_tokens = padded_tokens[token_of].reshape(slot_count, HALF, width_dev)]
    psum x1 -> x0, blocking collectives: 11.7 us -> none  [shards(): gate_value_grad = lax.psum(inner_dots, 'dp')]
  transfers between devices with their start and end apart: 8 -> 24, of which waited for: 6 -> 12; matrix products, arithmetic and copies ran while one was open for 13% -> 29% of each run, Pallas kernels for 0% -> 0%
where the time goes in v1:
time: 153 us; the launch traced here: 150 us
  waiting for transfers between devices  68.7 us (45%)
  matrix products  30.1 us (20%)
  starting transfers between devices  27.9 us (18%)
  local copies, waits for them, and re-layouts  11 us (7%)
  other arithmetic  10.9 us (7%)
    ppermute x24, waiting for transfers between devices, hop(): lax.ppermute(x, axis, [(i, i ^ distance) for i in range(lax.axis_size(axi...  68.7 us
    dot_general x23, matrix products, dot32(): return lax.dot_general(a, b, dims, preferred_element_type=jnp.float32)  30.1 us
    ppermute x24, starting transfers between devices, hop(): lax.ppermute(x, axis, [(i, i ^ distance) for i in range(lax.axis_size(axi...  27.9 us
    unnamed x53, local copies, waits for them, and re-layouts  8.1 us
  transfers between devices with their start and end apart: 24, of which 12 were waited for; matrix products, arithmetic and copies ran while one was open for 29% of the time, Pallas kernels for 0%

profile of v1, /device:TPU:0, one launch (start us, length us, event | category | flops | bytes accessed | tf_op | source)
XLA Modules:
  0.0 150.0 jit_solution(13878840508885540990)
XLA Ops:
  0.7 0.8 bitcast_convert_fusion
  1.5 0.7 pad_maximum_fusion.16
  2.2 4.0 %collective-permute-start.12 = (f32[4,128]{1,0:T(4,128)S(1)}, f32[4,128]{1,0:T(4,128)S(1)}, u32[]{:S(2)}, u32[]{:S(2)}) collective-permute-start(f32[4,128]{1,0:T(4,128)S(1)} %pad_maximum_fusion.16), channel_id=1, source_target_pairs={{0,4},{1,5},{2,6},{3,7},{4,0},{5,1},{6,2},{7,3},{8,12},{9,13},{10,... | collective-permute-start | bytes 6152 | tf_op jit(solution)/shard_map/ppermute | solution.py:13
  6.3 2.9 %collective-permute-start.17 = (bf16[128,1280]{1,0:T(8,128)(2,1)}, bf16[128,1280]{1,0:T(8,128)(2,1)S(1)}, u32[]{:S(2)}, u32[]{:S(2)}) collective-permute-start(bf16[128,1280]{1,0:T(8,128)(2,1)} %param.9), channel_id=1, source_target_pairs={{0,4},{1,5},{2,6},{3,7},{4,0},{5,1},{6,2},{7,3},{8,12},{9,13},{10,... | collective-permute-start | bytes 983048 | tf_op jit(solution)/shard_map/ppermute | solution.py:13
  9.2 0.8 slice_bitcast_fusion.3
  10.0 0.8 select_reduce_fusion.3
  11.0 0.8 select_reduce_fusion.2
  12.3 0.8 bitcast_and_fusion.1
  13.1 1.3 convolution_convert_fusion.4
  14.8 0.9 constant_dynamic-update-slice_fusion.15
  15.6 2.5 %collective-permute-start.5 = (bf16[72,1280]{1,0:T(8,128)(2,1)}, bf16[72,1280]{1,0:T(8,128)(2,1)}, u32[]{:S(2)}, u32[]{:S(2)}) collective-permute-start(bf16[72,1280]{1,0:T(8,128)(2,1)} %get-tuple-element.41), channel_id=1, source_target_pairs={{0,3},{1,2},{2,1},{3,0},{4,7},{5,6},{6,5},{7,4},{8,11},{9,10},{10,... | collective-permute-start | bytes 552968 | tf_op jit(solution)/shard_map/ppermute | solution.py:13
  18.2 0.4 collective-permute-start.4
  18.6 0.5 collective-permute-start.3
  19.1 0.9 constant_dynamic-update-slice_fusion.7
  20.2 5.6 %collective-permute-done.5 = bf16[72,1280]{1,0:T(8,128)(2,1)} collective-permute-done((bf16[72,1280]{1,0:T(8,128)(2,1)}, bf16[72,1280]{1,0:T(8,128)(2,1)}, u32[]{:S(2)}, u32[]{:S(2)}) %collective-permute-start.5) | collective-permute-done | bytes 184352 | tf_op jit(solution)/shard_map/ppermute | solution.py:13
  25.8 3.4 %collective-permute-start.2 = (bf16[72,1280]{1,0:T(8,128)(2,1)}, bf16[72,1280]{1,0:T(8,128)(2,1)S(1)}, u32[]{:S(2)}, u32[]{:S(2)}) collective-permute-start(bf16[72,1280]{1,0:T(8,128)(2,1)} %get-tuple-element.51), channel_id=1, source_target_pairs={{0,3},{1,2},{2,1},{3,0},{4,7},{5,6},{6,5},{7,4},{8,11},{9,10},{10,... | collective-permute-start | bytes 552968 | tf_op jit(solution)/shard_map/ppermute | solution.py:13
  29.2 11.5 %collective-permute-done.4 = bf16[72,1280]{1,0:T(8,128)(2,1)} collective-permute-done((bf16[72,1280]{1,0:T(8,128)(2,1)}, bf16[72,1280]{1,0:T(8,128)(2,1)}, u32[]{:S(2)}, u32[]{:S(2)}) %collective-permute-start.4) | collective-permute-done | bytes 184352 | tf_op jit(solution)/shard_map/ppermute | solution.py:13
  40.8 3.1 %fusion.38 = bf16[288,1024]{1,0:T(8,128)(2,1)S(1)} fusion(bf16[1,1024,1280]{2,1,0:T(8,128)(2,1)} %param.15, bf16[72,1280]{1,0:T(8,128)(2,1)} %collective-permute-done.5, bf16[72,1280]{1,0:T(8,128)(2,1)} %collective-permute-done.4, bf16[72,1280]{1,0:T(8,128)(2,1)} %collective-permute-done.3, bf16[72,1280]{1,0:T(8,128)(2,1)S(1)} %get-tuple-element.44), kind=kOutput, calls=%fused_computation.48 | convolution fusion | flops 758218752 | bytes 3948544 | tf_op jit(solution)/shard_map/dot_general | solution.py:17
  44.0 3.1 %collective-permute-done.1 = bf16[72,1280]{1,0:T(8,128)(2,1)S(1)} collective-permute-done((bf16[72,1280]{1,0:T(8,128)(2,1)}, bf16[72,1280]{1,0:T(8,128)(2,1)S(1)}, u32[]{:S(2)}, u32[]{:S(2)}) %collective-permute-start.1) | collective-permute-done | bytes 184352 | tf_op jit(solution)/shard_map/ppermute | solution.py:13
  47.1 0.9 fusion.32
  48.1 0.9 fusion.26
  49.3 1.1 copy-done.12
  50.9 0.9 constant_dynamic-update-slice_fusion.14
  51.8 0.9 constant_dynamic-update-slice_fusion.13
  52.8 0.9 constant_dynamic-update-slice_fusion.12
  53.7 1.3 convolution_convert_fusion.3
  55.1 0.6 collective-permute-start.14
  55.7 1.0 collective-permute-start.15
  56.7 2.0 %collective-permute-start.16 = (bf16[72,1280]{1,0:T(8,128)(2,1)S(1)}, bf16[72,1280]{1,0:T(8,128)(2,1)S(1)}, u32[]{:S(2)}, u32[]{:S(2)}) collective-permute-start(bf16[72,1280]{1,0:T(8,128)(2,1)S(1)} %get-tuple-element.47), channel_id=1, source_target_pairs={{0,3},{1,2},{2,1},{3,0},{4,7},{5,6},{6,5},{7,4},{8,11},{9,10},{10,... | collective-permute-start | bytes 552968 | tf_op jit(solution)/shard_map/ppermute | solution.py:13
  59.1 1.0 collective-permute-start.20
  60.1 1.8 %collective-permute-done.14 = bf16[72,1280]{1,0:T(8,128)(2,1)S(1)} collective-permute-done((bf16[72,1280]{1,0:T(8,128)(2,1)S(1)}, bf16[72,1280]{1,0:T(8,128)(2,1)S(1)}, u32[]{:S(2)}, u32[]{:S(2)}) %collective-permute-start.14) | collective-permute-done | bytes 184352 | tf_op jit(solution)/shard_map/ppermute | solution.py:13
  61.8 1.4 collective-permute-start.19
  63.3 1.5 %collective-permute-start.18 = (bf16[72,1280]{1,0:T(8,128)(2,1)S(1)}, bf16[72,1280]{1,0:T(8,128)(2,1)S(1)}, u32[]{:S(2)}, u32[]{:S(2)}) collective-permute-start(bf16[72,1280]{1,0:T(8,128)(2,1)S(1)} %get-tuple-element.38), channel_id=1, source_target_pairs={{0,1},{1,0},{2,3},{3,2},{4,5},{5,4},{6,7},{7,6},{8,9},{9,8},{10,11... | collective-permute-start | bytes 552968 | tf_op jit(solution)/shard_map/ppermute | solution.py:13
  64.8 3.4 %collective-permute-done.16 = bf16[72,1280]{1,0:T(8,128)(2,1)S(1)} collective-permute-done((bf16[72,1280]{1,0:T(8,128)(2,1)S(1)}, bf16[72,1280]{1,0:T(8,128)(2,1)S(1)}, u32[]{:S(2)}, u32[]{:S(2)}) %collective-permute-start.16) | collective-permute-done | bytes 184352 | tf_op jit(solution)/shard_map/ppermute | solution.py:13
  68.2 0.9 fusion.35
  69.1 1.0 fusion.29
  70.1 1.7 %collective-permute-done.20 = bf16[72,1280]{1,0:T(8,128)(2,1)S(1)} collective-permute-done((bf16[72,1280]{1,0:T(8,128)(2,1)S(1)}, bf16[72,1280]{1,0:T(8,128)(2,1)S(1)}, u32[]{:S(2)}, u32[]{:S(2)}) %collective-permute-start.20) | collective-permute-done | bytes 184352 | tf_op jit(solution)/shard_map/ppermute | solution.py:13
  71.8 1.7 %collective-permute-done.19 = bf16[72,1280]{1,0:T(8,128)(2,1)S(1)} collective-permute-done((bf16[72,1280]{1,0:T(8,128)(2,1)S(1)}, bf16[72,1280]{1,0:T(8,128)(2,1)S(1)}, u32[]{:S(2)}, u32[]{:S(2)}) %collective-permute-start.19) | collective-permute-done | bytes 184352 | tf_op jit(solution)/shard_map/ppermute | solution.py:13
  73.5 1.0 fusion.41
  75.1 1.6 %collective-permute-start.7 = (bf16[288,1536]{1,0:T(8,128)(2,1)S(1)}, bf16[288,1536]{1,0:T(8,128)(2,1)S(1)}, u32[]{:S(2)}, u32[]{:S(2)}) collective-permute-start(bf16[288,1536]{1,0:T(8,128)(2,1)S(1)} %add_convert_fusion.3), channel_id=1, source_target_pairs={{0,16},{8,24},{16,0},{24,8},{1,17},{9,25},{17,1},{25,9},{2,18},{10... | collective-permute-start | bytes 2654216 | tf_op jit(solution)/shard_map/ppermute | solution.py:13
  76.7 0.5 collective-permute-done.21
  77.8 1.2 collective-permute-start.22
  79.1 18.6 %collective-permute-done.7 = bf16[288,1536]{1,0:T(8,128)(2,1)S(1)} collective-permute-done((bf16[288,1536]{1,0:T(8,128)(2,1)S(1)}, bf16[288,1536]{1,0:T(8,128)(2,1)S(1)}, u32[]{:S(2)}, u32[]{:S(2)}) %collective-permute-start.7) | collective-permute-done | bytes 884768 | tf_op jit(solution)/shard_map/ppermute | solution.py:13
  98.0 18.2 %collective-permute-done.22 = bf16[288,1536]{1,0:T(8,128)(2,1)S(1)} collective-permute-done((bf16[288,1536]{1,0:T(8,128)(2,1)S(1)}, bf16[288,1536]{1,0:T(8,128)(2,1)S(1)}, u32[]{:S(2)}, u32[]{:S(2)}) %collective-permute-start.22) | collective-permute-done | bytes 884768 | tf_op jit(solution)/shard_map/ppermute | solution.py:13
  117.1 2.1 %multiply_reduce_fusion = (f32[288]{0:T(512)S(1)}, bf16[288,1024]{1,0:T(8,128)(2,1)}, bf16[288,1024]{1,0:T(8,128)(2,1)}, bf16[288,1024]{1,0:T(8,128)(2,1)}) fusion(f32[288,512]{1,0:T(8,128)S(1)} %get-tuple-element.27, f32[288,512]{1,0:T(8,128)S(1)} %get-tuple-element.24, f32[288,512]{1,0:T(8,128)S(1)} %get-tuple-element.28, ...), kind=kLoop, calls=%fused_computation.70 | loop fusion | flops 6192864 | bytes 5309568 | tf_op jit(solution)/shard_map/reduce_sum | solution.py:104
  119.2 0.8 copy.17
  120.0 2.2 %fusion.19 = f32[288,1280]{1,0:T(8,128)S(1)} fusion(bf16[288,1024]{1,0:T(8,128)(2,1)} %get-tuple-element.10, bf16[1,1280,1024]{2,1,0:T(8,128)(2,1)S(1)} %copy-done), kind=kOutput, calls=%fused_computation.29 | convolution fusion | flops 754974720 | bytes 4685824 | tf_op jit(solution)/shard_map/dot_general | solution.py:17
  122.2 1.1 convolution_convert_fusion.5
  123.4 0.8 copy-done.19
  124.1 1.0 fusion.5
  125.4 1.7 %collective-permute-start.11 = (bf16[72,2688]{1,0:T(8,128)(2,1)S(1)}, bf16[72,2688]{1,0:T(8,128)(2,1)S(1)}, u32[]{:S(2)}, u32[]{:S(2)}) collective-permute-start(bf16[72,2688]{1,0:T(8,128)(2,1)S(1)} %get-tuple-element.32), channel_id=1, source_target_pairs={{0,3},{1,2},{2,1},{3,0},{4,7},{5,6},{6,5},{7,4},{8,11},{9,10},{10,... | collective-permute-start | bytes 1161224 | tf_op jit(solution)/shard_map/ppermute | solution.py:13
  127.1 0.6 collective-permute-start.10
  127.7 1.2 collective-permute-start.9
  129.0 1.4 select_convert_fusion.1
  130.7 0.9 multiply_convert_fusion
  131.7 0.5 copy-done.14
  132.2 3.7 %fusion = bf16[1,1280,1024]{2,1,0:T(8,128)(2,1)} fusion(bf16[576,1280]{1,0:T(8,128)(2,1)S(1)} %copy-done.14, bf16[288,1024]{1,0:T(8,128)(2,1)S(1)} %get-tuple-element.12, bf16[288,1024]{1,0:T(8,128)(2,1)S(1)} %copy-done.4), kind=kOutput, calls=%fused_computation.3 | convolution fusion | flops 1513619456 | bytes 5275648 | tf_op jit(solution)/shard_map/dot_general | solution.py:17
  136.0 3.7 %fusion.1 = bf16[1,1280,1024]{2,1,0:T(8,128)(2,1)} fusion(bf16[576,1280]{1,0:T(8,128)(2,1)S(1)} %copy-done.14, bf16[288,1024]{1,0:T(8,128)(2,1)S(1)} %get-tuple-element.13, bf16[288,1024]{1,0:T(8,128)(2,1)S(1)} %copy-done.3), kind=kOutput, calls=%fused_computation.4 | convolution fusion | flops 1513619456 | bytes 5275648 | tf_op jit(solution)/shard_map/dot_general | solution.py:17
  139.7 3.8 %fusion.2 = bf16[1,1024,1280]{2,1,0:T(8,128)(2,1)} fusion(bf16[576,1280]{1,0:T(8,128)(2,1)S(1)} %copy-done.11, bf16[288,1024]{1,0:T(8,128)(2,1)S(1)} %get-tuple-element.11, bf16[288,1024]{1,0:T(8,128)(2,1)S(1)} %copy-done.2), kind=kOutput, calls=%fused_computation.5 | convolution fusion | flops 1513619456 | bytes 5275648 | tf_op jit(solution)/shard_map/dot_general | solution.py:17
  143.5 1.9 %collective-permute-done.10 = bf16[72,2688]{1,0:T(8,128)(2,1)S(1)} collective-permute-done((bf16[72,2688]{1,0:T(8,128)(2,1)S(1)}, bf16[72,2688]{1,0:T(8,128)(2,1)S(1)}, u32[]{:S(2)}, u32[]{:S(2)}) %collective-permute-start.10) | collective-permute-done | bytes 387104 | tf_op jit(solution)/shard_map/ppermute | solution.py:13
  145.4 0.6 collective-permute-done.9
  146.1 1.1 convolution_convert_fusion.6
  148.3 1.1 fusion.24
  149.4 0.6 maximum_divide_fusion
  (109 shorter events, 6.7 us)
Async XLA Ops:
  0.6 47.4 %copy-start = (bf16[1,1280,1024]{2,1,0:T(8,128)(2,1)S(1)}, bf16[1,1280,1024]{2,1,0:T(8,128)(2,1)}, u32[]{:S(2)}) copy-start(bf16[1,1280,1024]{2,1,0:T(8,128)(2,1)} %param.13) | copy-start | bytes 7864324
  0.6 13.7 %copy-start.7 = (bf16[128,1280]{1,0:T(8,128)(2,1)S(1)}, bf16[128,1280]{1,0:T(8,128)(2,1)}, u32[]{:S(2)}) copy-start(bf16[128,1280]{1,0:T(8,128)(2,1)} %param.9) | copy-start | bytes 983044
  2.2 8.7 %collective-permute-start.12 = (f32[4,128]{1,0:T(4,128)S(1)}, f32[4,128]{1,0:T(4,128)S(1)}, u32[]{:S(2)}, u32[]{:S(2)}) collective-permute-start(f32[4,128]{1,0:T(4,128)S(1)} %pad_maximum_fusion.16), channel_id=1, source_target_pairs={{0,4},{1,5},{2,6},{3,7},{4,0},{5,1},{6,2},{7,3},{8,12},{9,13},{10,... | collective-permute-start | bytes 6152 | tf_op jit(solution)/shard_map/ppermute | solution.py:13
  6.3 47.4 %collective-permute-start.13 = (bf16[128,1280]{1,0:T(8,128)(2,1)}, bf16[128,1280]{1,0:T(8,128)(2,1)}, u32[]{:S(2)}, u32[]{:S(2)}) collective-permute-start(bf16[128,1280]{1,0:T(8,128)(2,1)} %param.8), channel_id=1, source_target_pairs={{0,4},{1,5},{2,6},{3,7},{4,0},{5,1},{6,2},{7,3},{8,12},{9,13},{10,... | collective-permute-start | bytes 983048 | tf_op jit(solution)/shard_map/ppermute | solution.py:13
  6.3 52.3 %collective-permute-start.17 = (bf16[128,1280]{1,0:T(8,128)(2,1)}, bf16[128,1280]{1,0:T(8,128)(2,1)S(1)}, u32[]{:S(2)}, u32[]{:S(2)}) collective-permute-start(bf16[128,1280]{1,0:T(8,128)(2,1)} %param.9), channel_id=1, source_target_pairs={{0,4},{1,5},{2,6},{3,7},{4,0},{5,1},{6,2},{7,3},{8,12},{9,13},{10,... | collective-permute-start | bytes 983048 | tf_op jit(solution)/shard_map/ppermute | solution.py:13
  15.6 10.2 %collective-permute-start.5 = (bf16[72,1280]{1,0:T(8,128)(2,1)}, bf16[72,1280]{1,0:T(8,128)(2,1)}, u32[]{:S(2)}, u32[]{:S(2)}) collective-permute-start(bf16[72,1280]{1,0:T(8,128)(2,1)} %get-tuple-element.41), channel_id=1, source_target_pairs={{0,3},{1,2},{2,1},{3,0},{4,7},{5,6},{6,5},{7,4},{8,11},{9,10},{10,... | collective-permute-start | bytes 552968 | tf_op jit(solution)/shard_map/ppermute | solution.py:13
  18.2 22.6 %collective-permute-start.4 = (bf16[72,1280]{1,0:T(8,128)(2,1)}, bf16[72,1280]{1,0:T(8,128)(2,1)}, u32[]{:S(2)}, u32[]{:S(2)}) collective-permute-start(bf16[72,1280]{1,0:T(8,128)(2,1)} %get-tuple-element.42), channel_id=1, source_target_pairs={{0,2},{1,3},{2,0},{3,1},{4,6},{5,7},{6,4},{7,5},{8,10},{9,11},{10,... | collective-permute-start | bytes 552968 | tf_op jit(solution)/shard_map/ppermute | solution.py:13
  18.6 22.1 %collective-permute-start.3 = (bf16[72,1280]{1,0:T(8,128)(2,1)}, bf16[72,1280]{1,0:T(8,128)(2,1)}, u32[]{:S(2)}, u32[]{:S(2)}) collective-permute-start(bf16[72,1280]{1,0:T(8,128)(2,1)} %get-tuple-element.43), channel_id=1, source_target_pairs={{0,1},{1,0},{2,3},{3,2},{4,5},{5,4},{6,7},{7,6},{8,9},{9,8},{10,11... | collective-permute-start | bytes 552968 | tf_op jit(solution)/shard_map/ppermute | solution.py:13
  25.8 18.1 %collective-permute-start.2 = (bf16[72,1280]{1,0:T(8,128)(2,1)}, bf16[72,1280]{1,0:T(8,128)(2,1)S(1)}, u32[]{:S(2)}, u32[]{:S(2)}) collective-permute-start(bf16[72,1280]{1,0:T(8,128)(2,1)} %get-tuple-element.51), channel_id=1, source_target_pairs={{0,3},{1,2},{2,1},{3,0},{4,7},{5,6},{6,5},{7,4},{8,11},{9,10},{10,... | collective-permute-start | bytes 552968 | tf_op jit(solution)/shard_map/ppermute | solution.py:13
  40.7 6.4 %collective-permute-start.1 = (bf16[72,1280]{1,0:T(8,128)(2,1)}, bf16[72,1280]{1,0:T(8,128)(2,1)S(1)}, u32[]{:S(2)}, u32[]{:S(2)}) collective-permute-start(bf16[72,1280]{1,0:T(8,128)(2,1)} %get-tuple-element.52), channel_id=1, source_target_pairs={{0,2},{1,3},{2,0},{3,1},{4,6},{5,7},{6,4},{7,5},{8,10},{9,11},{10,... | collective-permute-start | bytes 552968 | tf_op jit(solution)/shard_map/ppermute | solution.py:13
  40.7 6.4 %collective-permute-start = (bf16[72,1280]{1,0:T(8,128)(2,1)}, bf16[72,1280]{1,0:T(8,128)(2,1)S(1)}, u32[]{:S(2)}, u32[]{:S(2)}) collective-permute-start(bf16[72,1280]{1,0:T(8,128)(2,1)} %get-tuple-element.53), channel_id=1, source_target_pairs={{0,1},{1,0},{2,3},{3,2},{4,5},{5,4},{6,7},{7,6},{8,9},{9,8},{10,11... | collective-permute-start | bytes 552968 | tf_op jit(solution)/shard_map/ppermute | solution.py:13
  40.8 6.4 %copy-start.18 = (bf16[1,1280,1024]{2,1,0:T(8,128)(2,1)S(1)}, bf16[1,1280,1024]{2,1,0:T(8,128)(2,1)}, u32[]{:S(2)}) copy-start(bf16[1,1280,1024]{2,1,0:T(8,128)(2,1)} %param.14) | copy-start | bytes 7864324
  49.0 1.4 copy-start.12
  49.2 1.7 %copy-start.9 = (bf16[576,1280]{1,0:T(8,128)(2,1)S(1)}, bf16[576,1280]{1,0:T(8,128)(2,1)}, u32[]{:S(2)}) copy-start(bf16[576,1280]{1,0:T(8,128)(2,1)} %get-tuple-element.40) | copy-start | bytes 4423684
  49.3 25.6 %collective-permute-start.6 = (bf16[288,1536]{1,0:T(8,128)(2,1)S(1)}, bf16[288,1536]{1,0:T(8,128)(2,1)S(1)}, u32[]{:S(2)}, u32[]{:S(2)}) collective-permute-start(bf16[288,1536]{1,0:T(8,128)(2,1)S(1)} %pad_maximum_fusion.7), channel_id=1, source_target_pairs={{0,8},{8,0},{16,24},{24,16},{1,9},{9,1},{17,25},{25,17},{2,10},{10... | collective-permute-start | bytes 2654216 | tf_op jit(solution)/shard_map/ppermute | solution.py:13
  55.1 6.7 %collective-permute-start.14 = (bf16[72,1280]{1,0:T(8,128)(2,1)S(1)}, bf16[72,1280]{1,0:T(8,128)(2,1)S(1)}, u32[]{:S(2)}, u32[]{:S(2)}) collective-permute-start(bf16[72,1280]{1,0:T(8,128)(2,1)S(1)} %get-tuple-element.49), channel_id=1, source_target_pairs={{0,1},{1,0},{2,3},{3,2},{4,5},{5,4},{6,7},{7,6},{8,9},{9,8},{10,11... | collective-permute-start | bytes 552968 | tf_op jit(solution)/shard_map/ppermute | solution.py:13
  55.7 7.6 %collective-permute-start.15 = (bf16[72,1280]{1,0:T(8,128)(2,1)S(1)}, bf16[72,1280]{1,0:T(8,128)(2,1)S(1)}, u32[]{:S(2)}, u32[]{:S(2)}) collective-permute-start(bf16[72,1280]{1,0:T(8,128)(2,1)S(1)} %get-tuple-element.48), channel_id=1, source_target_pairs={{0,2},{1,3},{2,0},{3,1},{4,6},{5,7},{6,4},{7,5},{8,10},{9,11},{10,... | collective-permute-start | bytes 552968 | tf_op jit(solution)/shard_map/ppermute | solution.py:13
  56.7 11.5 %collective-permute-start.16 = (bf16[72,1280]{1,0:T(8,128)(2,1)S(1)}, bf16[72,1280]{1,0:T(8,128)(2,1)S(1)}, u32[]{:S(2)}, u32[]{:S(2)}) collective-permute-start(bf16[72,1280]{1,0:T(8,128)(2,1)S(1)} %get-tuple-element.47), channel_id=1, source_target_pairs={{0,3},{1,2},{2,1},{3,0},{4,7},{5,6},{6,5},{7,4},{8,11},{9,10},{10,... | collective-permute-start | bytes 552968 | tf_op jit(solution)/shard_map/ppermute | solution.py:13
  59.1 12.7 %collective-permute-start.20 = (bf16[72,1280]{1,0:T(8,128)(2,1)S(1)}, bf16[72,1280]{1,0:T(8,128)(2,1)S(1)}, u32[]{:S(2)}, u32[]{:S(2)}) collective-permute-start(bf16[72,1280]{1,0:T(8,128)(2,1)S(1)} %get-tuple-element.36), channel_id=1, source_target_pairs={{0,3},{1,2},{2,1},{3,0},{4,7},{5,6},{6,5},{7,4},{8,11},{9,10},{10,... | collective-permute-start | bytes 552968 | tf_op jit(solution)/shard_map/ppermute | solution.py:13
  61.8 11.7 %collective-permute-start.19 = (bf16[72,1280]{1,0:T(8,128)(2,1)S(1)}, bf16[72,1280]{1,0:T(8,128)(2,1)S(1)}, u32[]{:S(2)}, u32[]{:S(2)}) collective-permute-start(bf16[72,1280]{1,0:T(8,128)(2,1)S(1)} %get-tuple-element.37), channel_id=1, source_target_pairs={{0,2},{1,3},{2,0},{3,1},{4,6},{5,7},{6,4},{7,5},{8,10},{9,11},{10,... | collective-permute-start | bytes 552968 | tf_op jit(solution)/shard_map/ppermute | solution.py:13
  63.3 10.3 %collective-permute-start.18 = (bf16[72,1280]{1,0:T(8,128)(2,1)S(1)}, bf16[72,1280]{1,0:T(8,128)(2,1)S(1)}, u32[]{:S(2)}, u32[]{:S(2)}) collective-permute-start(bf16[72,1280]{1,0:T(8,128)(2,1)S(1)} %get-tuple-element.38), channel_id=1, source_target_pairs={{0,1},{1,0},{2,3},{3,2},{4,5},{5,4},{6,7},{7,6},{8,9},{9,8},{10,11... | collective-permute-start | bytes 552968 | tf_op jit(solution)/shard_map/ppermute | solution.py:13
  69.1 4.4 %copy-start.16 = (bf16[1,1024,1280]{2,1,0:T(8,128)(2,1)S(1)}, bf16[1,1024,1280]{2,1,0:T(8,128)(2,1)}, u32[]{:S(2)}) copy-start(bf16[1,1024,1280]{2,1,0:T(8,128)(2,1)} %param.15) | copy-start | bytes 7864324
  74.8 2.5 %collective-permute-start.21 = (bf16[288,1536]{1,0:T(8,128)(2,1)S(1)}, bf16[288,1536]{1,0:T(8,128)(2,1)S(1)}, u32[]{:S(2)}, u32[]{:S(2)}) collective-permute-start(bf16[288,1536]{1,0:T(8,128)(2,1)S(1)} %pad_maximum_fusion.8), channel_id=1, source_target_pairs={{0,8},{8,0},{16,24},{24,16},{1,9},{9,1},{17,25},{25,17},{2,10},{10... | collective-permute-start | bytes 2654216 | tf_op jit(solution)/shard_map/ppermute | solution.py:13
  75.1 22.5 %collective-permute-start.7 = (bf16[288,1536]{1,0:T(8,128)(2,1)S(1)}, bf16[288,1536]{1,0:T(8,128)(2,1)S(1)}, u32[]{:S(2)}, u32[]{:S(2)}) collective-permute-start(bf16[288,1536]{1,0:T(8,128)(2,1)S(1)} %add_convert_fusion.3), channel_id=1, source_target_pairs={{0,16},{8,24},{16,0},{24,8},{1,17},{9,25},{17,1},{25,9},{2,18},{10... | collective-permute-start | bytes 2654216 | tf_op jit(solution)/shard_map/ppermute | solution.py:13
  76.7 1.1 copy-start.13
  77.8 38.4 %collective-permute-start.22 = (bf16[288,1536]{1,0:T(8,128)(2,1)S(1)}, bf16[288,1536]{1,0:T(8,128)(2,1)S(1)}, u32[]{:S(2)}, u32[]{:S(2)}) collective-permute-start(bf16[288,1536]{1,0:T(8,128)(2,1)S(1)} %add_convert_fusion.1), channel_id=1, source_target_pairs={{0,16},{8,24},{16,0},{24,8},{1,17},{9,25},{17,1},{25,9},{2,18},{10... | collective-permute-start | bytes 2654216 | tf_op jit(solution)/shard_map/ppermute | solution.py:13
  97.9 18.7 %collective-permute-start.8 = (bf16[288,1536]{1,0:T(8,128)(2,1)S(1)}, bf16[288,1536]{1,0:T(8,128)(2,1)S(1)}, u32[]{:S(2)}, u32[]{:S(2)}) collective-permute-start(bf16[288,1536]{1,0:T(8,128)(2,1)S(1)} %add_convert_fusion.2), channel_id=1, source_target_pairs={{0,8},{8,0},{16,24},{24,16},{1,9},{9,1},{17,25},{25,17},{2,10},{10... | collective-permute-start | bytes 2654216 | tf_op jit(solution)/shard_map/ppermute | solution.py:13
  98.0 18.5 %copy-start.10 = (bf16[576,1280]{1,0:T(8,128)(2,1)}, bf16[576,1280]{1,0:T(8,128)(2,1)S(1)}, u32[]{:S(2)}) copy-start(bf16[576,1280]{1,0:T(8,128)(2,1)S(1)} %constant_dynamic-update-slice_fusion.8) | copy-start | bytes 4423684
  116.4 12.5 %collective-permute-start.23 = (bf16[288,1536]{1,0:T(8,128)(2,1)S(1)}, bf16[288,1536]{1,0:T(8,128)(2,1)}, u32[]{:S(2)}, u32[]{:S(2)}) collective-permute-start(bf16[288,1536]{1,0:T(8,128)(2,1)S(1)} %add_convert_fusion), channel_id=1, source_target_pairs={{0,8},{8,0},{16,24},{24,16},{1,9},{9,1},{17,25},{25,17},{2,10},{10... | collective-permute-start | bytes 2654216 | tf_op jit(solution)/shard_map/ppermute | solution.py:13
  120.0 2.2 %copy-start.2 = (bf16[288,1024]{1,0:T(8,128)(2,1)S(1)}, bf16[288,1024]{1,0:T(8,128)(2,1)}, u32[]{:S(2)}) copy-start(bf16[288,1024]{1,0:T(8,128)(2,1)} %get-tuple-element.7) | copy-start | bytes 1769476
  120.0 2.2 %copy-start.17 = (bf16[1,1024,1280]{2,1,0:T(8,128)(2,1)S(1)}, bf16[1,1024,1280]{2,1,0:T(8,128)(2,1)}, u32[]{:S(2)}) copy-start(bf16[1,1024,1280]{2,1,0:T(8,128)(2,1)} %param.15) | copy-start | bytes 7864324
  122.2 1.2 copy-start.3
  122.2 1.9 %copy-start.19 = (bf16[1,1280,1024]{2,1,0:T(8,128)(2,1)S(1)}, bf16[1,1280,1024]{2,1,0:T(8,128)(2,1)}, u32[]{:S(2)}) copy-start(bf16[1,1280,1024]{2,1,0:T(8,128)(2,1)} %param.14) | copy-start | bytes 7864324
  124.1 1.0 copy-start.8
  125.4 18.1 %collective-permute-start.11 = (bf16[72,2688]{1,0:T(8,128)(2,1)S(1)}, bf16[72,2688]{1,0:T(8,128)(2,1)S(1)}, u32[]{:S(2)}, u32[]{:S(2)}) collective-permute-start(bf16[72,2688]{1,0:T(8,128)(2,1)S(1)} %get-tuple-element.32), channel_id=1, source_target_pairs={{0,3},{1,2},{2,1},{3,0},{4,7},{5,6},{6,5},{7,4},{8,11},{9,10},{10,... | collective-permute-start | bytes 1161224 | tf_op jit(solution)/shard_map/ppermute | solution.py:13
  127.1 18.3 %collective-permute-start.10 = (bf16[72,2688]{1,0:T(8,128)(2,1)S(1)}, bf16[72,2688]{1,0:T(8,128)(2,1)S(1)}, u32[]{:S(2)}, u32[]{:S(2)}) collective-permute-start(bf16[72,2688]{1,0:T(8,128)(2,1)S(1)} %get-tuple-element.33), channel_id=1, source_target_pairs={{0,2},{1,3},{2,0},{3,1},{4,6},{5,7},{6,4},{7,5},{8,10},{9,11},{10,... | collective-permute-start | bytes 1161224 | tf_op jit(solution)/shard_map/ppermute | solution.py:13
  127.7 18.3 %collective-permute-start.9 = (bf16[72,2688]{1,0:T(8,128)(2,1)S(1)}, bf16[72,2688]{1,0:T(8,128)(2,1)S(1)}, u32[]{:S(2)}, u32[]{:S(2)}) collective-permute-start(bf16[72,2688]{1,0:T(8,128)(2,1)S(1)} %get-tuple-element.34), channel_id=1, source_target_pairs={{0,1},{1,0},{2,3},{3,2},{4,5},{5,4},{6,7},{7,6},{8,9},{9,8},{10,11... | collective-permute-start | bytes 1161224 | tf_op jit(solution)/shard_map/ppermute | solution.py:13
  130.7 1.1 copy-start.4
  130.7 1.6 %copy-start.14 = (bf16[576,1280]{1,0:T(8,128)(2,1)S(1)}, bf16[576,1280]{1,0:T(8,128)(2,1)}, u32[]{:S(2)}) copy-start(bf16[576,1280]{1,0:T(8,128)(2,1)} %copy-done.13) | copy-start | bytes 4423684
  136.0 3.7 %copy-start.11 = (bf16[576,1280]{1,0:T(8,128)(2,1)S(1)}, bf16[576,1280]{1,0:T(8,128)(2,1)}, u32[]{:S(2)}) copy-start(bf16[576,1280]{1,0:T(8,128)(2,1)} %copy-done.10) | copy-start | bytes 4423684
  146.0 1.2 copy-start.6
  147.3 0.8 copy-start.5
  147.3 2.7 %copy-start.1 = (bf16[1,1280,1024]{2,1,0:T(8,128)(2,1)S(1)}, bf16[1,1280,1024]{2,1,0:T(8,128)(2,1)}, u32[]{:S(2)}) copy-start(bf16[1,1280,1024]{2,1,0:T(8,128)(2,1)} %param.13) | copy-start | bytes 7864324
  147.7 1.7 %copy-start.15 = (f32[128,2]{0,1:T(2,128)S(1)}, f32[128,2]{0,1:T(2,128)}, u32[]{:S(2)}) copy-start(f32[128,2]{0,1:T(2,128)} %param.10) | copy-start | bytes 3076

commit v2 on v1

v2 whole, which is shorter than its diff:
```python
import functools

import jax
import jax.numpy as jnp
from jax import lax
from jax.experimental import pallas as pl
from jax.experimental.pallas import tpu as pltpu
from jax.sharding import PartitionSpec as P

HALF = 36
CAP = 2 * HALF
EXTRA = 128
BLOCK = 32
FIRST = (((0,), (0,)), ((), ()))
SECOND = (((1,), (1,)), ((), ()))
PLAIN = (((1,), (0,)), ((), ()))
F32 = jnp.float32
BF16 = jnp.bfloat16

VMEM = pl.BlockSpec(memory_space=pltpu.VMEM)
SMEM = pl.BlockSpec(memory_space=pltpu.SMEM)
ANY = pl.BlockSpec(memory_space=pl.ANY)


def hop(x, axis, distance):
    return lax.ppermute(x, axis, [(i, i ^ distance) for i in range(lax.axis_size(axis))])


def after(x, *first):
    return lax.optimization_barrier((x, *first))[0]


def dot32(a, b, dims=PLAIN):
    return lax.dot_general(a, b, dims, preferred_element_type=F32)


def struct(shape, dtype=BF16):
    return jax.ShapeDtypeStruct(shape, dtype)


def call(kernel, name, out_shape, in_specs, out_specs, scratch=(), mib=20):
    return pl.pallas_call(
        kernel,
        out_shape=out_shape,
        in_specs=in_specs,
        out_specs=out_specs,
        scratch_shapes=scratch,
        compiler_params=pltpu.CompilerParams(vmem_limit_bytes=mib * 2**20),
        cost_estimate=pl.CostEstimate(flops=1024, bytes_accessed=1 << 19, transcendentals=0),
        name=name,
    )


def row_slots(pairs_ref):
    pairs = pairs_ref.shape[0]
    low = lax.axis_index("expert") % pairs
    at = lax.broadcasted_iota(jnp.int32, (pairs * CAP, 1), 0)
    name = jnp.full(at.shape, pairs_ref[low], jnp.int32)
    place = at
    for d in range(1, pairs):
        later = at >= d * CAP
        name = jnp.where(later, pairs_ref[low ^ d], name)
        place = jnp.where(later, at - d * CAP, place)
    return name.astype(F32), place.astype(F32)


def pick_rows(routes, gates, pairs_ref):
    top, tok = routes.shape
    name, place = row_slots(pairs_ref)
    gate = jnp.zeros((name.shape[0], tok), F32)
    named = jnp.zeros((name.shape[0], tok), F32)
    hits = [routes[k : k + 1] == name for k in range(top)]
    for k in range(top):
        named = jnp.where(hits[k], 1.0, named)
        gate = jnp.where(hits[k], gates[k : k + 1], gate)
    earlier = (
        lax.broadcasted_iota(jnp.int32, (tok, tok), 0) < lax.broadcasted_iota(jnp.int32, (tok, tok), 1)
    )
    before = dot32(named.astype(BF16), jnp.where(earlier, 1.0, 0.0).astype(BF16))
    return jnp.where(before == place, named, 0.0), gate, hits


def put_chunks(rows, refs):
    for d, ref in enumerate(refs):
        ref[...] = rows[d * CAP : (d + 1) * CAP].astype(BF16)


def join(refs):
    return jnp.concatenate([r[...].astype(F32) for r in refs], axis=0).astype(BF16)


def pack_own_kernel(pairs, pairs_ref, routes_ref, gates_ref, tok_ref, grad_ref, far_ref, *outs):
    top, tok = routes_ref.shape
    width = tok_ref.shape[1]
    routes = routes_ref[...].astype(F32)
    gates = gates_ref[...]
    far_ref[:, :width] = tok_ref[...]
    high = gates.astype(BF16).astype(F32)
    mid = (gates - high).astype(BF16).astype(F32)
    filler = jnp.zeros((EXTRA - 4 * top, tok), F32)
    info = jnp.concatenate([routes, high, mid, gates - high - mid, filler], axis=0)
    far_ref[:, width:] = info.T.astype(BF16)
    pick, gate, _ = pick_rows(routes, gates, pairs_ref)
    row_gate = jnp.sum(pick * gate, axis=1, keepdims=True)
    pick = pick.astype(BF16)
    put_chunks(dot32(pick, tok_ref[...]), [ref.at[:, :width] for ref in outs])
    put_chunks(dot32(pick, grad_ref[...]) * row_gate, [ref.at[:, width:] for ref in outs])


def pack_own(expert_pairs, routes, gates, tokens, out_grad):
    tok, width = tokens.shape
    pairs = expert_pairs.shape[0]
    out = call(
        functools.partial(pack_own_kernel, pairs),
        "pack_own",
        [struct((tok, width + EXTRA))] + [struct((CAP, 2 * width))] * pairs,
        [SMEM] + [VMEM] * 4,
        [VMEM] * (1 + pairs),
        mib=PACK_MIB,
    )(expert_pairs, routes, gates, tokens, out_grad)
    return out[0], list(out[1:])


PACK_MIB = 56


def pack_far_kernel(top, pairs_ref, far_ref, grad_ref, *outs):
    width = grad_ref.shape[1]
    info = far_ref[:, width:].astype(F32).T
    gates = info[top : 2 * top] + info[2 * top : 3 * top] + info[3 * top : 4 * top]
    pick, gate, _ = pick_rows(info[:top], gates, pairs_ref)
    row_gate = jnp.sum(pick * gate, axis=1, keepdims=True)
    pick = pick.astype(BF16)
    put_chunks(dot32(pick, far_ref[:, :width]), [ref.at[:, :width] for ref in outs])
    put_chunks(dot32(pick, grad_ref[...]) * row_gate, [ref.at[:, width:] for ref in outs])


def pack_far(expert_pairs, far, out_grad, top):
    pairs = expert_pairs.shape[0]
    out = call(
        functools.partial(pack_far_kernel, top),
        "pack_far",
        [struct((CAP, 2 * out_grad.shape[1]))] * pairs,
        [SMEM, VMEM, VMEM],
        [VMEM] * pairs,
    )(expert_pairs, far, out_grad)
    return list(out)


def dispatch(chunks, ordered=True):
    pairs = len(chunks)
    split = pairs - pairs // 4 if ordered else pairs
    near = [chunks[0]] + [hop(chunks[d], "expert", d) for d in range(1, split)]
    rest = [hop(after(chunks[d], *near[1:]), "expert", d) for d in range(split, pairs)]
    return near + rest


def load_kernel(*refs):
    copies = [pltpu.make_async_copy(refs[i], refs[3 + i], refs[6].at[i]) for i in range(3)]
    for copy in copies:
        copy.start()
    for copy in copies:
        copy.wait()


def load(weights):
    return call(
        load_kernel,
        "load",
        [struct(w.shape) for w in weights],
        [ANY] * 3,
        [VMEM] * 3,
        [pltpu.SemaphoreType.DMA((3,))],
    )(*weights)


def terms_kernel(count, *refs):
    chunks, (w_gate, w_up, w_down, rows_ref, cot_ref, send_ref, keep_ref) = refs[:count], refs[count:]
    half = send_ref.shape[2]
    width = rows_ref.shape[1]
    core = lax.axis_index("dp") % 2
    rows_ref[...] = join([ref.at[:, :width] for ref in chunks])
    cot_ref[...] = join([ref.at[:, width:] for ref in chunks])
    for ref, side in ((send_ref, 1 - core), (keep_ref, core)):
        at = pl.ds(pl.multiple_of(side * half, half), half)
        ref[0] = dot32(rows_ref[...], w_gate[:, at]).astype(BF16)
        ref[1] = dot32(rows_ref[...], w_up[:, at]).astype(BF16)
        ref[2] = dot32(cot_ref[...], w_down[at, :], SECOND).astype(BF16)


def terms(chunks, weights):
    total, width = len(chunks) * CAP, chunks[0].shape[1] // 2
    out = struct((3, total, weights[0].shape[1] // 2))
    return call(
        functools.partial(terms_kernel, len(chunks)),
        "terms",
        [struct((total, width))] * 2 + [out, out],
        [VMEM] * (len(chunks) + 3),
        [VMEM] * 4,
    )(*chunks, *weights)


def add_kernel(*refs):
    *parts, out = refs
    for i in range(out.shape[0]):
        sums = [a[i].astype(F32) + b[i].astype(F32) for a, b in zip(parts[::2], parts[1::2])]
        out[i] = jnp.concatenate(sums, axis=0).astype(BF16)


def add(*arrays):
    total = sum(a.shape[1] for a in arrays[::2])
    shape = arrays[0].shape
    return call(
        add_kernel, "add", struct((shape[0], total, shape[2])), [VMEM] * len(arrays), VMEM
    )(*arrays)


def core_hop(x):
    return hop(x, "dp", 1)


def across(total):
    distance = 2
    parts = [total, hop(total, "dp", distance)]
    while 2 * distance < lax.axis_size("dp"):
        distance *= 2
        total = add(*parts)
        parts = [total, hop(total, "dp", distance)]
    return parts


def middle(gate_pre, up_pre, hidden_grad):
    sig = jax.nn.sigmoid(gate_pre)
    silu = gate_pre * sig
    hidden = silu * up_pre
    up_grad = hidden_grad * silu
    pre_grad = hidden_grad * up_pre * sig * (1.0 + gate_pre * (1.0 - sig))
    return hidden, up_grad, pre_grad


def by_blocks(total, body):
    block = BLOCK if total % BLOCK == 0 else 16

    def step(i, carry):
        body(pl.ds(pl.multiple_of(i * block, block), block))
        return carry

    lax.fori_loop(0, total // block, step, 0)


def sides(mine, other):
    lower = lax.axis_index("dp") % 2 == 0

    def read(side, i, rows):
        a, b = mine[i, rows].astype(F32), other[i, rows].astype(F32)
        return jnp.where(lower, a, b) if side == 0 else jnp.where(lower, b, a)

    return read


def outputs_kernel(pairs, mine, other, w_gate, w_up, w_down, hidden_ref, up_ref, pre_ref, *refs):
    chunks, ends = refs[:pairs], refs[pairs]
    total, half = mine.shape[1:]
    width = w_gate.shape[0]
    read = sides(mine, other)

    def block(rows):
        inner = 0.0
        for side in range(2):
            values = [read(side, i, rows) for i in range(3)]
            hidden, up_grad, pre_grad = middle(*values)
            inner += jnp.sum(hidden * values[2], axis=1, keepdims=True)
            at = slice(side * half, (side + 1) * half)
            hidden_ref[rows, at] = hidden.astype(BF16)
            up_ref[rows, at] = up_grad.astype(BF16)
            pre_ref[rows, at] = pre_grad.astype(BF16)
        high = inner.astype(BF16).astype(F32)
        lane = lax.broadcasted_iota(jnp.int32, (inner.shape[0], EXTRA), 1)
        ends[rows] = jnp.where(lane == 0, high, jnp.where(lane == 1, inner - high, 0.0))

    by_blocks(total, block)
    put_chunks(ends[...], [ref.at[:, 2 * width :] for ref in chunks])
    out = dot32(hidden_ref[...], w_down[...])
    put_chunks(out, [ref.at[:, :width] for ref in chunks])
    out = dot32(pre_ref[...], w_gate[...], SECOND) + dot32(up_ref[...], w_up[...], SECOND)
    put_chunks(out, [ref.at[:, width : 2 * width] for ref in chunks])


def outputs(mine, other, weights, pairs):
    width, hidden = weights[0].shape
    total = pairs * CAP
    out = call(
        functools.partial(outputs_kernel, pairs),
        "outputs",
        [struct((total, hidden))] * 3 + [struct((CAP, 2 * width + EXTRA))] * pairs,
        [VMEM] * 5,
        [VMEM] * (3 + pairs),
        [pltpu.VMEM((total, EXTRA), F32)],
    )(mine, other, *weights)
    return out[:3], list(out[3:])


def combine_kernel(pairs, pairs_ref, routes_ref, gates_ref, *refs):
    chunks = refs[:pairs]
    out_ref, grad_ref, value_ref, back = refs[pairs:]
    tok, width = out_ref.shape
    top = routes_ref.shape[0]
    gates = gates_ref[...]
    pick, gate, hits = pick_rows(routes_ref[...].astype(F32), gates, pairs_ref)
    back[...] = join(chunks)
    scaled = pick * gate
    high = scaled.astype(BF16).astype(F32)
    both = jnp.concatenate([high, scaled - high], axis=1).astype(BF16)
    out = dot32(both, back[:, :width], FIRST)
    out_ref[...] = (out[:tok] + out[tok:]).astype(BF16)
    grad_ref[...] = dot32(pick.astype(BF16), back[:, width : 2 * width], FIRST).astype(BF16)
    ends = back[:, 2 * width :].astype(F32)
    inner = ends[:, 0:1] + ends[:, 1:2]
    values = [jnp.sum(jnp.where(hit, pick * inner, 0.0), axis=0, keepdims=True) for hit in hits]
    value_ref[...] = jnp.concatenate(values, axis=0) / gates


def combine(expert_pairs, routes, gates, chunks, width):
    top, tok = routes.shape
    pairs = len(chunks)
    return call(
        functools.partial(combine_kernel, pairs),
        "combine",
        [struct((tok, width)), struct((tok, width)), struct((top, tok), F32)],
        [SMEM] + [VMEM] * (2 + pairs),
        [VMEM] * 3,
        [pltpu.VMEM((pairs * CAP, chunks[0].shape[1]), BF16)],
    )(expert_pairs, routes, gates, *chunks)


def turn_kernel(*refs):
    *parts, out = refs
    out[...] = join(parts).T


def turn(parts):
    shape = (parts[0].shape[1], sum(p.shape[0] for p in parts))
    return call(turn_kernel, "turn", struct(shape), [VMEM] * len(parts), VMEM)(*parts)


def column_step(*widths):
    step = 256
    while any(w % step for w in widths):
        step //= 2
    return step


def grad_shapes(width, units):
    return [struct(shape) for shape in ((width, units), (width, units), (units, width))]


def own_grads_kernel(step, turned, pre_grad, up_grad, hidden, *refs):
    *cots, gate_out, up_out, down_out, cot = refs
    cot[...] = join(cots)
    for left, right, out in (
        (turned[...], pre_grad, gate_out),
        (turned[...], up_grad, up_out),
        (hidden[...].T, cot, down_out),
    ):
        for j in range(out.shape[1] // step):
            at = slice(j * step, (j + 1) * step)
            out[:, at] = dot32(left, right[:, at]).astype(BF16)


def own_grads(turned, pre_grad, up_grad, hidden, cots):
    width, total = turned.shape
    units = hidden.shape[1]
    return call(
        functools.partial(own_grads_kernel, column_step(units, width)),
        "own_grads",
        grad_shapes(width, units),
        [VMEM] * (4 + len(cots)),
        [VMEM] * 3,
        [pltpu.VMEM((total, width), BF16)],
    )(turned, pre_grad, up_grad, hidden, *cots)


def grads_kernel(step, mine, other, turned, cot, *refs):
    partial, outs, held, buffers, sems = refs[:3], refs[3:6], refs[6], refs[7:10], refs[10]
    total, half = mine.shape[1:]
    read = sides(mine, other)

    def block(rows):
        for side in range(2):
            far_hidden, up, pre = middle(*(read(side, i, rows) for i in range(3)))
            at = slice(side * half, (side + 1) * half)
            for i, part in enumerate((pre, up, far_hidden)):
                held[i, rows, at] = part.astype(BF16)

    by_blocks(total, block)
    copies = []
    for i, right in enumerate((held.at[0], held.at[1], cot)):
        left = held[2].T if i == 2 else turned[...]
        for j in range(outs[i].shape[1] // step):
            at = slice(j * step, (j + 1) * step)
            part = dot32(left, right[:, at]) + partial[i][:, at].astype(F32)
            buffers[i][:, at] = part.astype(BF16)
            copy = pltpu.make_async_copy(buffers[i].at[:, at], outs[i].at[:, at], sems.at[len(copies)])
            copy.start()
            copies.append(copy)
    for copy in copies:
        copy.wait()


def grads(mine, other, turned, cot, partial):
    width, total = turned.shape
    units = partial[0].shape[1]
    step = column_step(units, width)
    shapes = grad_shapes(width, units)
    return call(
        functools.partial(grads_kernel, step),
        "grads",
        shapes,
        [VMEM] * 7,
        [ANY] * 3,
        [pltpu.VMEM((3, total, units), BF16)]
        + [pltpu.VMEM(shape.shape, BF16) for shape in shapes]
        + [pltpu.SemaphoreType.DMA((2 * units // step + width // step,))],
        mib=24,
    )(mine, other, turned, cot, *partial)


def shards(
    tokens, out_grad, gate_values, route_lists, expert_pairs, gate_weight, up_weight, down_weight
):
    top = route_lists.shape[1]
    width = tokens.shape[1]
    pairs = lax.axis_size("expert") // 2
    routes, gates = route_lists.T, gate_values.T

    far, chunks = pack_own(expert_pairs, routes, gates, tokens, out_grad)
    weights = load([after(gate_weight[0], far), up_weight[0], down_weight[0]])
    far = hop(far, "expert", pairs)
    far_grad = hop(after(out_grad, far), "expert", pairs)
    chunks = dispatch(chunks)

    rows_a, cot_a, send, keep = terms(chunks[:1], weights)
    sums_a = across(add(keep, core_hop(send)))

    far_chunks = pack_far(expert_pairs, far, after(far_grad, sums_a[1]), top)
    chunks[1] = after(chunks[1], far_chunks[0])
    rows_b, cot_b, send, keep = terms(chunks[1:], weights)
    far_chunks = dispatch(far_chunks)
    sums_b = across(add(keep, core_hop(send)))

    far_chunks[1] = after(far_chunks[1], sums_b[1])
    mine = add(*sums_a, *sums_b)
    other = core_hop(mine)
    far_chunks[2] = after(far_chunks[2], mine)
    far_rows, far_cot, send, keep = terms(far_chunks, weights)
    got = core_hop(send)
    (hidden, up_grad, pre_grad), sent = outputs(after(mine, send), other, weights, pairs)
    far_sums = across(add(keep, after(got, sent[0])))
    arrived = dispatch(sent, False)
    turned = turn([after(rows_a, far_sums[0]), rows_b])
    far_turned = turn([after(far_rows, turned)])
    partial = own_grads(turned, pre_grad, up_grad, hidden, [cot_a, cot_b])

    far_sums[1] = after(far_sums[1], far_turned, *partial, *arrived)
    mine = add(*far_sums)
    other = core_hop(mine)
    layer_output, token_grad, values = combine(
        expert_pairs, routes, gates, [after(arrived[0], mine)] + arrived[1:], width
    )
    grad_gate, grad_up, grad_down = grads(
        mine, after(other, token_grad), far_turned, far_cot, partial
    )
    return layer_output, token_grad, values.T, grad_gate[None], grad_up[None], grad_down[None]


def solution(mesh):
    row = P("expert", "dp")
    small = P("expert", None)
    tall = P("expert", "dp", None)
    wide = P("expert", None, "dp")
    return jax.shard_map(
        shards,
        mesh=mesh,
        in_specs=(row, row, small, small, P(), tall, tall, wide),
        out_specs=(row, row, small, tall, tall, wide),
        check_vma=False,
    )
```

time: 153 us -> 106 us (0.69); the launches traced: 150 us -> 105 us
  matrix products: 30.1 us -> 0 us
  Pallas kernels: 0 us -> 29.8 us
  waiting for transfers between devices: 68.7 us -> 44.9 us
  other arithmetic: 10.9 us -> 0 us
  local copies, waits for them, and re-layouts: 11 us -> 5.67 us
  starting transfers between devices: 27.9 us -> 23.9 us
    dot_general x23 -> x0, matrix products: 30.1 us -> none  [dot32(): return lax.dot_general(a, b, dims, preferred_element_type=jnp.float32)]
    pallas_call x0 -> x17, Pallas kernels: none -> 29.8 us  [the longest x3 6.45 us: terms(): call(functools.partial(terms_kernel, len(chunks)), 'terms', [struct((tota...]
    ppermute x24 -> x19, waiting for transfers between devices: 68.7 us -> 44.9 us  [hop(): lax.ppermute(x, axis, [(i, i ^ distance) for i in range(lax.axis_size(axi...]
    convert_element_type x9 -> x0, other arithmetic: 4.29 us -> none  [the longest x2 1.64 us: forward(): low = jnp.where(core == 0, total, other).astype(jnp.float32)]
    reduce_sum x5 -> x0, other arithmetic: 4.02 us -> none  [the longest x1 2.12 us: shards(): jnp.sum(hidden.astype(jnp.float32) * hidden_grad, axis=1, keepdims=True)]
    ppermute x24 -> x19, starting transfers between devices: 27.9 us -> 23.9 us  [hop(): lax.ppermute(x, axis, [(i, i ^ distance) for i in range(lax.axis_size(axi...]
    unnamed x53 -> x18, local copies, waits for them, and re-layouts: 8.1 us -> 5.67 us
  transfers between devices with their start and end apart: 24 -> 19, of which waited for: 12 -> 12; matrix products, arithmetic and copies ran while one was open for 29% -> 0% of each run, Pallas kernels for 0% -> 17%
where the time goes in v2:
time: 106 us; the launch traced here: 105 us
  waiting for transfers between devices  44.9 us (42%)
  Pallas kernels  29.8 us (28%)
  starting transfers between devices  23.9 us (23%)
  local copies, waits for them, and re-layouts  5.67 us (5%)
    ppermute x19, waiting for transfers between devices, hop(): lax.ppermute(x, axis, [(i, i ^ distance) for i in range(lax.axis_size(axi...  44.9 us
    ppermute x19, starting transfers between devices, hop(): lax.ppermute(x, axis, [(i, i ^ distance) for i in range(lax.axis_size(axi...  23.9 us
    pallas_call x3, Pallas kernels, terms(): call(functools.partial(terms_kernel, len(chunks)), 'terms', [struct((tota...  6.45 us
    pallas_call x1, Pallas kernels, grads(): call(functools.partial(grads_kernel, step), 'grads', shapes, [VMEM] * 7,...  6.44 us
    unnamed x18, local copies, waits for them, and re-layouts  5.67 us
    pallas_call x1, Pallas kernels, outputs(): call(functools.partial(outputs_kernel, pairs), 'outputs', [struct((total,...  4.29 us
    pallas_call x1, Pallas kernels, own_grads(): call(functools.partial(own_grads_kernel, column_step(units, width)), 'own...  4.24 us
    pallas_call x1, Pallas kernels, pack_own(): call(functools.partial(pack_own_kernel, pairs), 'pack_own', [struct((tok,...  2.94 us
  transfers between devices with their start and end apart: 19, of which 12 were waited for; matrix products, arithmetic and copies ran while one was open for 0% of the time, Pallas kernels for 17%

profile of v2, /device:TPU:0, one launch (start us, length us, event | category | flops | bytes accessed | tf_op | source)
XLA Modules:
  0.0 105.3 jit_solution(875965068274156300)
XLA Ops:
  0.6 2.9 %pack_own.1 = (bf16[128,1408]{1,0:T(8,128)(2,1)}, bf16[72,2560]{1,0:T(8,128)(2,1)}, bf16[72,2560]{1,0:T(8,128)(2,1)}, bf16[72,2560]{1,0:T(8,128)(2,1)}, bf16[72,2560]{1,0:T(8,128)(2,1)}) custom-call(s32[4]{0:T(128)} %pairs_ref.5, s32[2,128]{1,0:T(2,128)} %bitcast.12, f32[2,128]{1,0:T(2,128)} %bitcast.14, bf16[128,1280]{1,0:T(8,128)(2,1)} %tok_ref.1, ...), custom_call_target="tpu_custom_call" | custom-call | flops 1024 | bytes 524288 | tf_op jit(solution)/shard_map/pack_own/pallas_call | solution.py:113
  3.6 3.0 %collective-permute-start.2 = (bf16[72,2560]{1,0:T(8,128)(2,1)}, bf16[72,2560]{1,0:T(8,128)(2,1)S(1)}, u32[]{:S(2)}, u32[]{:S(2)}) collective-permute-start(bf16[72,2560]{1,0:T(8,128)(2,1)} %get-tuple-element.69), channel_id=1, source_target_pairs={{0,1},{1,0},{2,3},{3,2},{4,5},{5,4},{6,7},{7,6},{8,9},{9,8},{10,11... | collective-permute-start | bytes 1105928 | tf_op jit(solution)/shard_map/ppermute | solution.py:26
  6.5 1.6 %collective-permute-start.5 = (bf16[72,2560]{1,0:T(8,128)(2,1)}, bf16[72,2560]{1,0:T(8,128)(2,1)S(1)}, u32[]{:S(2)}, u32[]{:S(2)}) collective-permute-start(bf16[72,2560]{1,0:T(8,128)(2,1)} %get-tuple-element.74), channel_id=1, source_target_pairs={{0,2},{1,3},{2,0},{3,1},{4,6},{5,7},{6,4},{7,5},{8,10},{9,11},{10,... | collective-permute-start | bytes 1105928 | tf_op jit(solution)/shard_map/ppermute | solution.py:26
  8.1 2.6 %collective-permute-start.3 = (bf16[128,1408]{1,0:T(8,128)(2,1)}, bf16[128,1408]{1,0:T(8,128)(2,1)S(1)}, u32[]{:S(2)}, u32[]{:S(2)}) collective-permute-start(bf16[128,1408]{1,0:T(8,128)(2,1)} %get-tuple-element.62), channel_id=1, source_target_pairs={{0,4},{1,5},{2,6},{3,7},{4,0},{5,1},{6,2},{7,3},{8,12},{9,13},{10,... | collective-permute-start | bytes 1081352 | tf_op jit(solution)/shard_map/ppermute | solution.py:26
  10.7 1.7 %copy-done = bf16[1,1280,1024]{2,1,0:T(8,128)(2,1)S(1)} copy-done((bf16[1,1280,1024]{2,1,0:T(8,128)(2,1)S(1)}, bf16[1,1280,1024]{2,1,0:T(8,128)(2,1)}, u32[]{:S(2)}) %copy-start) | copy-done | bytes 2621464
  12.5 1.7 %copy-done.1 = bf16[1,1280,1024]{2,1,0:T(8,128)(2,1)S(1)} copy-done((bf16[1,1280,1024]{2,1,0:T(8,128)(2,1)S(1)}, bf16[1,1280,1024]{2,1,0:T(8,128)(2,1)}, u32[]{:S(2)}) %copy-start.1) | copy-done | bytes 2621464
  14.2 1.7 %copy-done.2 = bf16[1,1024,1280]{2,1,0:T(8,128)(2,1)S(1)} copy-done((bf16[1,1024,1280]{2,1,0:T(8,128)(2,1)S(1)}, bf16[1,1024,1280]{2,1,0:T(8,128)(2,1)}, u32[]{:S(2)}) %copy-start.2) | copy-done | bytes 2621464
  15.9 0.6 load.1
  16.5 0.4 copy-done.3
  16.9 1.8 %terms.3 = (bf16[72,1280]{1,0:T(8,128)(2,1)S(1)}, bf16[72,1280]{1,0:T(8,128)(2,1)S(1)}, bf16[3,72,512]{2,1,0:T(8,128)(2,1)S(1)}, bf16[3,72,512]{2,1,0:T(8,128)(2,1)S(1)}) custom-call(bf16[72,2560]{1,0:T(8,128)(2,1)S(1)} %copy-done.3, bf16[1280,1024]{1,0:T(8,128)(2,1)S(1)} %get-tuple-element.64.refs_1_.refs_3_.refs_4_.w_gate, ...), custom_call_target="tpu_custom_call" | custom-call | flops 1024 | bytes 524288 | tf_op jit(solution)/shard_map/terms/pallas_call | solution.py:194
  18.8 0.1 collective-permute-start
  18.9 0.0 collective-permute-done.2.refs_0_
  18.9 5.7 %collective-permute-done.5.refs_1_ = bf16[72,2560]{1,0:T(8,128)(2,1)S(1)} collective-permute-done((bf16[72,2560]{1,0:T(8,128)(2,1)}, bf16[72,2560]{1,0:T(8,128)(2,1)S(1)}, u32[]{:S(2)}, u32[]{:S(2)}) %collective-permute-start.5) | collective-permute-done | bytes 368672 | tf_op jit(solution)/shard_map/ppermute | solution.py:26
  24.5 0.0 copy-done.8
  24.5 0.0 collective-permute-start.6
  24.5 0.0 collective-permute-done.3.far_ref
  24.5 0.0 copy-done.7
  24.6 3.0 %collective-permute-start.4 = (bf16[128,1280]{1,0:T(8,128)(2,1)S(1)}, bf16[128,1280]{1,0:T(8,128)(2,1)S(1)}, u32[]{:S(2)}, u32[]{:S(2)}) collective-permute-start(bf16[128,1280]{1,0:T(8,128)(2,1)S(1)} %copy-done.7), channel_id=1, source_target_pairs={{0,4},{1,5},{2,6},{3,7},{4,0},{5,1},{6,2},{7,3},{8,12},{9,13},{10,... | collective-permute-start | bytes 983048 | tf_op jit(solution)/shard_map/ppermute | solution.py:26
  27.6 0.0 collective-permute-done.refs_1_
  27.6 0.1 add.5.refs_0_
  27.6 1.6 %collective-permute-start.1 = (bf16[3,72,512]{2,1,0:T(8,128)(2,1)S(1)}, bf16[3,72,512]{2,1,0:T(8,128)(2,1)S(1)}, u32[]{:S(2)}, u32[]{:S(2)}) collective-permute-start(bf16[3,72,512]{2,1,0:T(8,128)(2,1)S(1)} %add.5.refs_0_), channel_id=1, source_target_pairs={{0,16},{8,24},{16,0},{24,8},{1,17},{9,25},{17,1},{25,9},{2,18},{10... | collective-permute-start | bytes 663560 | tf_op jit(solution)/shard_map/ppermute | solution.py:26
  29.2 4.4 %collective-permute-done.1.refs_1_ = bf16[3,72,512]{2,1,0:T(8,128)(2,1)S(1)} collective-permute-done((bf16[3,72,512]{2,1,0:T(8,128)(2,1)S(1)}, bf16[3,72,512]{2,1,0:T(8,128)(2,1)S(1)}, u32[]{:S(2)}, u32[]{:S(2)}) %collective-permute-start.1) | collective-permute-done | bytes 221216 | tf_op jit(solution)/shard_map/ppermute | solution.py:26
  33.6 5.0 %collective-permute-done.4.grad_ref = bf16[128,1280]{1,0:T(8,128)(2,1)S(1)} collective-permute-done((bf16[128,1280]{1,0:T(8,128)(2,1)S(1)}, bf16[128,1280]{1,0:T(8,128)(2,1)S(1)}, u32[]{:S(2)}, u32[]{:S(2)}) %collective-permute-start.4) | collective-permute-done | bytes 327712 | tf_op jit(solution)/shard_map/ppermute | solution.py:26
  38.6 0.0 copy-done.4
  38.6 1.3 %pack_far.1 = (bf16[72,2560]{1,0:T(8,128)(2,1)S(1)}, bf16[72,2560]{1,0:T(8,128)(2,1)S(1)}, bf16[72,2560]{1,0:T(8,128)(2,1)S(1)}, bf16[72,2560]{1,0:T(8,128)(2,1)S(1)}) custom-call(s32[4]{0:T(128)S(1)} %copy-done.4, bf16[128,1408]{1,0:T(8,128)(2,1)S(1)} %collective-permute-done.3.far_ref, bf16[128,1280]{1,0:T(8,128)(2,1)S(1)} %collective-permute-done.4.grad_ref), custom_call_target="tpu_custom_call" | custom-call | flops 1024 | bytes 524288 | tf_op jit(solution)/shard_map/pack_far/pallas_call | solution.py:140
  39.9 1.7 %collective-permute-done.6.refs_2_ = bf16[72,2560]{1,0:T(8,128)(2,1)S(1)} collective-permute-done((bf16[72,2560]{1,0:T(8,128)(2,1)S(1)}, bf16[72,2560]{1,0:T(8,128)(2,1)S(1)}, u32[]{:S(2)}, u32[]{:S(2)}) %collective-permute-start.6) | collective-permute-done | bytes 368672 | tf_op jit(solution)/shard_map/ppermute | solution.py:26
  41.6 2.1 %terms.4 = (bf16[216,1280]{1,0:T(8,128)(2,1)S(1)}, bf16[216,1280]{1,0:T(8,128)(2,1)S(1)}, bf16[3,216,512]{2,1,0:T(8,128)(2,1)S(1)}, bf16[3,216,512]{2,1,0:T(8,128)(2,1)S(1)}) custom-call(bf16[72,2560]{1,0:T(8,128)(2,1)S(1)} %collective-permute-done.2.refs_0_, bf16[72,2560]{1,0:T(8,128)(2,1)S(1)} %collective-permute-done.5.refs_1_, ...), custom_call_target="tpu_custom_call" | custom-call | flops 1024 | bytes 524288 | tf_op jit(solution)/shard_map/terms/pallas_call | solution.py:194
  43.7 0.1 collective-permute-start.7
  43.8 0.7 collective-permute-start.9
  44.5 2.3 %collective-permute-start.10 = (bf16[72,2560]{1,0:T(8,128)(2,1)S(1)}, bf16[72,2560]{1,0:T(8,128)(2,1)S(1)}, u32[]{:S(2)}, u32[]{:S(2)}) collective-permute-start(bf16[72,2560]{1,0:T(8,128)(2,1)S(1)} %get-tuple-element.81), channel_id=1, source_target_pairs={{0,2},{1,3},{2,0},{3,1},{4,6},{5,7},{6,4},{7,5},{8,10},{9,11},{10,... | collective-permute-start | bytes 1105928 | tf_op jit(solution)/shard_map/ppermute | solution.py:26
  46.8 0.0 collective-permute-done.7.refs_1_
  46.8 0.2 add.6.refs_2_
  47.0 1.5 %collective-permute-start.8 = (bf16[3,216,512]{2,1,0:T(8,128)(2,1)S(1)}, bf16[3,216,512]{2,1,0:T(8,128)(2,1)S(1)}, u32[]{:S(2)}, u32[]{:S(2)}) collective-permute-start(bf16[3,216,512]{2,1,0:T(8,128)(2,1)S(1)} %add.6.refs_2_), channel_id=1, source_target_pairs={{0,16},{8,24},{16,0},{24,8},{1,17},{9,25},{17,1},{25,9},{2,18},{10... | collective-permute-start | bytes 1990664 | tf_op jit(solution)/shard_map/ppermute | solution.py:26
  48.5 6.3 %collective-permute-done.9.refs_1_ = bf16[72,2560]{1,0:T(8,128)(2,1)S(1)} collective-permute-done((bf16[72,2560]{1,0:T(8,128)(2,1)S(1)}, bf16[72,2560]{1,0:T(8,128)(2,1)S(1)}, u32[]{:S(2)}, u32[]{:S(2)}) %collective-permute-start.9) | collective-permute-done | bytes 368672 | tf_op jit(solution)/shard_map/ppermute | solution.py:26
  54.8 0.9 collective-permute-done.10.refs_2_
  55.7 2.3 %collective-permute-start.11 = (bf16[72,2560]{1,0:T(8,128)(2,1)S(1)}, bf16[72,2560]{1,0:T(8,128)(2,1)S(1)}, u32[]{:S(2)}, u32[]{:S(2)}) collective-permute-start(bf16[72,2560]{1,0:T(8,128)(2,1)S(1)} %get-tuple-element.84), channel_id=1, source_target_pairs={{0,3},{1,2},{2,1},{3,0},{4,7},{5,6},{6,5},{7,4},{8,11},{9,10},{10,... | collective-permute-start | bytes 1105928 | tf_op jit(solution)/shard_map/ppermute | solution.py:26
  58.0 5.7 %collective-permute-done.8.refs_3_ = bf16[3,216,512]{2,1,0:T(8,128)(2,1)S(1)} collective-permute-done((bf16[3,216,512]{2,1,0:T(8,128)(2,1)S(1)}, bf16[3,216,512]{2,1,0:T(8,128)(2,1)S(1)}, u32[]{:S(2)}, u32[]{:S(2)}) %collective-permute-start.8) | collective-permute-done | bytes 663584 | tf_op jit(solution)/shard_map/ppermute | solution.py:26
  63.8 0.2 add.7.mine
  64.0 0.1 collective-permute-start.12
  64.0 2.8 %collective-permute-done.11.refs_3_ = bf16[72,2560]{1,0:T(8,128)(2,1)S(1)} collective-permute-done((bf16[72,2560]{1,0:T(8,128)(2,1)S(1)}, bf16[72,2560]{1,0:T(8,128)(2,1)S(1)}, u32[]{:S(2)}, u32[]{:S(2)}) %collective-permute-start.11) | collective-permute-done | bytes 368672 | tf_op jit(solution)/shard_map/ppermute | solution.py:26
  66.8 2.5 %terms.5 = (bf16[288,1280]{1,0:T(8,128)(2,1)S(1)}, bf16[288,1280]{1,0:T(8,128)(2,1)S(1)}, bf16[3,288,512]{2,1,0:T(8,128)(2,1)S(1)}, bf16[3,288,512]{2,1,0:T(8,128)(2,1)S(1)}) custom-call(bf16[72,2560]{1,0:T(8,128)(2,1)S(1)} %get-tuple-element.72.refs_0_, bf16[72,2560]{1,0:T(8,128)(2,1)S(1)} %collective-permute-done.9.refs_1_, ...), custom_call_target="tpu_custom_call" | custom-call | flops 1024 | bytes 524288 | tf_op jit(solution)/shard_map/terms/pallas_call | solution.py:194
  69.3 0.1 collective-permute-start.13
  69.3 0.0 collective-permute-done.12.other
  69.4 4.3 %outputs.1 = (bf16[288,1024]{1,0:T(8,128)(2,1)S(1)}, bf16[288,1024]{1,0:T(8,128)(2,1)S(1)}, bf16[288,1024]{1,0:T(8,128)(2,1)S(1)}, bf16[72,2688]{1,0:T(8,128)(2,...) custom-call(bf16[3,288,512]{2,1,0:T(8,128)(2,1)S(1)} %add.7.mine, ...), custom_call_target="tpu_custom_call" | custom-call | flops 1024 | bytes 524288 | tf_op jit(solution)/shard_map/outputs/pallas_call | solution.py:292
  73.7 0.0 collective-permute-done.13.refs_1_
  73.7 0.2 add.8.refs_0_
  73.9 1.5 %collective-permute-start.14 = (bf16[3,288,512]{2,1,0:T(8,128)(2,1)S(1)}, bf16[3,288,512]{2,1,0:T(8,128)(2,1)S(1)}, u32[]{:S(2)}, u32[]{:S(2)}) collective-permute-start(bf16[3,288,512]{2,1,0:T(8,128)(2,1)S(1)} %add.8.refs_0_), channel_id=1, source_target_pairs={{0,16},{8,24},{16,0},{24,8},{1,17},{9,25},{17,1},{25,9},{2,18},{10... | collective-permute-start | bytes 2654216 | tf_op jit(solution)/shard_map/ppermute | solution.py:26
  75.4 1.1 %collective-permute-start.15 = (bf16[72,2688]{1,0:T(8,128)(2,1)S(1)}, bf16[72,2688]{1,0:T(8,128)(2,1)S(1)}, u32[]{:S(2)}, u32[]{:S(2)}) collective-permute-start(bf16[72,2688]{1,0:T(8,128)(2,1)S(1)} %get-tuple-element.103), channel_id=1, source_target_pairs={{0,1},{1,0},{2,3},{3,2},{4,5},{5,4},{6,7},{7,6},{8,9},{9,8},{10,11... | collective-permute-start | bytes 1161224 | tf_op jit(solution)/shard_map/ppermute | solution.py:26
  76.5 1.5 %collective-permute-start.16 = (bf16[72,2688]{1,0:T(8,128)(2,1)S(1)}, bf16[72,2688]{1,0:T(8,128)(2,1)S(1)}, u32[]{:S(2)}, u32[]{:S(2)}) collective-permute-start(bf16[72,2688]{1,0:T(8,128)(2,1)S(1)} %get-tuple-element.104), channel_id=1, source_target_pairs={{0,2},{1,3},{2,0},{3,1},{4,6},{5,7},{6,4},{7,5},{8,10},{9,11},{10,... | collective-permute-start | bytes 1161224 | tf_op jit(solution)/shard_map/ppermute | solution.py:26
  78.0 1.0 collective-permute-start.17
  78.9 0.3 turn.2.turned
  79.2 0.3 turn.3.turned
  79.5 0.0 copy-start.5
  79.6 0.0 copy-start.6
  79.6 4.2 %own_grads.1 = (bf16[1280,1024]{1,0:T(8,128)(2,1)S(1)}, bf16[1280,1024]{1,0:T(8,128)(2,1)S(1)}, bf16[1024,1280]{1,0:T(8,128)(2,1)S(1)}) custom-call(bf16[1280,288]{1,0:T(8,128)(2,1)S(1)} %turn.2.turned, bf16[288,1024]{1,0:T(8,128)(2,1)S(1)} %get-tuple-element.95.pre_grad, bf16[288,1024]{1,0:T(8,128)(2,1)S(1)} %get-tuple-element.96.up_grad, ...), custom_call_target="tpu_custom_call" | custom-call | flops 1024 | bytes 524288 | tf_op jit(solution)/shard_map/own_grads/pallas_call | solution.py:373
  83.8 2.7 %collective-permute-done.15.refs_1_ = bf16[72,2688]{1,0:T(8,128)(2,1)S(1)} collective-permute-done((bf16[72,2688]{1,0:T(8,128)(2,1)S(1)}, bf16[72,2688]{1,0:T(8,128)(2,1)S(1)}, u32[]{:S(2)}, u32[]{:S(2)}) %collective-permute-start.15) | collective-permute-done | bytes 387104 | tf_op jit(solution)/shard_map/ppermute | solution.py:26
  86.5 1.9 %collective-permute-done.16.refs_2_ = bf16[72,2688]{1,0:T(8,128)(2,1)S(1)} collective-permute-done((bf16[72,2688]{1,0:T(8,128)(2,1)S(1)}, bf16[72,2688]{1,0:T(8,128)(2,1)S(1)}, u32[]{:S(2)}, u32[]{:S(2)}) %collective-permute-start.16) | collective-permute-done | bytes 387104 | tf_op jit(solution)/shard_map/ppermute | solution.py:26
  88.4 7.6 %collective-permute-done.17.refs_3_ = bf16[72,2688]{1,0:T(8,128)(2,1)S(1)} collective-permute-done((bf16[72,2688]{1,0:T(8,128)(2,1)S(1)}, bf16[72,2688]{1,0:T(8,128)(2,1)S(1)}, u32[]{:S(2)}, u32[]{:S(2)}) %collective-permute-start.17) | collective-permute-done | bytes 387104 | tf_op jit(solution)/shard_map/ppermute | solution.py:26
  96.0 0.0 collective-permute-done.14.refs_1_
  96.0 0.2 add.9.mine
  96.2 0.1 collective-permute-start.18
  96.3 2.2 %combine.1 = (bf16[128,1280]{1,0:T(8,128)(2,1)}, bf16[128,1280]{1,0:T(8,128)(2,1)}, f32[2,128]{1,0:T(2,128)}) custom-call(s32[4]{0:T(128)S(1)} %copy-done.4, s32[2,128]{1,0:T(2,128)S(1)} %bitcast.13, f32[2,128]{1,0:T(2,128)S(1)} %bitcast.15, bf16[72,2688]{1,0:T(8,128)(2,1)S(1)} %get-tuple-element.107.refs_0_, ...), custom_call_target="tpu_custom_call" | custom-call | flops 1024 | bytes 524288 | tf_op jit(solution)/shard_map/combine/pallas_call | solution.py:326
  98.5 0.2 collective-permute-done.18.other
  98.7 6.4 %grads.1 = (bf16[1280,1024]{1,0:T(8,128)(2,1)}, bf16[1280,1024]{1,0:T(8,128)(2,1)}, bf16[1024,1280]{1,0:T(8,128)(2,1)}) custom-call(bf16[3,288,512]{2,1,0:T(8,128)(2,1)S(1)} %add.9.mine, bf16[3,288,512]{2,1,0:T(8,128)(2,1)S(1)} %collective-permute-done.18.other, bf16[1280,288]{1,0:T(8,128)(2,1)S(1)} %turn.3.turned, ...), custom_call_target="tpu_custom_call" | custom-call | flops 1024 | bytes 524288 | tf_op jit(solution)/shard_map/grads/pallas_call | solution.py:415
  (9 shorter events, 0.0 us)
Async XLA Ops:
  3.6 15.3 %collective-permute-start.2 = (bf16[72,2560]{1,0:T(8,128)(2,1)}, bf16[72,2560]{1,0:T(8,128)(2,1)S(1)}, u32[]{:S(2)}, u32[]{:S(2)}) collective-permute-start(bf16[72,2560]{1,0:T(8,128)(2,1)} %get-tuple-element.69), channel_id=1, source_target_pairs={{0,1},{1,0},{2,3},{3,2},{4,5},{5,4},{6,7},{7,6},{8,9},{9,8},{10,11... | collective-permute-start | bytes 1105928 | tf_op jit(solution)/shard_map/ppermute | solution.py:26
  6.5 18.0 %collective-permute-start.5 = (bf16[72,2560]{1,0:T(8,128)(2,1)}, bf16[72,2560]{1,0:T(8,128)(2,1)S(1)}, u32[]{:S(2)}, u32[]{:S(2)}) collective-permute-start(bf16[72,2560]{1,0:T(8,128)(2,1)} %get-tuple-element.74), channel_id=1, source_target_pairs={{0,2},{1,3},{2,0},{3,1},{4,6},{5,7},{6,4},{7,5},{8,10},{9,11},{10,... | collective-permute-start | bytes 1105928 | tf_op jit(solution)/shard_map/ppermute | solution.py:26
  8.1 16.4 %collective-permute-start.3 = (bf16[128,1408]{1,0:T(8,128)(2,1)}, bf16[128,1408]{1,0:T(8,128)(2,1)S(1)}, u32[]{:S(2)}, u32[]{:S(2)}) collective-permute-start(bf16[128,1408]{1,0:T(8,128)(2,1)} %get-tuple-element.62), channel_id=1, source_target_pairs={{0,4},{1,5},{2,6},{3,7},{4,0},{5,1},{6,2},{7,3},{8,12},{9,13},{10,... | collective-permute-start | bytes 1081352 | tf_op jit(solution)/shard_map/ppermute | solution.py:26
  10.7 1.7 %copy-start = (bf16[1,1280,1024]{2,1,0:T(8,128)(2,1)S(1)}, bf16[1,1280,1024]{2,1,0:T(8,128)(2,1)}, u32[]{:S(2)}) copy-start(bf16[1,1280,1024]{2,1,0:T(8,128)(2,1)} %param.13) | copy-start | bytes 7864324
  12.5 1.7 %copy-start.1 = (bf16[1,1280,1024]{2,1,0:T(8,128)(2,1)S(1)}, bf16[1,1280,1024]{2,1,0:T(8,128)(2,1)}, u32[]{:S(2)}) copy-start(bf16[1,1280,1024]{2,1,0:T(8,128)(2,1)} %param.14) | copy-start | bytes 7864324
  14.2 1.7 %copy-start.2 = (bf16[1,1024,1280]{2,1,0:T(8,128)(2,1)S(1)}, bf16[1,1024,1280]{2,1,0:T(8,128)(2,1)}, u32[]{:S(2)}) copy-start(bf16[1,1024,1280]{2,1,0:T(8,128)(2,1)} %param.15) | copy-start | bytes 7864324
  15.9 1.0 copy-start.3
  16.9 7.6 %copy-start.8 = (bf16[72,2560]{1,0:T(8,128)(2,1)S(1)}, bf16[72,2560]{1,0:T(8,128)(2,1)}, u32[]{:S(2)}) copy-start(bf16[72,2560]{1,0:T(8,128)(2,1)} %get-tuple-element.76) | copy-start | bytes 1105924
  16.9 7.6 %copy-start.7 = (bf16[128,1280]{1,0:T(8,128)(2,1)S(1)}, bf16[128,1280]{1,0:T(8,128)(2,1)}, u32[]{:S(2)}) copy-start(bf16[128,1280]{1,0:T(8,128)(2,1)} %grad_ref.1) | copy-start | bytes 983044
  16.9 21.7 %copy-start.4 = (s32[4]{0:T(128)S(1)}, s32[4]{0:T(128)}, u32[]{:S(2)}) copy-start(s32[4]{0:T(128)} %pairs_ref.5) | copy-start | bytes 52
  18.8 8.8 %collective-permute-start = (bf16[3,72,512]{2,1,0:T(8,128)(2,1)S(1)}, bf16[3,72,512]{2,1,0:T(8,128)(2,1)S(1)}, u32[]{:S(2)}, u32[]{:S(2)}) collective-permute-start(bf16[3,72,512]{2,1,0:T(8,128)(2,1)S(1)} %get-tuple-element.68), channel_id=1, source_target_pairs={{0,8},{8,0},{16,24},{24,16},{1,9},{9,1},{17,25},{25,17},{2,10},{10... | collective-permute-start | bytes 663560 | tf_op jit(solution)/shard_map/ppermute | solution.py:26
  24.5 17.1 %collective-permute-start.6 = (bf16[72,2560]{1,0:T(8,128)(2,1)S(1)}, bf16[72,2560]{1,0:T(8,128)(2,1)S(1)}, u32[]{:S(2)}, u32[]{:S(2)}) collective-permute-start(bf16[72,2560]{1,0:T(8,128)(2,1)S(1)} %copy-done.8), channel_id=1, source_target_pairs={{0,3},{1,2},{2,1},{3,0},{4,7},{5,6},{6,5},{7,4},{8,11},{9,10},{10,... | collective-permute-start | bytes 1105928 | tf_op jit(solution)/shard_map/ppermute | solution.py:26
  24.6 14.1 %collective-permute-start.4 = (bf16[128,1280]{1,0:T(8,128)(2,1)S(1)}, bf16[128,1280]{1,0:T(8,128)(2,1)S(1)}, u32[]{:S(2)}, u32[]{:S(2)}) collective-permute-start(bf16[128,1280]{1,0:T(8,128)(2,1)S(1)} %copy-done.7), channel_id=1, source_target_pairs={{0,4},{1,5},{2,6},{3,7},{4,0},{5,1},{6,2},{7,3},{8,12},{9,13},{10,... | collective-permute-start | bytes 983048 | tf_op jit(solution)/shard_map/ppermute | solution.py:26
  27.6 6.0 %collective-permute-start.1 = (bf16[3,72,512]{2,1,0:T(8,128)(2,1)S(1)}, bf16[3,72,512]{2,1,0:T(8,128)(2,1)S(1)}, u32[]{:S(2)}, u32[]{:S(2)}) collective-permute-start(bf16[3,72,512]{2,1,0:T(8,128)(2,1)S(1)} %add.5.refs_0_), channel_id=1, source_target_pairs={{0,16},{8,24},{16,0},{24,8},{1,17},{9,25},{17,1},{25,9},{2,18},{10... | collective-permute-start | bytes 663560 | tf_op jit(solution)/shard_map/ppermute | solution.py:26
  43.7 3.1 %collective-permute-start.7 = (bf16[3,216,512]{2,1,0:T(8,128)(2,1)S(1)}, bf16[3,216,512]{2,1,0:T(8,128)(2,1)S(1)}, u32[]{:S(2)}, u32[]{:S(2)}) collective-permute-start(bf16[3,216,512]{2,1,0:T(8,128)(2,1)S(1)} %get-tuple-element.78), channel_id=1, source_target_pairs={{0,8},{8,0},{16,24},{24,16},{1,9},{9,1},{17,25},{25,17},{2,10},{10... | collective-permute-start | bytes 1990664 | tf_op jit(solution)/shard_map/ppermute | solution.py:26
  43.8 11.0 %collective-permute-start.9 = (bf16[72,2560]{1,0:T(8,128)(2,1)S(1)}, bf16[72,2560]{1,0:T(8,128)(2,1)S(1)}, u32[]{:S(2)}, u32[]{:S(2)}) collective-permute-start(bf16[72,2560]{1,0:T(8,128)(2,1)S(1)} %get-tuple-element.79), channel_id=1, source_target_pairs={{0,1},{1,0},{2,3},{3,2},{4,5},{5,4},{6,7},{7,6},{8,9},{9,8},{10,11... | collective-permute-start | bytes 1105928 | tf_op jit(solution)/shard_map/ppermute | solution.py:26
  44.5 11.2 %collective-permute-start.10 = (bf16[72,2560]{1,0:T(8,128)(2,1)S(1)}, bf16[72,2560]{1,0:T(8,128)(2,1)S(1)}, u32[]{:S(2)}, u32[]{:S(2)}) collective-permute-start(bf16[72,2560]{1,0:T(8,128)(2,1)S(1)} %get-tuple-element.81), channel_id=1, source_target_pairs={{0,2},{1,3},{2,0},{3,1},{4,6},{5,7},{6,4},{7,5},{8,10},{9,11},{10,... | collective-permute-start | bytes 1105928 | tf_op jit(solution)/shard_map/ppermute | solution.py:26
  47.0 16.8 %collective-permute-start.8 = (bf16[3,216,512]{2,1,0:T(8,128)(2,1)S(1)}, bf16[3,216,512]{2,1,0:T(8,128)(2,1)S(1)}, u32[]{:S(2)}, u32[]{:S(2)}) collective-permute-start(bf16[3,216,512]{2,1,0:T(8,128)(2,1)S(1)} %add.6.refs_2_), channel_id=1, source_target_pairs={{0,16},{8,24},{16,0},{24,8},{1,17},{9,25},{17,1},{25,9},{2,18},{10... | collective-permute-start | bytes 1990664 | tf_op jit(solution)/shard_map/ppermute | solution.py:26
  55.7 11.1 %collective-permute-start.11 = (bf16[72,2560]{1,0:T(8,128)(2,1)S(1)}, bf16[72,2560]{1,0:T(8,128)(2,1)S(1)}, u32[]{:S(2)}, u32[]{:S(2)}) collective-permute-start(bf16[72,2560]{1,0:T(8,128)(2,1)S(1)} %get-tuple-element.84), channel_id=1, source_target_pairs={{0,3},{1,2},{2,1},{3,0},{4,7},{5,6},{6,5},{7,4},{8,11},{9,10},{10,... | collective-permute-start | bytes 1105928 | tf_op jit(solution)/shard_map/ppermute | solution.py:26
  64.0 5.4 %collective-permute-start.12 = (bf16[3,288,512]{2,1,0:T(8,128)(2,1)S(1)}, bf16[3,288,512]{2,1,0:T(8,128)(2,1)S(1)}, u32[]{:S(2)}, u32[]{:S(2)}) collective-permute-start(bf16[3,288,512]{2,1,0:T(8,128)(2,1)S(1)} %add.7.mine), channel_id=1, source_target_pairs={{0,8},{8,0},{16,24},{24,16},{1,9},{9,1},{17,25},{25,17},{2,10},{10... | collective-permute-start | bytes 2654216 | tf_op jit(solution)/shard_map/ppermute | solution.py:26
  69.3 4.4 %collective-permute-start.13 = (bf16[3,288,512]{2,1,0:T(8,128)(2,1)S(1)}, bf16[3,288,512]{2,1,0:T(8,128)(2,1)S(1)}, u32[]{:S(2)}, u32[]{:S(2)}) collective-permute-start(bf16[3,288,512]{2,1,0:T(8,128)(2,1)S(1)} %get-tuple-element.85), channel_id=1, source_target_pairs={{0,8},{8,0},{16,24},{24,16},{1,9},{9,1},{17,25},{25,17},{2,10},{10... | collective-permute-start | bytes 2654216 | tf_op jit(solution)/shard_map/ppermute | solution.py:26
  73.9 22.1 %collective-permute-start.14 = (bf16[3,288,512]{2,1,0:T(8,128)(2,1)S(1)}, bf16[3,288,512]{2,1,0:T(8,128)(2,1)S(1)}, u32[]{:S(2)}, u32[]{:S(2)}) collective-permute-start(bf16[3,288,512]{2,1,0:T(8,128)(2,1)S(1)} %add.8.refs_0_), channel_id=1, source_target_pairs={{0,16},{8,24},{16,0},{24,8},{1,17},{9,25},{17,1},{25,9},{2,18},{10... | collective-permute-start | bytes 2654216 | tf_op jit(solution)/shard_map/ppermute | solution.py:26
  75.4 11.1 %collective-permute-start.15 = (bf16[72,2688]{1,0:T(8,128)(2,1)S(1)}, bf16[72,2688]{1,0:T(8,128)(2,1)S(1)}, u32[]{:S(2)}, u32[]{:S(2)}) collective-permute-start(bf16[72,2688]{1,0:T(8,128)(2,1)S(1)} %get-tuple-element.103), channel_id=1, source_target_pairs={{0,1},{1,0},{2,3},{3,2},{4,5},{5,4},{6,7},{7,6},{8,9},{9,8},{10,11... | collective-permute-start | bytes 1161224 | tf_op jit(solution)/shard_map/ppermute | solution.py:26
  76.5 11.9 %collective-permute-start.16 = (bf16[72,2688]{1,0:T(8,128)(2,1)S(1)}, bf16[72,2688]{1,0:T(8,128)(2,1)S(1)}, u32[]{:S(2)}, u32[]{:S(2)}) collective-permute-start(bf16[72,2688]{1,0:T(8,128)(2,1)S(1)} %get-tuple-element.104), channel_id=1, source_target_pairs={{0,2},{1,3},{2,0},{3,1},{4,6},{5,7},{6,4},{7,5},{8,10},{9,11},{10,... | collective-permute-start | bytes 1161224 | tf_op jit(solution)/shard_map/ppermute | solution.py:26
  78.0 18.0 %collective-permute-start.17 = (bf16[72,2688]{1,0:T(8,128)(2,1)S(1)}, bf16[72,2688]{1,0:T(8,128)(2,1)S(1)}, u32[]{:S(2)}, u32[]{:S(2)}) collective-permute-start(bf16[72,2688]{1,0:T(8,128)(2,1)S(1)} %get-tuple-element.105), channel_id=1, source_target_pairs={{0,3},{1,2},{2,1},{3,0},{4,7},{5,6},{6,5},{7,4},{8,11},{9,10},{10,... | collective-permute-start | bytes 1161224 | tf_op jit(solution)/shard_map/ppermute | solution.py:26
  79.5 16.7 %copy-start.5 = (s32[128,2]{0,1:T(2,128)S(1)}, s32[128,2]{0,1:T(2,128)}, u32[]{:S(2)}) copy-start(s32[128,2]{0,1:T(2,128)} %param.11) | copy-start | bytes 3076
  79.6 16.7 %copy-start.6 = (f32[128,2]{0,1:T(2,128)S(1)}, f32[128,2]{0,1:T(2,128)}, u32[]{:S(2)}) copy-start(f32[128,2]{0,1:T(2,128)} %param.10) | copy-start | bytes 3076
  96.2 2.5 %collective-permute-start.18 = (bf16[3,288,512]{2,1,0:T(8,128)(2,1)S(1)}, bf16[3,288,512]{2,1,0:T(8,128)(2,1)S(1)}, u32[]{:S(2)}, u32[]{:S(2)}) collective-permute-start(bf16[3,288,512]{2,1,0:T(8,128)(2,1)S(1)} %add.9.mine), channel_id=1, source_target_pairs={{0,8},{8,0},{16,24},{24,16},{1,9},{9,1},{17,25},{25,17},{2,10},{10... | collective-permute-start | bytes 2654216 | tf_op jit(solution)/shard_map/ppermute | solution.py:26

commit v3 on v2

--- a/solution.py
+++ b/solution.py
@@ -10,7 +10,7 @@
 HALF = 36
 CAP = 2 * HALF
 EXTRA = 128
-BLOCK = 32
+BLOCK = 96
 FIRST = (((0,), (0,)), ((), ()))
 SECOND = (((1,), (1,)), ((), ()))
 PLAIN = (((1,), (0,)), ((), ()))
@@ -175,43 +175,50 @@
 
 
 def terms_kernel(count, *refs):
-    chunks, (w_gate, w_up, w_down, rows_ref, cot_ref, send_ref, keep_ref) = refs[:count], refs[count:]
+    chunks, (w_gate, w_up, w_down, send_ref, keep_ref) = refs[:count], refs[count:]
     half = send_ref.shape[2]
-    width = rows_ref.shape[1]
+    width = w_gate.shape[0]
     core = lax.axis_index("dp") % 2
-    rows_ref[...] = join([ref.at[:, :width] for ref in chunks])
-    cot_ref[...] = join([ref.at[:, width:] for ref in chunks])
+    rows = join([ref.at[:, :width] for ref in chunks])
+    cot = join([ref.at[:, width:] for ref in chunks])
     for ref, side in ((send_ref, 1 - core), (keep_ref, core)):
         at = pl.ds(pl.multiple_of(side * half, half), half)
-        ref[0] = dot32(rows_ref[...], w_gate[:, at]).astype(BF16)
-        ref[1] = dot32(rows_ref[...], w_up[:, at]).astype(BF16)
-        ref[2] = dot32(cot_ref[...], w_down[at, :], SECOND).astype(BF16)
+        ref[0] = dot32(rows, w_gate[:, at]).astype(BF16)
+        ref[1] = dot32(rows, w_up[:, at]).astype(BF16)
+        ref[2] = dot32(cot, w_down[at, :], SECOND).astype(BF16)
 
 
 def terms(chunks, weights):
-    total, width = len(chunks) * CAP, chunks[0].shape[1] // 2
-    out = struct((3, total, weights[0].shape[1] // 2))
+    out = struct((3, len(chunks) * CAP, weights[0].shape[1] // 2))
     return call(
         functools.partial(terms_kernel, len(chunks)),
         "terms",
-        [struct((total, width))] * 2 + [out, out],
+        [out, out],
         [VMEM] * (len(chunks) + 3),
-        [VMEM] * 4,
+        [VMEM] * 2,
     )(*chunks, *weights)
 
 
-def add_kernel(*refs):
+def add_kernel(spans, *refs):
     *parts, out = refs
     for i in range(out.shape[0]):
-        sums = [a[i].astype(F32) + b[i].astype(F32) for a, b in zip(parts[::2], parts[1::2])]
+        sums = [
+            (a[i].astype(F32) + b[i].astype(F32))[lo:hi]
+            for a, b, (lo, hi) in zip(parts[::2], parts[1::2], spans)
+        ]
         out[i] = jnp.concatenate(sums, axis=0).astype(BF16)
 
 
-def add(*arrays):
-    total = sum(a.shape[1] for a in arrays[::2])
+def add(*arrays, spans=None):
+    spans = spans or [(0, a.shape[1]) for a in arrays[::2]]
+    total = sum(hi - lo for lo, hi in spans)
     shape = arrays[0].shape
     return call(
-        add_kernel, "add", struct((shape[0], total, shape[2])), [VMEM] * len(arrays), VMEM
+        functools.partial(add_kernel, spans),
+        "add",
+        struct((shape[0], total, shape[2])),
+        [VMEM] * len(arrays),
+        VMEM,
     )(*arrays)
 
 
@@ -333,14 +340,22 @@
     )(expert_pairs, routes, gates, *chunks)
 
 
-def turn_kernel(*refs):
-    *parts, out = refs
-    out[...] = join(parts).T
-
-
-def turn(parts):
-    shape = (parts[0].shape[1], sum(p.shape[0] for p in parts))
-    return call(turn_kernel, "turn", struct(shape), [VMEM] * len(parts), VMEM)(*parts)
+def turn_kernel(count, *refs):
+    turned, cot = refs[count:]
+    width = cot.shape[1]
+    turned[...] = join([ref.at[:, :width] for ref in refs[:count]]).T
+    cot[...] = join([ref.at[:, width:] for ref in refs[:count]])
+
+
+def turn(chunks):
+    total, width = len(chunks) * CAP, chunks[0].shape[1] // 2
+    return call(
+        functools.partial(turn_kernel, len(chunks)),
+        "turn",
+        [struct((width, total)), struct((total, width))],
+        [VMEM] * len(chunks),
+        [VMEM] * 2,
+    )(*chunks)
 
 
 def column_step(*widths):
@@ -354,9 +369,7 @@
     return [struct(shape) for shape in ((width, units), (width, units), (units, width))]
 
 
-def own_grads_kernel(step, turned, pre_grad, up_grad, hidden, *refs):
-    *cots, gate_out, up_out, down_out, cot = refs
-    cot[...] = join(cots)
+def own_grads_kernel(step, turned, cot, pre_grad, up_grad, hidden, gate_out, up_out, down_out):
     for left, right, out in (
         (turned[...], pre_grad, gate_out),
         (turned[...], up_grad, up_out),
@@ -367,17 +380,15 @@
             out[:, at] = dot32(left, right[:, at]).astype(BF16)
 
 
-def own_grads(turned, pre_grad, up_grad, hidden, cots):
-    width, total = turned.shape
-    units = hidden.shape[1]
+def own_grads(turned, cot, pre_grad, up_grad, hidden):
+    width, units = turned.shape[0], hidden.shape[1]
     return call(
         functools.partial(own_grads_kernel, column_step(units, width)),
         "own_grads",
         grad_shapes(width, units),
-        [VMEM] * (4 + len(cots)),
+        [VMEM] * 5,
         [VMEM] * 3,
-        [pltpu.VMEM((total, width), BF16)],
-    )(turned, pre_grad, up_grad, hidden, *cots)
+    )(turned, cot, pre_grad, up_grad, hidden)
 
 
 def grads_kernel(step, mine, other, turned, cot, *refs):
@@ -439,37 +450,35 @@
     far_grad = hop(after(out_grad, far), "expert", pairs)
     chunks = dispatch(chunks)
 
-    rows_a, cot_a, send, keep = terms(chunks[:1], weights)
+    send, keep = terms(chunks[:1], weights)
     sums_a = across(add(keep, core_hop(send)))
 
     far_chunks = pack_far(expert_pairs, far, after(far_grad, sums_a[1]), top)
     chunks[1] = after(chunks[1], far_chunks[0])
-    rows_b, cot_b, send, keep = terms(chunks[1:], weights)
+    send, keep = terms(chunks[1:], weights)
     far_chunks = dispatch(far_chunks)
     sums_b = across(add(keep, core_hop(send)))
 
     far_chunks[1] = after(far_chunks[1], sums_b[1])
     mine = add(*sums_a, *sums_b)
     other = core_hop(mine)
-    far_chunks[2] = after(far_chunks[2], mine)
-    far_rows, far_cot, send, keep = terms(far_chunks, weights)
+    send, keep = terms(far_chunks, weights)
     got = core_hop(send)
     (hidden, up_grad, pre_grad), sent = outputs(after(mine, send), other, weights, pairs)
     far_sums = across(add(keep, after(got, sent[0])))
     arrived = dispatch(sent, False)
-    turned = turn([after(rows_a, far_sums[0]), rows_b])
-    far_turned = turn([after(far_rows, turned)])
-    partial = own_grads(turned, pre_grad, up_grad, hidden, [cot_a, cot_b])
-
-    far_sums[1] = after(far_sums[1], far_turned, *partial, *arrived)
+
+    turned, cot = turn([after(chunks[0], far_sums[0])] + chunks[1:])
+    partial = own_grads(turned, cot, pre_grad, up_grad, hidden)
+    turned, cot = turn([after(far_chunks[0], partial[0])] + far_chunks[1:])
+
+    far_sums[1] = after(far_sums[1], turned, *arrived[1:])
     mine = add(*far_sums)
     other = core_hop(mine)
     layer_output, token_grad, values = combine(
         expert_pairs, routes, gates, [after(arrived[0], mine)] + arrived[1:], width
     )
-    grad_gate, grad_up, grad_down = grads(
-        mine, after(other, token_grad), far_turned, far_cot, partial
-    )
+    grad_gate, grad_up, grad_down = grads(mine, after(other, token_grad), turned, cot, partial)
     return layer_output, token_grad, values.T, grad_gate[None], grad_up[None], grad_down[None]
 
 

time: 106 us -> 105 us (level)
  no operation moved by 1% of the time
where the time goes in v3:
time: 105 us
  waiting for transfers between devices  44.9 us (43%)
  Pallas kernels  29.2 us (28%)
  starting transfers between devices  23.9 us (23%)
  local copies, waits for them, and re-layouts  5.67 us (5%)
    ppermute x19, waiting for transfers between devices, hop(): lax.ppermute(x, axis, [(i, i ^ distance) for i in range(lax.axis_size(axi...  44.9 us
    ppermute x19, starting transfers between devices, hop(): lax.ppermute(x, axis, [(i, i ^ distance) for i in range(lax.axis_size(axi...  23.9 us
    pallas_call x1, Pallas kernels, grads(): call(functools.partial(grads_kernel, step), 'grads', shapes, [VMEM] * 7,...  6.42 us
    pallas_call x3, Pallas kernels, terms(): call(functools.partial(terms_kernel, len(chunks)), 'terms', [out, out], [...  6.38 us
    unnamed x18, local copies, waits for them, and re-layouts  5.67 us
    pallas_call x1, Pallas kernels, own_grads(): call(functools.partial(own_grads_kernel, column_step(units, width)), 'own...  4.24 us
    pallas_call x1, Pallas kernels, outputs(): call(functools.partial(outputs_kernel, pairs), 'outputs', [struct((total,...  3.78 us
    pallas_call x1, Pallas kernels, pack_own(): call(functools.partial(pack_own_kernel, pairs), 'pack_own', [struct((tok,...  2.94 us
  transfers between devices with their start and end apart: 19, of which 12 were waited for; matrix products, arithmetic and copies ran while one was open for 0% of the time, Pallas kernels for 17%

profile of v3, /device:TPU:0, one launch (start us, length us, event | category | flops | bytes accessed | tf_op | source)
XLA Modules:
  0.0 104.7 jit_solution(1424102052846671886)
XLA Ops:
  0.6 2.9 %pack_own.1 = (bf16[128,1408]{1,0:T(8,128)(2,1)}, bf16[72,2560]{1,0:T(8,128)(2,1)}, bf16[72,2560]{1,0:T(8,128)(2,1)}, bf16[72,2560]{1,0:T(8,128)(2,1)}, bf16[72,2560]{1,0:T(8,128)(2,1)}) custom-call(s32[4]{0:T(128)} %pairs_ref.5, s32[2,128]{1,0:T(2,128)} %bitcast.12, f32[2,128]{1,0:T(2,128)} %bitcast.14, bf16[128,1280]{1,0:T(8,128)(2,1)} %tok_ref.1, ...), custom_call_target="tpu_custom_call" | custom-call | flops 1024 | bytes 524288 | tf_op jit(solution)/shard_map/pack_own/pallas_call | solution.py:113
  3.6 3.0 %collective-permute-start.2 = (bf16[72,2560]{1,0:T(8,128)(2,1)}, bf16[72,2560]{1,0:T(8,128)(2,1)S(1)}, u32[]{:S(2)}, u32[]{:S(2)}) collective-permute-start(bf16[72,2560]{1,0:T(8,128)(2,1)} %get-tuple-element.66), channel_id=1, source_target_pairs={{0,1},{1,0},{2,3},{3,2},{4,5},{5,4},{6,7},{7,6},{8,9},{9,8},{10,11... | collective-permute-start | bytes 1105928 | tf_op jit(solution)/shard_map/ppermute | solution.py:26
  6.5 1.6 %collective-permute-start.5 = (bf16[72,2560]{1,0:T(8,128)(2,1)}, bf16[72,2560]{1,0:T(8,128)(2,1)S(1)}, u32[]{:S(2)}, u32[]{:S(2)}) collective-permute-start(bf16[72,2560]{1,0:T(8,128)(2,1)} %get-tuple-element.71), channel_id=1, source_target_pairs={{0,2},{1,3},{2,0},{3,1},{4,6},{5,7},{6,4},{7,5},{8,10},{9,11},{10,... | collective-permute-start | bytes 1105928 | tf_op jit(solution)/shard_map/ppermute | solution.py:26
  8.1 2.6 %collective-permute-start.3 = (bf16[128,1408]{1,0:T(8,128)(2,1)}, bf16[128,1408]{1,0:T(8,128)(2,1)S(1)}, u32[]{:S(2)}, u32[]{:S(2)}) collective-permute-start(bf16[128,1408]{1,0:T(8,128)(2,1)} %get-tuple-element.59), channel_id=1, source_target_pairs={{0,4},{1,5},{2,6},{3,7},{4,0},{5,1},{6,2},{7,3},{8,12},{9,13},{10,... | collective-permute-start | bytes 1081352 | tf_op jit(solution)/shard_map/ppermute | solution.py:26
  10.7 1.7 %copy-done = bf16[1,1280,1024]{2,1,0:T(8,128)(2,1)S(1)} copy-done((bf16[1,1280,1024]{2,1,0:T(8,128)(2,1)S(1)}, bf16[1,1280,1024]{2,1,0:T(8,128)(2,1)}, u32[]{:S(2)}) %copy-start) | copy-done | bytes 2621464
  12.5 1.7 %copy-done.1 = bf16[1,1280,1024]{2,1,0:T(8,128)(2,1)S(1)} copy-done((bf16[1,1280,1024]{2,1,0:T(8,128)(2,1)S(1)}, bf16[1,1280,1024]{2,1,0:T(8,128)(2,1)}, u32[]{:S(2)}) %copy-start.1) | copy-done | bytes 2621464
  14.2 1.7 %copy-done.2 = bf16[1,1024,1280]{2,1,0:T(8,128)(2,1)S(1)} copy-done((bf16[1,1024,1280]{2,1,0:T(8,128)(2,1)S(1)}, bf16[1,1024,1280]{2,1,0:T(8,128)(2,1)}, u32[]{:S(2)}) %copy-start.2) | copy-done | bytes 2621464
  15.9 0.6 load.1
  16.5 0.4 copy-done.3
  16.9 1.8 %terms.3 = (bf16[3,72,512]{2,1,0:T(8,128)(2,1)S(1)}, bf16[3,72,512]{2,1,0:T(8,128)(2,1)S(1)}) custom-call(bf16[72,2560]{1,0:T(8,128)(2,1)S(1)} %copy-done.3, bf16[1280,1024]{1,0:T(8,128)(2,1)S(1)} %get-tuple-element.61.refs_1_.refs_3_.refs_4_.w_gate, bf16[1280,1024]{1,0:T(8,128)(2,1)S(1)} %get-tuple-element.62.refs_2_.refs_4_.refs_5_.w_up, ...), custom_call_target="tpu_custom_call" | custom-call | flops 1024 | bytes 524288 | tf_op jit(solution)/shard_map/terms/pallas_call | solution.py:193
  18.7 0.1 collective-permute-start
  18.8 0.0 collective-permute-done.2.refs_0_.refs_1_
  18.8 5.7 %collective-permute-done.5.refs_1_.refs_2_ = bf16[72,2560]{1,0:T(8,128)(2,1)S(1)} collective-permute-done((bf16[72,2560]{1,0:T(8,128)(2,1)}, bf16[72,2560]{1,0:T(8,128)(2,1)S(1)}, u32[]{:S(2)}, u32[]{:S(2)}) %collective-permute-start.5) | collective-permute-done | bytes 368672 | tf_op jit(solution)/shard_map/ppermute | solution.py:26
  24.5 0.0 copy-done.8
  24.5 0.0 collective-permute-start.6
  24.5 0.0 collective-permute-done.3.far_ref
  24.5 0.0 copy-done.7
  24.6 3.0 %collective-permute-start.4 = (bf16[128,1280]{1,0:T(8,128)(2,1)S(1)}, bf16[128,1280]{1,0:T(8,128)(2,1)S(1)}, u32[]{:S(2)}, u32[]{:S(2)}) collective-permute-start(bf16[128,1280]{1,0:T(8,128)(2,1)S(1)} %copy-done.7), channel_id=1, source_target_pairs={{0,4},{1,5},{2,6},{3,7},{4,0},{5,1},{6,2},{7,3},{8,12},{9,13},{10,... | collective-permute-start | bytes 983048 | tf_op jit(solution)/shard_map/ppermute | solution.py:26
  27.6 0.0 collective-permute-done.refs_1_
  27.6 0.1 add.5.refs_0_
  27.6 1.6 %collective-permute-start.1 = (bf16[3,72,512]{2,1,0:T(8,128)(2,1)S(1)}, bf16[3,72,512]{2,1,0:T(8,128)(2,1)S(1)}, u32[]{:S(2)}, u32[]{:S(2)}) collective-permute-start(bf16[3,72,512]{2,1,0:T(8,128)(2,1)S(1)} %add.5.refs_0_), channel_id=1, source_target_pairs={{0,16},{8,24},{16,0},{24,8},{1,17},{9,25},{17,1},{25,9},{2,18},{10... | collective-permute-start | bytes 663560 | tf_op jit(solution)/shard_map/ppermute | solution.py:26
  29.2 4.4 %collective-permute-done.1.refs_1_ = bf16[3,72,512]{2,1,0:T(8,128)(2,1)S(1)} collective-permute-done((bf16[3,72,512]{2,1,0:T(8,128)(2,1)S(1)}, bf16[3,72,512]{2,1,0:T(8,128)(2,1)S(1)}, u32[]{:S(2)}, u32[]{:S(2)}) %collective-permute-start.1) | collective-permute-done | bytes 221216 | tf_op jit(solution)/shard_map/ppermute | solution.py:26
  33.6 5.0 %collective-permute-done.4.grad_ref = bf16[128,1280]{1,0:T(8,128)(2,1)S(1)} collective-permute-done((bf16[128,1280]{1,0:T(8,128)(2,1)S(1)}, bf16[128,1280]{1,0:T(8,128)(2,1)S(1)}, u32[]{:S(2)}, u32[]{:S(2)}) %collective-permute-start.4) | collective-permute-done | bytes 327712 | tf_op jit(solution)/shard_map/ppermute | solution.py:26
  38.6 0.0 copy-done.4
  38.6 1.3 %pack_far.1 = (bf16[72,2560]{1,0:T(8,128)(2,1)S(1)}, bf16[72,2560]{1,0:T(8,128)(2,1)S(1)}, bf16[72,2560]{1,0:T(8,128)(2,1)S(1)}, bf16[72,2560]{1,0:T(8,128)(2,1)S(1)}) custom-call(s32[4]{0:T(128)S(1)} %copy-done.4, bf16[128,1408]{1,0:T(8,128)(2,1)S(1)} %collective-permute-done.3.far_ref, bf16[128,1280]{1,0:T(8,128)(2,1)S(1)} %collective-permute-done.4.grad_ref), custom_call_target="tpu_custom_call" | custom-call | flops 1024 | bytes 524288 | tf_op jit(solution)/shard_map/pack_far/pallas_call | solution.py:140
  39.9 1.7 %collective-permute-done.6.refs_2_.refs_3_ = bf16[72,2560]{1,0:T(8,128)(2,1)S(1)} collective-permute-done((bf16[72,2560]{1,0:T(8,128)(2,1)S(1)}, bf16[72,2560]{1,0:T(8,128)(2,1)S(1)}, u32[]{:S(2)}, u32[]{:S(2)}) %collective-permute-start.6) | collective-permute-done | bytes 368672 | tf_op jit(solution)/shard_map/ppermute | solution.py:26
  41.6 2.1 %terms.4 = (bf16[3,216,512]{2,1,0:T(8,128)(2,1)S(1)}, bf16[3,216,512]{2,1,0:T(8,128)(2,1)S(1)}) custom-call(bf16[72,2560]{1,0:T(8,128)(2,1)S(1)} %collective-permute-done.2.refs_0_.refs_1_, bf16[72,2560]{1,0:T(8,128)(2,1)S(1)} %collective-permute-done.5.refs_1_.refs_2_, bf16[72,2560]{1,0:T(8,128)(2,1)S(1)} %collective-permute-done.6.refs_2_.refs_3_, ...), custom_call_target="tpu_custom_call" | custom-call | flops 1024 | bytes 524288 | tf_op jit(solution)/shard_map/terms/pallas_call | solution.py:193
  43.7 0.1 collective-permute-start.7
  43.8 0.7 collective-permute-start.9
  44.5 2.3 %collective-permute-start.10 = (bf16[72,2560]{1,0:T(8,128)(2,1)S(1)}, bf16[72,2560]{1,0:T(8,128)(2,1)S(1)}, u32[]{:S(2)}, u32[]{:S(2)}) collective-permute-start(bf16[72,2560]{1,0:T(8,128)(2,1)S(1)} %get-tuple-element.78), channel_id=1, source_target_pairs={{0,2},{1,3},{2,0},{3,1},{4,6},{5,7},{6,4},{7,5},{8,10},{9,11},{10,... | collective-permute-start | bytes 1105928 | tf_op jit(solution)/shard_map/ppermute | solution.py:26
  46.8 0.0 collective-permute-done.7.refs_1_
  46.8 0.2 add.6.refs_2_
  47.0 1.5 %collective-permute-start.8 = (bf16[3,216,512]{2,1,0:T(8,128)(2,1)S(1)}, bf16[3,216,512]{2,1,0:T(8,128)(2,1)S(1)}, u32[]{:S(2)}, u32[]{:S(2)}) collective-permute-start(bf16[3,216,512]{2,1,0:T(8,128)(2,1)S(1)} %add.6.refs_2_), channel_id=1, source_target_pairs={{0,16},{8,24},{16,0},{24,8},{1,17},{9,25},{17,1},{25,9},{2,18},{10... | collective-permute-start | bytes 1990664 | tf_op jit(solution)/shard_map/ppermute | solution.py:26
  48.5 6.3 %collective-permute-done.9.refs_1_ = bf16[72,2560]{1,0:T(8,128)(2,1)S(1)} collective-permute-done((bf16[72,2560]{1,0:T(8,128)(2,1)S(1)}, bf16[72,2560]{1,0:T(8,128)(2,1)S(1)}, u32[]{:S(2)}, u32[]{:S(2)}) %collective-permute-start.9) | collective-permute-done | bytes 368672 | tf_op jit(solution)/shard_map/ppermute | solution.py:26
  54.8 0.9 collective-permute-done.10.refs_2_
  55.7 2.3 %collective-permute-start.11 = (bf16[72,2560]{1,0:T(8,128)(2,1)S(1)}, bf16[72,2560]{1,0:T(8,128)(2,1)S(1)}, u32[]{:S(2)}, u32[]{:S(2)}) collective-permute-start(bf16[72,2560]{1,0:T(8,128)(2,1)S(1)} %get-tuple-element.80), channel_id=1, source_target_pairs={{0,3},{1,2},{2,1},{3,0},{4,7},{5,6},{6,5},{7,4},{8,11},{9,10},{10,... | collective-permute-start | bytes 1105928 | tf_op jit(solution)/shard_map/ppermute | solution.py:26
  58.0 5.7 %collective-permute-done.8.refs_3_ = bf16[3,216,512]{2,1,0:T(8,128)(2,1)S(1)} collective-permute-done((bf16[3,216,512]{2,1,0:T(8,128)(2,1)S(1)}, bf16[3,216,512]{2,1,0:T(8,128)(2,1)S(1)}, u32[]{:S(2)}, u32[]{:S(2)}) %collective-permute-start.8) | collective-permute-done | bytes 663584 | tf_op jit(solution)/shard_map/ppermute | solution.py:26
  63.7 0.2 add.7.mine
  63.9 0.1 collective-permute-start.12
  64.0 2.8 %collective-permute-done.11.refs_3_ = bf16[72,2560]{1,0:T(8,128)(2,1)S(1)} collective-permute-done((bf16[72,2560]{1,0:T(8,128)(2,1)S(1)}, bf16[72,2560]{1,0:T(8,128)(2,1)S(1)}, u32[]{:S(2)}, u32[]{:S(2)}) %collective-permute-start.11) | collective-permute-done | bytes 368672 | tf_op jit(solution)/shard_map/ppermute | solution.py:26
  66.8 2.4 %terms.5 = (bf16[3,288,512]{2,1,0:T(8,128)(2,1)S(1)}, bf16[3,288,512]{2,1,0:T(8,128)(2,1)S(1)}) custom-call(bf16[72,2560]{1,0:T(8,128)(2,1)S(1)} %get-tuple-element.93.refs_0_, bf16[72,2560]{1,0:T(8,128)(2,1)S(1)} %collective-permute-done.9.refs_1_, bf16[72,2560]{1,0:T(8,128)(2,1)S(1)} %collective-permute-done.10.refs_2_, ...), custom_call_target="tpu_custom_call" | custom-call | flops 1024 | bytes 524288 | tf_op jit(solution)/shard_map/terms/pallas_call | solution.py:193
  69.2 0.1 collective-permute-start.13
  69.3 0.0 collective-permute-done.12.other
  69.3 3.8 %outputs.1 = (bf16[288,1024]{1,0:T(8,128)(2,1)S(1)}, bf16[288,1024]{1,0:T(8,128)(2,1)S(1)}, bf16[288,1024]{1,0:T(8,128)(2,1)S(1)}, bf16[72,2688]{1,0:T(8,128)(2,...) custom-call(bf16[3,288,512]{2,1,0:T(8,128)(2,1)S(1)} %add.7.mine, ...), custom_call_target="tpu_custom_call" | custom-call | flops 1024 | bytes 524288 | tf_op jit(solution)/shard_map/outputs/pallas_call | solution.py:299
  73.1 0.0 collective-permute-done.13.refs_1_
  73.1 0.2 add.8.refs_0_
  73.3 1.5 %collective-permute-start.14 = (bf16[3,288,512]{2,1,0:T(8,128)(2,1)S(1)}, bf16[3,288,512]{2,1,0:T(8,128)(2,1)S(1)}, u32[]{:S(2)}, u32[]{:S(2)}) collective-permute-start(bf16[3,288,512]{2,1,0:T(8,128)(2,1)S(1)} %add.8.refs_0_), channel_id=1, source_target_pairs={{0,16},{8,24},{16,0},{24,8},{1,17},{9,25},{17,1},{25,9},{2,18},{10... | collective-permute-start | bytes 2654216 | tf_op jit(solution)/shard_map/ppermute | solution.py:26
  74.9 1.1 %collective-permute-start.15 = (bf16[72,2688]{1,0:T(8,128)(2,1)S(1)}, bf16[72,2688]{1,0:T(8,128)(2,1)S(1)}, u32[]{:S(2)}, u32[]{:S(2)}) collective-permute-start(bf16[72,2688]{1,0:T(8,128)(2,1)S(1)} %get-tuple-element.95), channel_id=1, source_target_pairs={{0,1},{1,0},{2,3},{3,2},{4,5},{5,4},{6,7},{7,6},{8,9},{9,8},{10,11... | collective-permute-start | bytes 1161224 | tf_op jit(solution)/shard_map/ppermute | solution.py:26
  75.9 1.5 %collective-permute-start.16 = (bf16[72,2688]{1,0:T(8,128)(2,1)S(1)}, bf16[72,2688]{1,0:T(8,128)(2,1)S(1)}, u32[]{:S(2)}, u32[]{:S(2)}) collective-permute-start(bf16[72,2688]{1,0:T(8,128)(2,1)S(1)} %get-tuple-element.96), channel_id=1, source_target_pairs={{0,2},{1,3},{2,0},{3,1},{4,6},{5,7},{6,4},{7,5},{8,10},{9,11},{10,... | collective-permute-start | bytes 1161224 | tf_op jit(solution)/shard_map/ppermute | solution.py:26
  77.4 1.0 collective-permute-start.17
  78.3 0.3 turn.2
  78.7 4.2 %own_grads.1 = (bf16[1280,1024]{1,0:T(8,128)(2,1)S(1)}, bf16[1280,1024]{1,0:T(8,128)(2,1)S(1)}, bf16[1024,1280]{1,0:T(8,128)(2,1)S(1)}) custom-call(bf16[1280,288]{1,0:T(8,128)(2,1)S(1)} %get-tuple-element.87.turned, bf16[288,1280]{1,0:T(8,128)(2,1)S(1)} %get-tuple-element.88.cot, bf16[288,1024]{1,0:T(8,128)(2,1)S(1)} %get-tuple-element.89.pre_grad, ...), custom_call_target="tpu_custom_call" | custom-call | flops 1024 | bytes 524288 | tf_op jit(solution)/shard_map/own_grads/pallas_call | solution.py:385
  82.9 0.0 copy-start.5
  82.9 0.0 copy-start.6
  82.9 0.3 turn.3
  83.3 2.7 %collective-permute-done.15.refs_1_ = bf16[72,2688]{1,0:T(8,128)(2,1)S(1)} collective-permute-done((bf16[72,2688]{1,0:T(8,128)(2,1)S(1)}, bf16[72,2688]{1,0:T(8,128)(2,1)S(1)}, u32[]{:S(2)}, u32[]{:S(2)}) %collective-permute-start.15) | collective-permute-done | bytes 387104 | tf_op jit(solution)/shard_map/ppermute | solution.py:26
  85.9 1.9 %collective-permute-done.16.refs_2_ = bf16[72,2688]{1,0:T(8,128)(2,1)S(1)} collective-permute-done((bf16[72,2688]{1,0:T(8,128)(2,1)S(1)}, bf16[72,2688]{1,0:T(8,128)(2,1)S(1)}, u32[]{:S(2)}, u32[]{:S(2)}) %collective-permute-start.16) | collective-permute-done | bytes 387104 | tf_op jit(solution)/shard_map/ppermute | solution.py:26
  87.8 7.6 %collective-permute-done.17.refs_3_ = bf16[72,2688]{1,0:T(8,128)(2,1)S(1)} collective-permute-done((bf16[72,2688]{1,0:T(8,128)(2,1)S(1)}, bf16[72,2688]{1,0:T(8,128)(2,1)S(1)}, u32[]{:S(2)}, u32[]{:S(2)}) %collective-permute-start.17) | collective-permute-done | bytes 387104 | tf_op jit(solution)/shard_map/ppermute | solution.py:26
  95.4 0.0 collective-permute-done.14.refs_1_
  95.4 0.2 add.9.mine
  95.6 0.1 collective-permute-start.18
  95.7 2.2 %combine.1 = (bf16[128,1280]{1,0:T(8,128)(2,1)}, bf16[128,1280]{1,0:T(8,128)(2,1)}, f32[2,128]{1,0:T(2,128)}) custom-call(s32[4]{0:T(128)S(1)} %copy-done.4, s32[2,128]{1,0:T(2,128)S(1)} %bitcast.13, f32[2,128]{1,0:T(2,128)S(1)} %bitcast.15, bf16[72,2688]{1,0:T(8,128)(2,1)S(1)} %get-tuple-element.99.refs_0_, ...), custom_call_target="tpu_custom_call" | custom-call | flops 1024 | bytes 524288 | tf_op jit(solution)/shard_map/combine/pallas_call | solution.py:333
  97.9 0.2 collective-permute-done.18.other
  98.1 6.4 %grads.1 = (bf16[1280,1024]{1,0:T(8,128)(2,1)}, bf16[1280,1024]{1,0:T(8,128)(2,1)}, bf16[1024,1280]{1,0:T(8,128)(2,1)}) custom-call(bf16[3,288,512]{2,1,0:T(8,128)(2,1)S(1)} %add.9.mine, bf16[3,288,512]{2,1,0:T(8,128)(2,1)S(1)} %collective-permute-done.18.other, bf16[1280,288]{1,0:T(8,128)(2,1)S(1)} %get-tuple-element.94.turned, ...), custom_call_target="tpu_custom_call" | custom-call | flops 1024 | bytes 524288 | tf_op jit(solution)/shard_map/grads/pallas_call | solution.py:426
  (9 shorter events, 0.0 us)
Async XLA Ops:
  3.6 15.3 %collective-permute-start.2 = (bf16[72,2560]{1,0:T(8,128)(2,1)}, bf16[72,2560]{1,0:T(8,128)(2,1)S(1)}, u32[]{:S(2)}, u32[]{:S(2)}) collective-permute-start(bf16[72,2560]{1,0:T(8,128)(2,1)} %get-tuple-element.66), channel_id=1, source_target_pairs={{0,1},{1,0},{2,3},{3,2},{4,5},{5,4},{6,7},{7,6},{8,9},{9,8},{10,11... | collective-permute-start | bytes 1105928 | tf_op jit(solution)/shard_map/ppermute | solution.py:26
  6.5 18.0 %collective-permute-start.5 = (bf16[72,2560]{1,0:T(8,128)(2,1)}, bf16[72,2560]{1,0:T(8,128)(2,1)S(1)}, u32[]{:S(2)}, u32[]{:S(2)}) collective-permute-start(bf16[72,2560]{1,0:T(8,128)(2,1)} %get-tuple-element.71), channel_id=1, source_target_pairs={{0,2},{1,3},{2,0},{3,1},{4,6},{5,7},{6,4},{7,5},{8,10},{9,11},{10,... | collective-permute-start | bytes 1105928 | tf_op jit(solution)/shard_map/ppermute | solution.py:26
  8.1 16.4 %collective-permute-start.3 = (bf16[128,1408]{1,0:T(8,128)(2,1)}, bf16[128,1408]{1,0:T(8,128)(2,1)S(1)}, u32[]{:S(2)}, u32[]{:S(2)}) collective-permute-start(bf16[128,1408]{1,0:T(8,128)(2,1)} %get-tuple-element.59), channel_id=1, source_target_pairs={{0,4},{1,5},{2,6},{3,7},{4,0},{5,1},{6,2},{7,3},{8,12},{9,13},{10,... | collective-permute-start | bytes 1081352 | tf_op jit(solution)/shard_map/ppermute | solution.py:26
  10.7 1.7 %copy-start = (bf16[1,1280,1024]{2,1,0:T(8,128)(2,1)S(1)}, bf16[1,1280,1024]{2,1,0:T(8,128)(2,1)}, u32[]{:S(2)}) copy-start(bf16[1,1280,1024]{2,1,0:T(8,128)(2,1)} %param.13) | copy-start | bytes 7864324
  12.5 1.7 %copy-start.1 = (bf16[1,1280,1024]{2,1,0:T(8,128)(2,1)S(1)}, bf16[1,1280,1024]{2,1,0:T(8,128)(2,1)}, u32[]{:S(2)}) copy-start(bf16[1,1280,1024]{2,1,0:T(8,128)(2,1)} %param.14) | copy-start | bytes 7864324
  14.2 1.7 %copy-start.2 = (bf16[1,1024,1280]{2,1,0:T(8,128)(2,1)S(1)}, bf16[1,1024,1280]{2,1,0:T(8,128)(2,1)}, u32[]{:S(2)}) copy-start(bf16[1,1024,1280]{2,1,0:T(8,128)(2,1)} %param.15) | copy-start | bytes 7864324
  15.9 1.0 copy-start.3
  16.9 7.6 %copy-start.8 = (bf16[72,2560]{1,0:T(8,128)(2,1)S(1)}, bf16[72,2560]{1,0:T(8,128)(2,1)}, u32[]{:S(2)}) copy-start(bf16[72,2560]{1,0:T(8,128)(2,1)} %get-tuple-element.73) | copy-start | bytes 1105924
  16.9 7.6 %copy-start.7 = (bf16[128,1280]{1,0:T(8,128)(2,1)S(1)}, bf16[128,1280]{1,0:T(8,128)(2,1)}, u32[]{:S(2)}) copy-start(bf16[128,1280]{1,0:T(8,128)(2,1)} %grad_ref.1) | copy-start | bytes 983044
  16.9 21.7 %copy-start.4 = (s32[4]{0:T(128)S(1)}, s32[4]{0:T(128)}, u32[]{:S(2)}) copy-start(s32[4]{0:T(128)} %pairs_ref.5) | copy-start | bytes 52
  18.7 8.8 %collective-permute-start = (bf16[3,72,512]{2,1,0:T(8,128)(2,1)S(1)}, bf16[3,72,512]{2,1,0:T(8,128)(2,1)S(1)}, u32[]{:S(2)}, u32[]{:S(2)}) collective-permute-start(bf16[3,72,512]{2,1,0:T(8,128)(2,1)S(1)} %get-tuple-element.65), channel_id=1, source_target_pairs={{0,8},{8,0},{16,24},{24,16},{1,9},{9,1},{17,25},{25,17},{2,10},{10... | collective-permute-start | bytes 663560 | tf_op jit(solution)/shard_map/ppermute | solution.py:26
  24.5 17.1 %collective-permute-start.6 = (bf16[72,2560]{1,0:T(8,128)(2,1)S(1)}, bf16[72,2560]{1,0:T(8,128)(2,1)S(1)}, u32[]{:S(2)}, u32[]{:S(2)}) collective-permute-start(bf16[72,2560]{1,0:T(8,128)(2,1)S(1)} %copy-done.8), channel_id=1, source_target_pairs={{0,3},{1,2},{2,1},{3,0},{4,7},{5,6},{6,5},{7,4},{8,11},{9,10},{10,... | collective-permute-start | bytes 1105928 | tf_op jit(solution)/shard_map/ppermute | solution.py:26
  24.6 14.1 %collective-permute-start.4 = (bf16[128,1280]{1,0:T(8,128)(2,1)S(1)}, bf16[128,1280]{1,0:T(8,128)(2,1)S(1)}, u32[]{:S(2)}, u32[]{:S(2)}) collective-permute-start(bf16[128,1280]{1,0:T(8,128)(2,1)S(1)} %copy-done.7), channel_id=1, source_target_pairs={{0,4},{1,5},{2,6},{3,7},{4,0},{5,1},{6,2},{7,3},{8,12},{9,13},{10,... | collective-permute-start | bytes 983048 | tf_op jit(solution)/shard_map/ppermute | solution.py:26
  27.6 6.0 %collective-permute-start.1 = (bf16[3,72,512]{2,1,0:T(8,128)(2,1)S(1)}, bf16[3,72,512]{2,1,0:T(8,128)(2,1)S(1)}, u32[]{:S(2)}, u32[]{:S(2)}) collective-permute-start(bf16[3,72,512]{2,1,0:T(8,128)(2,1)S(1)} %add.5.refs_0_), channel_id=1, source_target_pairs={{0,16},{8,24},{16,0},{24,8},{1,17},{9,25},{17,1},{25,9},{2,18},{10... | collective-permute-start | bytes 663560 | tf_op jit(solution)/shard_map/ppermute | solution.py:26
  43.7 3.1 %collective-permute-start.7 = (bf16[3,216,512]{2,1,0:T(8,128)(2,1)S(1)}, bf16[3,216,512]{2,1,0:T(8,128)(2,1)S(1)}, u32[]{:S(2)}, u32[]{:S(2)}) collective-permute-start(bf16[3,216,512]{2,1,0:T(8,128)(2,1)S(1)} %get-tuple-element.75), channel_id=1, source_target_pairs={{0,8},{8,0},{16,24},{24,16},{1,9},{9,1},{17,25},{25,17},{2,10},{10... | collective-permute-start | bytes 1990664 | tf_op jit(solution)/shard_map/ppermute | solution.py:26
  43.8 11.0 %collective-permute-start.9 = (bf16[72,2560]{1,0:T(8,128)(2,1)S(1)}, bf16[72,2560]{1,0:T(8,128)(2,1)S(1)}, u32[]{:S(2)}, u32[]{:S(2)}) collective-permute-start(bf16[72,2560]{1,0:T(8,128)(2,1)S(1)} %get-tuple-element.76), channel_id=1, source_target_pairs={{0,1},{1,0},{2,3},{3,2},{4,5},{5,4},{6,7},{7,6},{8,9},{9,8},{10,11... | collective-permute-start | bytes 1105928 | tf_op jit(solution)/shard_map/ppermute | solution.py:26
  44.5 11.2 %collective-permute-start.10 = (bf16[72,2560]{1,0:T(8,128)(2,1)S(1)}, bf16[72,2560]{1,0:T(8,128)(2,1)S(1)}, u32[]{:S(2)}, u32[]{:S(2)}) collective-permute-start(bf16[72,2560]{1,0:T(8,128)(2,1)S(1)} %get-tuple-element.78), channel_id=1, source_target_pairs={{0,2},{1,3},{2,0},{3,1},{4,6},{5,7},{6,4},{7,5},{8,10},{9,11},{10,... | collective-permute-start | bytes 1105928 | tf_op jit(solution)/shard_map/ppermute | solution.py:26
  47.0 16.8 %collective-permute-start.8 = (bf16[3,216,512]{2,1,0:T(8,128)(2,1)S(1)}, bf16[3,216,512]{2,1,0:T(8,128)(2,1)S(1)}, u32[]{:S(2)}, u32[]{:S(2)}) collective-permute-start(bf16[3,216,512]{2,1,0:T(8,128)(2,1)S(1)} %add.6.refs_2_), channel_id=1, source_target_pairs={{0,16},{8,24},{16,0},{24,8},{1,17},{9,25},{17,1},{25,9},{2,18},{10... | collective-permute-start | bytes 1990664 | tf_op jit(solution)/shard_map/ppermute | solution.py:26
  55.7 11.1 %collective-permute-start.11 = (bf16[72,2560]{1,0:T(8,128)(2,1)S(1)}, bf16[72,2560]{1,0:T(8,128)(2,1)S(1)}, u32[]{:S(2)}, u32[]{:S(2)}) collective-permute-start(bf16[72,2560]{1,0:T(8,128)(2,1)S(1)} %get-tuple-element.80), channel_id=1, source_target_pairs={{0,3},{1,2},{2,1},{3,0},{4,7},{5,6},{6,5},{7,4},{8,11},{9,10},{10,... | collective-permute-start | bytes 1105928 | tf_op jit(solution)/shard_map/ppermute | solution.py:26
  63.9 5.4 %collective-permute-start.12 = (bf16[3,288,512]{2,1,0:T(8,128)(2,1)S(1)}, bf16[3,288,512]{2,1,0:T(8,128)(2,1)S(1)}, u32[]{:S(2)}, u32[]{:S(2)}) collective-permute-start(bf16[3,288,512]{2,1,0:T(8,128)(2,1)S(1)} %add.7.mine), channel_id=1, source_target_pairs={{0,8},{8,0},{16,24},{24,16},{1,9},{9,1},{17,25},{25,17},{2,10},{10... | collective-permute-start | bytes 2654216 | tf_op jit(solution)/shard_map/ppermute | solution.py:26
  69.2 3.9 %collective-permute-start.13 = (bf16[3,288,512]{2,1,0:T(8,128)(2,1)S(1)}, bf16[3,288,512]{2,1,0:T(8,128)(2,1)S(1)}, u32[]{:S(2)}, u32[]{:S(2)}) collective-permute-start(bf16[3,288,512]{2,1,0:T(8,128)(2,1)S(1)} %get-tuple-element.81), channel_id=1, source_target_pairs={{0,8},{8,0},{16,24},{24,16},{1,9},{9,1},{17,25},{25,17},{2,10},{10... | collective-permute-start | bytes 2654216 | tf_op jit(solution)/shard_map/ppermute | solution.py:26
  73.3 22.1 %collective-permute-start.14 = (bf16[3,288,512]{2,1,0:T(8,128)(2,1)S(1)}, bf16[3,288,512]{2,1,0:T(8,128)(2,1)S(1)}, u32[]{:S(2)}, u32[]{:S(2)}) collective-permute-start(bf16[3,288,512]{2,1,0:T(8,128)(2,1)S(1)} %add.8.refs_0_), channel_id=1, source_target_pairs={{0,16},{8,24},{16,0},{24,8},{1,17},{9,25},{17,1},{25,9},{2,18},{10... | collective-permute-start | bytes 2654216 | tf_op jit(solution)/shard_map/ppermute | solution.py:26
  74.9 11.1 %collective-permute-start.15 = (bf16[72,2688]{1,0:T(8,128)(2,1)S(1)}, bf16[72,2688]{1,0:T(8,128)(2,1)S(1)}, u32[]{:S(2)}, u32[]{:S(2)}) collective-permute-start(bf16[72,2688]{1,0:T(8,128)(2,1)S(1)} %get-tuple-element.95), channel_id=1, source_target_pairs={{0,1},{1,0},{2,3},{3,2},{4,5},{5,4},{6,7},{7,6},{8,9},{9,8},{10,11... | collective-permute-start | bytes 1161224 | tf_op jit(solution)/shard_map/ppermute | solution.py:26
  75.9 11.9 %collective-permute-start.16 = (bf16[72,2688]{1,0:T(8,128)(2,1)S(1)}, bf16[72,2688]{1,0:T(8,128)(2,1)S(1)}, u32[]{:S(2)}, u32[]{:S(2)}) collective-permute-start(bf16[72,2688]{1,0:T(8,128)(2,1)S(1)} %get-tuple-element.96), channel_id=1, source_target_pairs={{0,2},{1,3},{2,0},{3,1},{4,6},{5,7},{6,4},{7,5},{8,10},{9,11},{10,... | collective-permute-start | bytes 1161224 | tf_op jit(solution)/shard_map/ppermute | solution.py:26
  77.4 18.0 %collective-permute-start.17 = (bf16[72,2688]{1,0:T(8,128)(2,1)S(1)}, bf16[72,2688]{1,0:T(8,128)(2,1)S(1)}, u32[]{:S(2)}, u32[]{:S(2)}) collective-permute-start(bf16[72,2688]{1,0:T(8,128)(2,1)S(1)} %get-tuple-element.97), channel_id=1, source_target_pairs={{0,3},{1,2},{2,1},{3,0},{4,7},{5,6},{6,5},{7,4},{8,11},{9,10},{10,... | collective-permute-start | bytes 1161224 | tf_op jit(solution)/shard_map/ppermute | solution.py:26
  82.9 12.8 %copy-start.5 = (s32[128,2]{0,1:T(2,128)S(1)}, s32[128,2]{0,1:T(2,128)}, u32[]{:S(2)}) copy-start(s32[128,2]{0,1:T(2,128)} %param.11) | copy-start | bytes 3076
  82.9 12.8 %copy-start.6 = (f32[128,2]{0,1:T(2,128)S(1)}, f32[128,2]{0,1:T(2,128)}, u32[]{:S(2)}) copy-start(f32[128,2]{0,1:T(2,128)} %param.10) | copy-start | bytes 3076
  95.6 2.5 %collective-permute-start.18 = (bf16[3,288,512]{2,1,0:T(8,128)(2,1)S(1)}, bf16[3,288,512]{2,1,0:T(8,128)(2,1)S(1)}, u32[]{:S(2)}, u32[]{:S(2)}) collective-permute-start(bf16[3,288,512]{2,1,0:T(8,128)(2,1)S(1)} %add.9.mine), channel_id=1, source_target_pairs={{0,8},{8,0},{16,24},{24,16},{1,9},{9,1},{17,25},{25,17},{2,10},{10... | collective-permute-start | bytes 2654216 | tf_op jit(solution)/shard_map/ppermute | solution.py:26

commit v4 on v3

--- a/solution.py
+++ b/solution.py
@@ -10,7 +10,7 @@
 HALF = 36
 CAP = 2 * HALF
 EXTRA = 128
-BLOCK = 96
+BLOCK = 144
 FIRST = (((0,), (0,)), ((), ()))
 SECOND = (((1,), (1,)), ((), ()))
 PLAIN = (((1,), (0,)), ((), ()))

time: 105 us -> 105 us (level)
  transfers between devices with their start and end apart: 19 -> 19, of which waited for: 12 -> 12; matrix products, arithmetic and copies ran while one was open for 0% -> 0% of each run, Pallas kernels for 17% -> 16%
where the time goes in v4:
time: 105 us
  waiting for transfers between devices  44.9 us (43%)
  Pallas kernels  29.1 us (28%)
  starting transfers between devices  23.9 us (23%)
  local copies, waits for them, and re-layouts  5.67 us (5%)
    ppermute x19, waiting for transfers between devices, hop(): lax.ppermute(x, axis, [(i, i ^ distance) for i in range(lax.axis_size(axi...  44.9 us
    ppermute x19, starting transfers between devices, hop(): lax.ppermute(x, axis, [(i, i ^ distance) for i in range(lax.axis_size(axi...  23.9 us
    pallas_call x1, Pallas kernels, grads(): call(functools.partial(grads_kernel, step), 'grads', shapes, [VMEM] * 7,...  6.44 us
    pallas_call x3, Pallas kernels, terms(): call(functools.partial(terms_kernel, len(chunks)), 'terms', [out, out], [...  6.38 us
    unnamed x18, local copies, waits for them, and re-layouts  5.67 us
    pallas_call x1, Pallas kernels, own_grads(): call(functools.partial(own_grads_kernel, column_step(units, width)), 'own...  4.24 us
    pallas_call x1, Pallas kernels, outputs(): call(functools.partial(outputs_kernel, pairs), 'outputs', [struct((total,...  3.7 us
    pallas_call x1, Pallas kernels, pack_own(): call(functools.partial(pack_own_kernel, pairs), 'pack_own', [struct((tok,...  2.94 us
  transfers between devices with their start and end apart: 19, of which 12 were waited for; matrix products, arithmetic and copies ran while one was open for 0% of the time, Pallas kernels for 16%

profile of v4, /device:TPU:0, one launch (start us, length us, event | category | flops | bytes accessed | tf_op | source)
XLA Modules:
  0.0 104.6 jit_solution(14239020607865653362)
XLA Ops:
  0.6 2.9 %pack_own.1 = (bf16[128,1408]{1,0:T(8,128)(2,1)}, bf16[72,2560]{1,0:T(8,128)(2,1)}, bf16[72,2560]{1,0:T(8,128)(2,1)}, bf16[72,2560]{1,0:T(8,128)(2,1)}, bf16[72,2560]{1,0:T(8,128)(2,1)}) custom-call(s32[4]{0:T(128)} %pairs_ref.5, s32[2,128]{1,0:T(2,128)} %bitcast.12, f32[2,128]{1,0:T(2,128)} %bitcast.14, bf16[128,1280]{1,0:T(8,128)(2,1)} %tok_ref.1, ...), custom_call_target="tpu_custom_call" | custom-call | flops 1024 | bytes 524288 | tf_op jit(solution)/shard_map/pack_own/pallas_call | solution.py:113
  3.6 3.0 %collective-permute-start.2 = (bf16[72,2560]{1,0:T(8,128)(2,1)}, bf16[72,2560]{1,0:T(8,128)(2,1)S(1)}, u32[]{:S(2)}, u32[]{:S(2)}) collective-permute-start(bf16[72,2560]{1,0:T(8,128)(2,1)} %get-tuple-element.66), channel_id=1, source_target_pairs={{0,1},{1,0},{2,3},{3,2},{4,5},{5,4},{6,7},{7,6},{8,9},{9,8},{10,11... | collective-permute-start | bytes 1105928 | tf_op jit(solution)/shard_map/ppermute | solution.py:26
  6.5 1.6 %collective-permute-start.5 = (bf16[72,2560]{1,0:T(8,128)(2,1)}, bf16[72,2560]{1,0:T(8,128)(2,1)S(1)}, u32[]{:S(2)}, u32[]{:S(2)}) collective-permute-start(bf16[72,2560]{1,0:T(8,128)(2,1)} %get-tuple-element.71), channel_id=1, source_target_pairs={{0,2},{1,3},{2,0},{3,1},{4,6},{5,7},{6,4},{7,5},{8,10},{9,11},{10,... | collective-permute-start | bytes 1105928 | tf_op jit(solution)/shard_map/ppermute | solution.py:26
  8.1 2.6 %collective-permute-start.3 = (bf16[128,1408]{1,0:T(8,128)(2,1)}, bf16[128,1408]{1,0:T(8,128)(2,1)S(1)}, u32[]{:S(2)}, u32[]{:S(2)}) collective-permute-start(bf16[128,1408]{1,0:T(8,128)(2,1)} %get-tuple-element.59), channel_id=1, source_target_pairs={{0,4},{1,5},{2,6},{3,7},{4,0},{5,1},{6,2},{7,3},{8,12},{9,13},{10,... | collective-permute-start | bytes 1081352 | tf_op jit(solution)/shard_map/ppermute | solution.py:26
  10.7 1.7 %copy-done = bf16[1,1280,1024]{2,1,0:T(8,128)(2,1)S(1)} copy-done((bf16[1,1280,1024]{2,1,0:T(8,128)(2,1)S(1)}, bf16[1,1280,1024]{2,1,0:T(8,128)(2,1)}, u32[]{:S(2)}) %copy-start) | copy-done | bytes 2621464
  12.5 1.7 %copy-done.1 = bf16[1,1280,1024]{2,1,0:T(8,128)(2,1)S(1)} copy-done((bf16[1,1280,1024]{2,1,0:T(8,128)(2,1)S(1)}, bf16[1,1280,1024]{2,1,0:T(8,128)(2,1)}, u32[]{:S(2)}) %copy-start.1) | copy-done | bytes 2621464
  14.2 1.7 %copy-done.2 = bf16[1,1024,1280]{2,1,0:T(8,128)(2,1)S(1)} copy-done((bf16[1,1024,1280]{2,1,0:T(8,128)(2,1)S(1)}, bf16[1,1024,1280]{2,1,0:T(8,128)(2,1)}, u32[]{:S(2)}) %copy-start.2) | copy-done | bytes 2621464
  15.9 0.6 load.1
  16.5 0.4 copy-done.3
  16.9 1.8 %terms.3 = (bf16[3,72,512]{2,1,0:T(8,128)(2,1)S(1)}, bf16[3,72,512]{2,1,0:T(8,128)(2,1)S(1)}) custom-call(bf16[72,2560]{1,0:T(8,128)(2,1)S(1)} %copy-done.3, bf16[1280,1024]{1,0:T(8,128)(2,1)S(1)} %get-tuple-element.61.refs_1_.refs_3_.refs_4_.w_gate, bf16[1280,1024]{1,0:T(8,128)(2,1)S(1)} %get-tuple-element.62.refs_2_.refs_4_.refs_5_.w_up, ...), custom_call_target="tpu_custom_call" | custom-call | flops 1024 | bytes 524288 | tf_op jit(solution)/shard_map/terms/pallas_call | solution.py:193
  18.7 0.1 collective-permute-start
  18.8 0.0 collective-permute-done.2.refs_0_.refs_1_
  18.8 5.7 %collective-permute-done.5.refs_1_.refs_2_ = bf16[72,2560]{1,0:T(8,128)(2,1)S(1)} collective-permute-done((bf16[72,2560]{1,0:T(8,128)(2,1)}, bf16[72,2560]{1,0:T(8,128)(2,1)S(1)}, u32[]{:S(2)}, u32[]{:S(2)}) %collective-permute-start.5) | collective-permute-done | bytes 368672 | tf_op jit(solution)/shard_map/ppermute | solution.py:26
  24.5 0.0 collective-permute-start.6
  24.5 0.0 collective-permute-done.3.far_ref
  24.6 3.0 %collective-permute-start.4 = (bf16[128,1280]{1,0:T(8,128)(2,1)S(1)}, bf16[128,1280]{1,0:T(8,128)(2,1)S(1)}, u32[]{:S(2)}, u32[]{:S(2)}) collective-permute-start(bf16[128,1280]{1,0:T(8,128)(2,1)S(1)} %copy-done.7), channel_id=1, source_target_pairs={{0,4},{1,5},{2,6},{3,7},{4,0},{5,1},{6,2},{7,3},{8,12},{9,13},{10,... | collective-permute-start | bytes 983048 | tf_op jit(solution)/shard_map/ppermute | solution.py:26
  27.6 0.0 collective-permute-done.refs_1_
  27.6 0.1 add.5.refs_0_
  27.6 1.6 %collective-permute-start.1 = (bf16[3,72,512]{2,1,0:T(8,128)(2,1)S(1)}, bf16[3,72,512]{2,1,0:T(8,128)(2,1)S(1)}, u32[]{:S(2)}, u32[]{:S(2)}) collective-permute-start(bf16[3,72,512]{2,1,0:T(8,128)(2,1)S(1)} %add.5.refs_0_), channel_id=1, source_target_pairs={{0,16},{8,24},{16,0},{24,8},{1,17},{9,25},{17,1},{25,9},{2,18},{10... | collective-permute-start | bytes 663560 | tf_op jit(solution)/shard_map/ppermute | solution.py:26
  29.2 4.4 %collective-permute-done.1.refs_1_ = bf16[3,72,512]{2,1,0:T(8,128)(2,1)S(1)} collective-permute-done((bf16[3,72,512]{2,1,0:T(8,128)(2,1)S(1)}, bf16[3,72,512]{2,1,0:T(8,128)(2,1)S(1)}, u32[]{:S(2)}, u32[]{:S(2)}) %collective-permute-start.1) | collective-permute-done | bytes 221216 | tf_op jit(solution)/shard_map/ppermute | solution.py:26
  33.6 5.0 %collective-permute-done.4.grad_ref = bf16[128,1280]{1,0:T(8,128)(2,1)S(1)} collective-permute-done((bf16[128,1280]{1,0:T(8,128)(2,1)S(1)}, bf16[128,1280]{1,0:T(8,128)(2,1)S(1)}, u32[]{:S(2)}, u32[]{:S(2)}) %collective-permute-start.4) | collective-permute-done | bytes 327712 | tf_op jit(solution)/shard_map/ppermute | solution.py:26
  38.6 0.0 copy-done.4
  38.6 1.3 %pack_far.1 = (bf16[72,2560]{1,0:T(8,128)(2,1)S(1)}, bf16[72,2560]{1,0:T(8,128)(2,1)S(1)}, bf16[72,2560]{1,0:T(8,128)(2,1)S(1)}, bf16[72,2560]{1,0:T(8,128)(2,1)S(1)}) custom-call(s32[4]{0:T(128)S(1)} %copy-done.4, bf16[128,1408]{1,0:T(8,128)(2,1)S(1)} %collective-permute-done.3.far_ref, bf16[128,1280]{1,0:T(8,128)(2,1)S(1)} %collective-permute-done.4.grad_ref), custom_call_target="tpu_custom_call" | custom-call | flops 1024 | bytes 524288 | tf_op jit(solution)/shard_map/pack_far/pallas_call | solution.py:140
  39.9 1.7 %collective-permute-done.6.refs_2_.refs_3_ = bf16[72,2560]{1,0:T(8,128)(2,1)S(1)} collective-permute-done((bf16[72,2560]{1,0:T(8,128)(2,1)S(1)}, bf16[72,2560]{1,0:T(8,128)(2,1)S(1)}, u32[]{:S(2)}, u32[]{:S(2)}) %collective-permute-start.6) | collective-permute-done | bytes 368672 | tf_op jit(solution)/shard_map/ppermute | solution.py:26
  41.6 2.1 %terms.4 = (bf16[3,216,512]{2,1,0:T(8,128)(2,1)S(1)}, bf16[3,216,512]{2,1,0:T(8,128)(2,1)S(1)}) custom-call(bf16[72,2560]{1,0:T(8,128)(2,1)S(1)} %collective-permute-done.2.refs_0_.refs_1_, bf16[72,2560]{1,0:T(8,128)(2,1)S(1)} %collective-permute-done.5.refs_1_.refs_2_, bf16[72,2560]{1,0:T(8,128)(2,1)S(1)} %collective-permute-done.6.refs_2_.refs_3_, ...), custom_call_target="tpu_custom_call" | custom-call | flops 1024 | bytes 524288 | tf_op jit(solution)/shard_map/terms/pallas_call | solution.py:193
  43.7 0.1 collective-permute-start.7
  43.8 0.7 collective-permute-start.9
  44.5 2.3 %collective-permute-start.10 = (bf16[72,2560]{1,0:T(8,128)(2,1)S(1)}, bf16[72,2560]{1,0:T(8,128)(2,1)S(1)}, u32[]{:S(2)}, u32[]{:S(2)}) collective-permute-start(bf16[72,2560]{1,0:T(8,128)(2,1)S(1)} %get-tuple-element.78), channel_id=1, source_target_pairs={{0,2},{1,3},{2,0},{3,1},{4,6},{5,7},{6,4},{7,5},{8,10},{9,11},{10,... | collective-permute-start | bytes 1105928 | tf_op jit(solution)/shard_map/ppermute | solution.py:26
  46.8 0.0 collective-permute-done.7.refs_1_
  46.8 0.2 add.6.refs_2_
  47.0 1.5 %collective-permute-start.8 = (bf16[3,216,512]{2,1,0:T(8,128)(2,1)S(1)}, bf16[3,216,512]{2,1,0:T(8,128)(2,1)S(1)}, u32[]{:S(2)}, u32[]{:S(2)}) collective-permute-start(bf16[3,216,512]{2,1,0:T(8,128)(2,1)S(1)} %add.6.refs_2_), channel_id=1, source_target_pairs={{0,16},{8,24},{16,0},{24,8},{1,17},{9,25},{17,1},{25,9},{2,18},{10... | collective-permute-start | bytes 1990664 | tf_op jit(solution)/shard_map/ppermute | solution.py:26
  48.5 6.3 %collective-permute-done.9.refs_1_ = bf16[72,2560]{1,0:T(8,128)(2,1)S(1)} collective-permute-done((bf16[72,2560]{1,0:T(8,128)(2,1)S(1)}, bf16[72,2560]{1,0:T(8,128)(2,1)S(1)}, u32[]{:S(2)}, u32[]{:S(2)}) %collective-permute-start.9) | collective-permute-done | bytes 368672 | tf_op jit(solution)/shard_map/ppermute | solution.py:26
  54.8 0.9 collective-permute-done.10.refs_2_
  55.7 2.3 %collective-permute-start.11 = (bf16[72,2560]{1,0:T(8,128)(2,1)S(1)}, bf16[72,2560]{1,0:T(8,128)(2,1)S(1)}, u32[]{:S(2)}, u32[]{:S(2)}) collective-permute-start(bf16[72,2560]{1,0:T(8,128)(2,1)S(1)} %get-tuple-element.80), channel_id=1, source_target_pairs={{0,3},{1,2},{2,1},{3,0},{4,7},{5,6},{6,5},{7,4},{8,11},{9,10},{10,... | collective-permute-start | bytes 1105928 | tf_op jit(solution)/shard_map/ppermute | solution.py:26
  58.0 5.7 %collective-permute-done.8.refs_3_ = bf16[3,216,512]{2,1,0:T(8,128)(2,1)S(1)} collective-permute-done((bf16[3,216,512]{2,1,0:T(8,128)(2,1)S(1)}, bf16[3,216,512]{2,1,0:T(8,128)(2,1)S(1)}, u32[]{:S(2)}, u32[]{:S(2)}) %collective-permute-start.8) | collective-permute-done | bytes 663584 | tf_op jit(solution)/shard_map/ppermute | solution.py:26
  63.7 0.2 add.7.mine
  63.9 0.1 collective-permute-start.12
  64.0 2.8 %collective-permute-done.11.refs_3_ = bf16[72,2560]{1,0:T(8,128)(2,1)S(1)} collective-permute-done((bf16[72,2560]{1,0:T(8,128)(2,1)S(1)}, bf16[72,2560]{1,0:T(8,128)(2,1)S(1)}, u32[]{:S(2)}, u32[]{:S(2)}) %collective-permute-start.11) | collective-permute-done | bytes 368672 | tf_op jit(solution)/shard_map/ppermute | solution.py:26
  66.8 2.4 %terms.5 = (bf16[3,288,512]{2,1,0:T(8,128)(2,1)S(1)}, bf16[3,288,512]{2,1,0:T(8,128)(2,1)S(1)}) custom-call(bf16[72,2560]{1,0:T(8,128)(2,1)S(1)} %get-tuple-element.93.refs_0_, bf16[72,2560]{1,0:T(8,128)(2,1)S(1)} %collective-permute-done.9.refs_1_, bf16[72,2560]{1,0:T(8,128)(2,1)S(1)} %collective-permute-done.10.refs_2_, ...), custom_call_target="tpu_custom_call" | custom-call | flops 1024 | bytes 524288 | tf_op jit(solution)/shard_map/terms/pallas_call | solution.py:193
  69.2 0.1 collective-permute-start.13
  69.3 0.0 collective-permute-done.12.other
  69.3 3.7 %outputs.1 = (bf16[288,1024]{1,0:T(8,128)(2,1)S(1)}, bf16[288,1024]{1,0:T(8,128)(2,1)S(1)}, bf16[288,1024]{1,0:T(8,128)(2,1)S(1)}, bf16[72,2688]{1,0:T(8,128)(2,...) custom-call(bf16[3,288,512]{2,1,0:T(8,128)(2,1)S(1)} %add.7.mine, ...), custom_call_target="tpu_custom_call" | custom-call | flops 1024 | bytes 524288 | tf_op jit(solution)/shard_map/outputs/pallas_call | solution.py:299
  73.0 0.0 collective-permute-done.13.refs_1_
  73.0 0.2 add.8.refs_0_
  73.2 1.5 %collective-permute-start.14 = (bf16[3,288,512]{2,1,0:T(8,128)(2,1)S(1)}, bf16[3,288,512]{2,1,0:T(8,128)(2,1)S(1)}, u32[]{:S(2)}, u32[]{:S(2)}) collective-permute-start(bf16[3,288,512]{2,1,0:T(8,128)(2,1)S(1)} %add.8.refs_0_), channel_id=1, source_target_pairs={{0,16},{8,24},{16,0},{24,8},{1,17},{9,25},{17,1},{25,9},{2,18},{10... | collective-permute-start | bytes 2654216 | tf_op jit(solution)/shard_map/ppermute | solution.py:26
  74.8 1.1 %collective-permute-start.15 = (bf16[72,2688]{1,0:T(8,128)(2,1)S(1)}, bf16[72,2688]{1,0:T(8,128)(2,1)S(1)}, u32[]{:S(2)}, u32[]{:S(2)}) collective-permute-start(bf16[72,2688]{1,0:T(8,128)(2,1)S(1)} %get-tuple-element.95), channel_id=1, source_target_pairs={{0,1},{1,0},{2,3},{3,2},{4,5},{5,4},{6,7},{7,6},{8,9},{9,8},{10,11... | collective-permute-start | bytes 1161224 | tf_op jit(solution)/shard_map/ppermute | solution.py:26
  75.8 1.5 %collective-permute-start.16 = (bf16[72,2688]{1,0:T(8,128)(2,1)S(1)}, bf16[72,2688]{1,0:T(8,128)(2,1)S(1)}, u32[]{:S(2)}, u32[]{:S(2)}) collective-permute-start(bf16[72,2688]{1,0:T(8,128)(2,1)S(1)} %get-tuple-element.96), channel_id=1, source_target_pairs={{0,2},{1,3},{2,0},{3,1},{4,6},{5,7},{6,4},{7,5},{8,10},{9,11},{10,... | collective-permute-start | bytes 1161224 | tf_op jit(solution)/shard_map/ppermute | solution.py:26
  77.3 1.0 collective-permute-start.17
  78.3 0.3 turn.2
  78.6 4.2 %own_grads.1 = (bf16[1280,1024]{1,0:T(8,128)(2,1)S(1)}, bf16[1280,1024]{1,0:T(8,128)(2,1)S(1)}, bf16[1024,1280]{1,0:T(8,128)(2,1)S(1)}) custom-call(bf16[1280,288]{1,0:T(8,128)(2,1)S(1)} %get-tuple-element.87.turned, bf16[288,1280]{1,0:T(8,128)(2,1)S(1)} %get-tuple-element.88.cot, bf16[288,1024]{1,0:T(8,128)(2,1)S(1)} %get-tuple-element.89.pre_grad, ...), custom_call_target="tpu_custom_call" | custom-call | flops 1024 | bytes 524288 | tf_op jit(solution)/shard_map/own_grads/pallas_call | solution.py:385
  82.8 0.0 copy-start.5
  82.8 0.0 copy-start.6
  82.9 0.3 turn.3
  83.2 2.7 %collective-permute-done.15.refs_1_ = bf16[72,2688]{1,0:T(8,128)(2,1)S(1)} collective-permute-done((bf16[72,2688]{1,0:T(8,128)(2,1)S(1)}, bf16[72,2688]{1,0:T(8,128)(2,1)S(1)}, u32[]{:S(2)}, u32[]{:S(2)}) %collective-permute-start.15) | collective-permute-done | bytes 387104 | tf_op jit(solution)/shard_map/ppermute | solution.py:26
  85.9 1.9 %collective-permute-done.16.refs_2_ = bf16[72,2688]{1,0:T(8,128)(2,1)S(1)} collective-permute-done((bf16[72,2688]{1,0:T(8,128)(2,1)S(1)}, bf16[72,2688]{1,0:T(8,128)(2,1)S(1)}, u32[]{:S(2)}, u32[]{:S(2)}) %collective-permute-start.16) | collective-permute-done | bytes 387104 | tf_op jit(solution)/shard_map/ppermute | solution.py:26
  87.7 7.6 %collective-permute-done.17.refs_3_ = bf16[72,2688]{1,0:T(8,128)(2,1)S(1)} collective-permute-done((bf16[72,2688]{1,0:T(8,128)(2,1)S(1)}, bf16[72,2688]{1,0:T(8,128)(2,1)S(1)}, u32[]{:S(2)}, u32[]{:S(2)}) %collective-permute-start.17) | collective-permute-done | bytes 387104 | tf_op jit(solution)/shard_map/ppermute | solution.py:26
  95.3 0.0 collective-permute-done.14.refs_1_
  95.3 0.2 add.9.mine
  95.5 0.1 collective-permute-start.18
  95.6 0.0 copy-done.5
  95.6 0.0 copy-done.6
  95.6 2.2 %combine.1 = (bf16[128,1280]{1,0:T(8,128)(2,1)}, bf16[128,1280]{1,0:T(8,128)(2,1)}, f32[2,128]{1,0:T(2,128)}) custom-call(s32[4]{0:T(128)S(1)} %copy-done.4, s32[2,128]{1,0:T(2,128)S(1)} %bitcast.13, f32[2,128]{1,0:T(2,128)S(1)} %bitcast.15, bf16[72,2688]{1,0:T(8,128)(2,1)S(1)} %get-tuple-element.99.refs_0_, ...), custom_call_target="tpu_custom_call" | custom-call | flops 1024 | bytes 524288 | tf_op jit(solution)/shard_map/combine/pallas_call | solution.py:333
  97.8 0.2 collective-permute-done.18.other
  98.0 6.4 %grads.1 = (bf16[1280,1024]{1,0:T(8,128)(2,1)}, bf16[1280,1024]{1,0:T(8,128)(2,1)}, bf16[1024,1280]{1,0:T(8,128)(2,1)}) custom-call(bf16[3,288,512]{2,1,0:T(8,128)(2,1)S(1)} %add.9.mine, bf16[3,288,512]{2,1,0:T(8,128)(2,1)S(1)} %collective-permute-done.18.other, bf16[1280,288]{1,0:T(8,128)(2,1)S(1)} %get-tuple-element.94.turned, ...), custom_call_target="tpu_custom_call" | custom-call | flops 1024 | bytes 524288 | tf_op jit(solution)/shard_map/grads/pallas_call | solution.py:426
  (9 shorter events, 0.0 us)
Async XLA Ops:
  3.6 15.3 %collective-permute-start.2 = (bf16[72,2560]{1,0:T(8,128)(2,1)}, bf16[72,2560]{1,0:T(8,128)(2,1)S(1)}, u32[]{:S(2)}, u32[]{:S(2)}) collective-permute-start(bf16[72,2560]{1,0:T(8,128)(2,1)} %get-tuple-element.66), channel_id=1, source_target_pairs={{0,1},{1,0},{2,3},{3,2},{4,5},{5,4},{6,7},{7,6},{8,9},{9,8},{10,11... | collective-permute-start | bytes 1105928 | tf_op jit(solution)/shard_map/ppermute | solution.py:26
  6.5 18.0 %collective-permute-start.5 = (bf16[72,2560]{1,0:T(8,128)(2,1)}, bf16[72,2560]{1,0:T(8,128)(2,1)S(1)}, u32[]{:S(2)}, u32[]{:S(2)}) collective-permute-start(bf16[72,2560]{1,0:T(8,128)(2,1)} %get-tuple-element.71), channel_id=1, source_target_pairs={{0,2},{1,3},{2,0},{3,1},{4,6},{5,7},{6,4},{7,5},{8,10},{9,11},{10,... | collective-permute-start | bytes 1105928 | tf_op jit(solution)/shard_map/ppermute | solution.py:26
  8.1 16.4 %collective-permute-start.3 = (bf16[128,1408]{1,0:T(8,128)(2,1)}, bf16[128,1408]{1,0:T(8,128)(2,1)S(1)}, u32[]{:S(2)}, u32[]{:S(2)}) collective-permute-start(bf16[128,1408]{1,0:T(8,128)(2,1)} %get-tuple-element.59), channel_id=1, source_target_pairs={{0,4},{1,5},{2,6},{3,7},{4,0},{5,1},{6,2},{7,3},{8,12},{9,13},{10,... | collective-permute-start | bytes 1081352 | tf_op jit(solution)/shard_map/ppermute | solution.py:26
  10.7 1.7 %copy-start = (bf16[1,1280,1024]{2,1,0:T(8,128)(2,1)S(1)}, bf16[1,1280,1024]{2,1,0:T(8,128)(2,1)}, u32[]{:S(2)}) copy-start(bf16[1,1280,1024]{2,1,0:T(8,128)(2,1)} %param.13) | copy-start | bytes 7864324
  12.5 1.7 %copy-start.1 = (bf16[1,1280,1024]{2,1,0:T(8,128)(2,1)S(1)}, bf16[1,1280,1024]{2,1,0:T(8,128)(2,1)}, u32[]{:S(2)}) copy-start(bf16[1,1280,1024]{2,1,0:T(8,128)(2,1)} %param.14) | copy-start | bytes 7864324
  14.2 1.7 %copy-start.2 = (bf16[1,1024,1280]{2,1,0:T(8,128)(2,1)S(1)}, bf16[1,1024,1280]{2,1,0:T(8,128)(2,1)}, u32[]{:S(2)}) copy-start(bf16[1,1024,1280]{2,1,0:T(8,128)(2,1)} %param.15) | copy-start | bytes 7864324
  15.9 1.0 copy-start.3
  16.9 7.6 %copy-start.8 = (bf16[72,2560]{1,0:T(8,128)(2,1)S(1)}, bf16[72,2560]{1,0:T(8,128)(2,1)}, u32[]{:S(2)}) copy-start(bf16[72,2560]{1,0:T(8,128)(2,1)} %get-tuple-element.73) | copy-start | bytes 1105924
  16.9 7.6 %copy-start.7 = (bf16[128,1280]{1,0:T(8,128)(2,1)S(1)}, bf16[128,1280]{1,0:T(8,128)(2,1)}, u32[]{:S(2)}) copy-start(bf16[128,1280]{1,0:T(8,128)(2,1)} %grad_ref.1) | copy-start | bytes 983044
  16.9 21.7 %copy-start.4 = (s32[4]{0:T(128)S(1)}, s32[4]{0:T(128)}, u32[]{:S(2)}) copy-start(s32[4]{0:T(128)} %pairs_ref.5) | copy-start | bytes 52
  18.7 8.8 %collective-permute-start = (bf16[3,72,512]{2,1,0:T(8,128)(2,1)S(1)}, bf16[3,72,512]{2,1,0:T(8,128)(2,1)S(1)}, u32[]{:S(2)}, u32[]{:S(2)}) collective-permute-start(bf16[3,72,512]{2,1,0:T(8,128)(2,1)S(1)} %get-tuple-element.65), channel_id=1, source_target_pairs={{0,8},{8,0},{16,24},{24,16},{1,9},{9,1},{17,25},{25,17},{2,10},{10... | collective-permute-start | bytes 663560 | tf_op jit(solution)/shard_map/ppermute | solution.py:26
  24.5 17.1 %collective-permute-start.6 = (bf16[72,2560]{1,0:T(8,128)(2,1)S(1)}, bf16[72,2560]{1,0:T(8,128)(2,1)S(1)}, u32[]{:S(2)}, u32[]{:S(2)}) collective-permute-start(bf16[72,2560]{1,0:T(8,128)(2,1)S(1)} %copy-done.8), channel_id=1, source_target_pairs={{0,3},{1,2},{2,1},{3,0},{4,7},{5,6},{6,5},{7,4},{8,11},{9,10},{10,... | collective-permute-start | bytes 1105928 | tf_op jit(solution)/shard_map/ppermute | solution.py:26
  24.6 14.1 %collective-permute-start.4 = (bf16[128,1280]{1,0:T(8,128)(2,1)S(1)}, bf16[128,1280]{1,0:T(8,128)(2,1)S(1)}, u32[]{:S(2)}, u32[]{:S(2)}) collective-permute-start(bf16[128,1280]{1,0:T(8,128)(2,1)S(1)} %copy-done.7), channel_id=1, source_target_pairs={{0,4},{1,5},{2,6},{3,7},{4,0},{5,1},{6,2},{7,3},{8,12},{9,13},{10,... | collective-permute-start | bytes 983048 | tf_op jit(solution)/shard_map/ppermute | solution.py:26
  27.6 6.0 %collective-permute-start.1 = (bf16[3,72,512]{2,1,0:T(8,128)(2,1)S(1)}, bf16[3,72,512]{2,1,0:T(8,128)(2,1)S(1)}, u32[]{:S(2)}, u32[]{:S(2)}) collective-permute-start(bf16[3,72,512]{2,1,0:T(8,128)(2,1)S(1)} %add.5.refs_0_), channel_id=1, source_target_pairs={{0,16},{8,24},{16,0},{24,8},{1,17},{9,25},{17,1},{25,9},{2,18},{10... | collective-permute-start | bytes 663560 | tf_op jit(solution)/shard_map/ppermute | solution.py:26
  43.7 3.1 %collective-permute-start.7 = (bf16[3,216,512]{2,1,0:T(8,128)(2,1)S(1)}, bf16[3,216,512]{2,1,0:T(8,128)(2,1)S(1)}, u32[]{:S(2)}, u32[]{:S(2)}) collective-permute-start(bf16[3,216,512]{2,1,0:T(8,128)(2,1)S(1)} %get-tuple-element.75), channel_id=1, source_target_pairs={{0,8},{8,0},{16,24},{24,16},{1,9},{9,1},{17,25},{25,17},{2,10},{10... | collective-permute-start | bytes 1990664 | tf_op jit(solution)/shard_map/ppermute | solution.py:26
  43.8 11.0 %collective-permute-start.9 = (bf16[72,2560]{1,0:T(8,128)(2,1)S(1)}, bf16[72,2560]{1,0:T(8,128)(2,1)S(1)}, u32[]{:S(2)}, u32[]{:S(2)}) collective-permute-start(bf16[72,2560]{1,0:T(8,128)(2,1)S(1)} %get-tuple-element.76), channel_id=1, source_target_pairs={{0,1},{1,0},{2,3},{3,2},{4,5},{5,4},{6,7},{7,6},{8,9},{9,8},{10,11... | collective-permute-start | bytes 1105928 | tf_op jit(solution)/shard_map/ppermute | solution.py:26
  44.5 11.2 %collective-permute-start.10 = (bf16[72,2560]{1,0:T(8,128)(2,1)S(1)}, bf16[72,2560]{1,0:T(8,128)(2,1)S(1)}, u32[]{:S(2)}, u32[]{:S(2)}) collective-permute-start(bf16[72,2560]{1,0:T(8,128)(2,1)S(1)} %get-tuple-element.78), channel_id=1, source_target_pairs={{0,2},{1,3},{2,0},{3,1},{4,6},{5,7},{6,4},{7,5},{8,10},{9,11},{10,... | collective-permute-start | bytes 1105928 | tf_op jit(solution)/shard_map/ppermute | solution.py:26
  47.0 16.8 %collective-permute-start.8 = (bf16[3,216,512]{2,1,0:T(8,128)(2,1)S(1)}, bf16[3,216,512]{2,1,0:T(8,128)(2,1)S(1)}, u32[]{:S(2)}, u32[]{:S(2)}) collective-permute-start(bf16[3,216,512]{2,1,0:T(8,128)(2,1)S(1)} %add.6.refs_2_), channel_id=1, source_target_pairs={{0,16},{8,24},{16,0},{24,8},{1,17},{9,25},{17,1},{25,9},{2,18},{10... | collective-permute-start | bytes 1990664 | tf_op jit(solution)/shard_map/ppermute | solution.py:26
  55.7 11.1 %collective-permute-start.11 = (bf16[72,2560]{1,0:T(8,128)(2,1)S(1)}, bf16[72,2560]{1,0:T(8,128)(2,1)S(1)}, u32[]{:S(2)}, u32[]{:S(2)}) collective-permute-start(bf16[72,2560]{1,0:T(8,128)(2,1)S(1)} %get-tuple-element.80), channel_id=1, source_target_pairs={{0,3},{1,2},{2,1},{3,0},{4,7},{5,6},{6,5},{7,4},{8,11},{9,10},{10,... | collective-permute-start | bytes 1105928 | tf_op jit(solution)/shard_map/ppermute | solution.py:26
  63.9 5.4 %collective-permute-start.12 = (bf16[3,288,512]{2,1,0:T(8,128)(2,1)S(1)}, bf16[3,288,512]{2,1,0:T(8,128)(2,1)S(1)}, u32[]{:S(2)}, u32[]{:S(2)}) collective-permute-start(bf16[3,288,512]{2,1,0:T(8,128)(2,1)S(1)} %add.7.mine), channel_id=1, source_target_pairs={{0,8},{8,0},{16,24},{24,16},{1,9},{9,1},{17,25},{25,17},{2,10},{10... | collective-permute-start | bytes 2654216 | tf_op jit(solution)/shard_map/ppermute | solution.py:26
  69.2 3.8 %collective-permute-start.13 = (bf16[3,288,512]{2,1,0:T(8,128)(2,1)S(1)}, bf16[3,288,512]{2,1,0:T(8,128)(2,1)S(1)}, u32[]{:S(2)}, u32[]{:S(2)}) collective-permute-start(bf16[3,288,512]{2,1,0:T(8,128)(2,1)S(1)} %get-tuple-element.81), channel_id=1, source_target_pairs={{0,8},{8,0},{16,24},{24,16},{1,9},{9,1},{17,25},{25,17},{2,10},{10... | collective-permute-start | bytes 2654216 | tf_op jit(solution)/shard_map/ppermute | solution.py:26
  73.2 22.1 %collective-permute-start.14 = (bf16[3,288,512]{2,1,0:T(8,128)(2,1)S(1)}, bf16[3,288,512]{2,1,0:T(8,128)(2,1)S(1)}, u32[]{:S(2)}, u32[]{:S(2)}) collective-permute-start(bf16[3,288,512]{2,1,0:T(8,128)(2,1)S(1)} %add.8.refs_0_), channel_id=1, source_target_pairs={{0,16},{8,24},{16,0},{24,8},{1,17},{9,25},{17,1},{25,9},{2,18},{10... | collective-permute-start | bytes 2654216 | tf_op jit(solution)/shard_map/ppermute | solution.py:26
  74.8 11.1 %collective-permute-start.15 = (bf16[72,2688]{1,0:T(8,128)(2,1)S(1)}, bf16[72,2688]{1,0:T(8,128)(2,1)S(1)}, u32[]{:S(2)}, u32[]{:S(2)}) collective-permute-start(bf16[72,2688]{1,0:T(8,128)(2,1)S(1)} %get-tuple-element.95), channel_id=1, source_target_pairs={{0,1},{1,0},{2,3},{3,2},{4,5},{5,4},{6,7},{7,6},{8,9},{9,8},{10,11... | collective-permute-start | bytes 1161224 | tf_op jit(solution)/shard_map/ppermute | solution.py:26
  75.8 11.9 %collective-permute-start.16 = (bf16[72,2688]{1,0:T(8,128)(2,1)S(1)}, bf16[72,2688]{1,0:T(8,128)(2,1)S(1)}, u32[]{:S(2)}, u32[]{:S(2)}) collective-permute-start(bf16[72,2688]{1,0:T(8,128)(2,1)S(1)} %get-tuple-element.96), channel_id=1, source_target_pairs={{0,2},{1,3},{2,0},{3,1},{4,6},{5,7},{6,4},{7,5},{8,10},{9,11},{10,... | collective-permute-start | bytes 1161224 | tf_op jit(solution)/shard_map/ppermute | solution.py:26
  77.3 18.0 %collective-permute-start.17 = (bf16[72,2688]{1,0:T(8,128)(2,1)S(1)}, bf16[72,2688]{1,0:T(8,128)(2,1)S(1)}, u32[]{:S(2)}, u32[]{:S(2)}) collective-permute-start(bf16[72,2688]{1,0:T(8,128)(2,1)S(1)} %get-tuple-element.97), channel_id=1, source_target_pairs={{0,3},{1,2},{2,1},{3,0},{4,7},{5,6},{6,5},{7,4},{8,11},{9,10},{10,... | collective-permute-start | bytes 1161224 | tf_op jit(solution)/shard_map/ppermute | solution.py:26
  82.8 12.8 %copy-start.5 = (s32[128,2]{0,1:T(2,128)S(1)}, s32[128,2]{0,1:T(2,128)}, u32[]{:S(2)}) copy-start(s32[128,2]{0,1:T(2,128)} %param.11) | copy-start | bytes 3076
  82.8 12.8 %copy-start.6 = (f32[128,2]{0,1:T(2,128)S(1)}, f32[128,2]{0,1:T(2,128)}, u32[]{:S(2)}) copy-start(f32[128,2]{0,1:T(2,128)} %param.10) | copy-start | bytes 3076
  95.5 2.5 %collective-permute-start.18 = (bf16[3,288,512]{2,1,0:T(8,128)(2,1)S(1)}, bf16[3,288,512]{2,1,0:T(8,128)(2,1)S(1)}, u32[]{:S(2)}, u32[]{:S(2)}) collective-permute-start(bf16[3,288,512]{2,1,0:T(8,128)(2,1)S(1)} %add.9.mine), channel_id=1, source_target_pairs={{0,8},{8,0},{16,24},{24,16},{1,9},{9,1},{17,25},{25,17},{2,10},{10... | collective-permute-start | bytes 2654216 | tf_op jit(solution)/shard_map/ppermute | solution.py:26
